TPU v7x, 256 devices: a whole 4x4x8 slice. The times are simulated.
256 devices in a mesh: fsdp: 16 (over z_lo, y), dp: 16 (over z_hi, x, core).
Axes of the slice: x: 4, y: 4, z: 8 (z_hi: 2, z_lo: 4; z = z_hi * 4 + z_lo), core: 2. Of those that a mesh axis runs over, the one named last changes fastest.
Arguments:
- block_in: bfloat16 [65536, 3072], P(('fsdp', 'dp')), may hold values from -6 to 6
- block_out: bfloat16 [65536, 3072], P(('fsdp', 'dp')), may hold values from -6 to 6
- weight: bfloat16 [3072, 3072], P('fsdp'), may hold values from -0.109375 to 0.109375
- adapter_a: bfloat16 [3072, 64], P('fsdp'), may hold values from -0.109375 to 0.109375
- adapter_b: bfloat16 [64, 3072], P(None, 'fsdp'), may hold values from -0.75 to 0.75
- proj: bfloat16 [3072, 64], replicated, may hold values from -0.109375 to 0.109375
- w_feature: bfloat16 [3136, 512], replicated, may hold values from -0.109375 to 0.109375
- w_embed: bfloat16 [512, 512], replicated, may hold values from -0.25 to 0.25
- id_table: bfloat16 [1024, 512], P('dp'), may hold values from -6 to 6
- box_rows: int32 [256, 6], P(('fsdp', 'dp')), may hold values from 0 to 9
- box_cols: int32 [256, 6], P(('fsdp', 'dp')), may hold values from 0 to 9
- identity: int32 [256, 6], P(('fsdp', 'dp')), may hold values from 0 to 1023, as said below
- face_count: int32 [256], P(('fsdp', 'dp')), may hold values from 3 to 6
Outputs:
- grad_in: bfloat16 [65536, 3072], P(('fsdp', 'dp'))
- grad_a: float32 [3072, 64], P('fsdp')
- grad_b: float32 [64, 3072], P(None, 'fsdp')
Inputs may be any that keep to these rules, and one draw needn't show every extreme that they name: `identity`: identity blocks are runs of 64 numbers; at most 1 slots of an image name identities of one block.
All inputs are finite; a program needn't handle non-finite values.
Results may differ from a plain program's by a relative error of at most 0.03.
Values may be sent and summed in bfloat16 or wider, within the bound.
No kernel may reach another device: no remote copies, remote signals or barrier semaphores. Data moves between devices by JAX's collectives and lax.ppermute only.
A program may use at most 128 MiB of HBM per device.

v0:
```python
import jax
import jax.numpy as jnp
from jax import lax
from jax.sharding import PartitionSpec as P

CH = 64
FACE = 7
MAXF = 6
GW = 16
GH = 16
IDS_DEV = 64
TOK_DEV = 256
CROP = 3136


loss_scale = 1024.0
eps_norm = 1e-06


def gelu_slope(preact):
    return jax.jvp(jax.nn.gelu, (preact,), (jnp.ones_like(preact),))[1]


def reward_grads(crops, refers, w_feature, w_embed):
    preact = jnp.dot(crops, w_feature, preferred_element_type=jnp.float32)
    feature = jax.nn.gelu(preact).astype(jnp.bfloat16)
    embedding = jnp.dot(feature, w_embed, preferred_element_type=jnp.float32)
    norm_e = jnp.sqrt(jnp.sum(embedding * embedding, axis=-1, keepdims=True) + eps_norm)
    norm_r = jnp.sqrt(jnp.sum(refers * refers, axis=-1, keepdims=True) + eps_norm)
    cosine = jnp.sum(embedding * refers, axis=-1, keepdims=True) / (norm_e * norm_r)
    d_embed = (
        loss_scale * (refers / (norm_e * norm_r) - cosine * embedding / (norm_e * norm_e))
    ).astype(jnp.bfloat16)
    d_feature = lax.dot_general(
        d_embed, w_embed, (((1,), (1,)), ((), ())), preferred_element_type=jnp.float32
    )
    d_pre = (d_feature * gelu_slope(preact)).astype(jnp.bfloat16)
    return lax.dot_general(
        d_pre, w_feature, (((1,), (1,)), ((), ())), preferred_element_type=jnp.float32
    ).astype(jnp.bfloat16)


def lookup_rows(tags, id_table):
    local_rows = id_table.shape[0]
    onehot = (
        tags.reshape(-1)[:, None] - 1 == jnp.arange(local_rows, dtype=jnp.int32)[None, :]
    ).astype(jnp.bfloat16)
    return jnp.dot(onehot, id_table, preferred_element_type=jnp.float32)


def local(
    block_in,
    block_out,
    weight,
    adapter_a,
    adapter_b,
    proj,
    w_feature,
    w_embed,
    id_table,
    box_rows,
    box_cols,
    identity,
    face_count,
):
    n_groups = lax.axis_size("dp")
    slot_cap = (MAXF + n_groups - 1) // n_groups
    latent = (
        jnp.dot(block_out, proj, preferred_element_type=jnp.float32)
        .astype(jnp.bfloat16)
        .reshape(GH, GW, CH)
    )
    anchor = jnp.zeros((), jnp.int32)
    row_start = box_rows[0]
    col_start = box_cols[0]
    crops = jnp.stack(
        [
            lax.dynamic_slice(
                latent, (row_start[number], col_start[number], anchor), (FACE, FACE, CH)
            ).reshape(CROP)
            for number in range(MAXF)
        ]
    )
    slot_ids = jnp.arange(MAXF, dtype=jnp.int32)
    alive = slot_ids < face_count[0]
    idents = identity[0]
    holders = idents // IDS_DEV
    local_id = idents - holders * IDS_DEV
    earlier = (holders[None, :] == holders[:, None]) & (slot_ids[None, :] < slot_ids[:, None])
    slot_pos = jnp.sum(earlier.astype(jnp.int32), axis=1)
    target = jnp.arange(n_groups, dtype=jnp.int32)[:, None, None]
    places = jnp.arange(slot_cap, dtype=jnp.int32)[None, :, None]
    chosen = (
        (holders[None, None, :] == target)
        & (slot_pos[None, None, :] == places)
        & alive[None, None, :]
    )
    select = chosen.astype(jnp.bfloat16)
    tags = jnp.sum(chosen.astype(jnp.int32) * (local_id + 1)[None, None, :], axis=2)
    got_tags = lax.all_to_all(tags, "dp", split_axis=0, concat_axis=0, tiled=True)
    outgoing = jnp.einsum("ock,kf->ocf", select, crops, preferred_element_type=jnp.float32).astype(
        jnp.bfloat16
    )
    arrived = lax.all_to_all(outgoing, "dp", split_axis=0, concat_axis=0, tiled=True)
    refers = lookup_rows(got_tags, id_table)
    d_arrived = reward_grads(
        arrived.reshape(n_groups * slot_cap, CROP), refers, w_feature, w_embed
    ).reshape(n_groups, slot_cap, CROP)
    returned = lax.all_to_all(d_arrived, "dp", split_axis=0, concat_axis=0, tiled=True)
    d_crops = jnp.einsum(
        "ock,ocf->kf", select, returned, preferred_element_type=jnp.float32
    ).astype(jnp.bfloat16)
    d_latent = jnp.zeros((GH, GW, CH), jnp.float32)
    for number in range(MAXF):
        corner = (row_start[number], col_start[number], anchor)
        window = lax.dynamic_slice(d_latent, corner, (FACE, FACE, CH))
        placed = d_crops[number].astype(jnp.float32).reshape(FACE, FACE, CH)
        d_latent = lax.dynamic_update_slice(d_latent, window + placed, corner)
    d_latent = d_latent.reshape(TOK_DEV, CH).astype(jnp.bfloat16)
    upstream = lax.dot_general(
        d_latent, proj, (((1,), (1,)), ((), ())), preferred_element_type=jnp.float32
    ).astype(jnp.bfloat16)
    whole_a, whole_b = (
        lax.all_gather(adapter_a, "fsdp", axis=0, tiled=True),
        lax.all_gather(adapter_b, "fsdp", axis=1, tiled=True),
    )
    low_grad = lax.dot_general(
        upstream, whole_b, (((1,), (1,)), ((), ())), preferred_element_type=jnp.float32
    ).astype(jnp.bfloat16)
    through = lax.dot_general(
        upstream,
        lax.all_gather(weight, "fsdp", axis=0, tiled=True),
        (((1,), (1,)), ((), ())),
        preferred_element_type=jnp.float32,
    )
    side = lax.dot_general(
        low_grad, whole_a, (((1,), (1,)), ((), ())), preferred_element_type=jnp.float32
    )
    grad_in = (upstream.astype(jnp.float32) + through + side).astype(jnp.bfloat16)
    x_low = jnp.dot(block_in, whole_a, preferred_element_type=jnp.float32).astype(jnp.bfloat16)
    term_a = lax.dot_general(
        block_in, low_grad, (((0,), (0,)), ((), ())), preferred_element_type=jnp.float32
    )
    term_b = lax.dot_general(
        x_low, upstream, (((0,), (0,)), ((), ())), preferred_element_type=jnp.float32
    )
    total_a, total_b = (
        lax.psum(term_a.astype(jnp.bfloat16), "dp").astype(jnp.float32),
        lax.psum(term_b.astype(jnp.bfloat16), "dp").astype(jnp.float32),
    )
    share_a, share_b = (
        lax.psum_scatter(
            total_a.astype(jnp.bfloat16), "fsdp", scatter_dimension=0, tiled=True
        ).astype(jnp.float32),
        lax.psum_scatter(
            total_b.astype(jnp.bfloat16), "fsdp", scatter_dimension=1, tiled=True
        ).astype(jnp.float32),
    )
    return (grad_in, share_a / loss_scale, share_b / loss_scale)


def solution(mesh):
    return jax.shard_map(
        local,
        mesh=mesh,
        in_specs=(
            P(("fsdp", "dp"), None),
            P(("fsdp", "dp"), None),
            P("fsdp", None),
            P("fsdp", None),
            P(None, "fsdp"),
            P(),
            P(),
            P(),
            P("dp", None),
            P(("fsdp", "dp"), None),
            P(("fsdp", "dp"), None),
            P(("fsdp", "dp"), None),
            P(("fsdp", "dp")),
        ),
        out_specs=(P(("fsdp", "dp"), None), P("fsdp", None), P(None, "fsdp")),
        check_vma=False,
    )
```

profile of v0, /device:TPU:64, one launch (start us, length us, event | category | flops | bytes accessed | tf_op | source)
XLA Modules:
  0.0 575.8 jit_solution(9593072408799686234)
XLA Ops:
  7.2 0.8 fusion.67
  8.0 0.8 fusion.68
  9.5 0.2 convert_reduce_fusion
  9.8 0.7 copy.31
  10.5 9.2 %all-to-all-start = ((s32[16,1,1]{2,1,0:T(1,128)}), s32[16,1,1]{2,1,0:T(1,128)S(1)}, u32[]{:S(2)}, u32[]{:S(2)}) async-start(s32[16,1,1]{2,1,0:T(1,128)} %copy.31), calls=%async_computation | async-start | bytes 16384 | tf_op jit(solution)/shard_map/all_to_all | solution.py:100
  19.7 1.6 fusion.83
  22.6 1.5 fusion.82
  37.9 2.1 convolution_convert_fusion.8
  48.6 0.5 broadcast.364
  49.1 0.7 reduce.15
  49.7 0.8 reshape.410
  50.6 9.6 %all-to-all-start.1 = ((bf16[16,2,1568]{2,1,0:T(2,128)(2,1)}), bf16[16,2,1568]{2,1,0:T(2,128)(2,1)S(1)}, u32[]{:S(2)}, u32[]{:S(2)}) async-start(bf16[16,2,1568]{2,1,0:T(2,128)(2,1)} %reshape.410), calls=%async_computation.1 | async-start | bytes 212992 | tf_op jit(solution)/shard_map/all_to_all | solution.py:104
  60.2 0.4 add_reduce_fusion
  60.6 11.1 %all-to-all-done.1 = bf16[16,2,1568]{2,1,0:T(2,128)(2,1)S(1)} async-done(((bf16[16,2,1568]{2,1,0:T(2,128)(2,1)}), bf16[16,2,1568]{2,1,0:T(2,128)(2,1)S(1)}, u32[]{:S(2)}, u32[]{:S(2)}) %all-to-all-start.1) | async-done | bytes 100384 | tf_op jit(solution)/shard_map/all_to_all | solution.py:104
  71.8 0.5 fusion.7
  72.3 0.5 copy-done.3
  72.8 0.2 fusion.26
  73.0 0.3 multiply_reduce_fusion.1
  73.4 2.2 fusion.1
  75.6 0.7 reduce.16
  76.3 0.8 reshape.412
  77.1 3.5 all-to-all-start.2
  80.7 35.9 %all-gather.1 = bf16[16,192,64]{1,2,0:T(8,128)(2,1)S(1)} all-gather(bf16[1,192,64]{1,2,0:T(8,128)(2,1)S(1)} %bitcast.82), channel_id=1, replica_groups=mesh['fsdp'=16,'dp'=16] {'fsdp'}, dimensions={0}, use_global_device_ids=true | all-gather | bytes 417792 | tf_op jit(solution)/shard_map/all_gather | solution.py:124
  116.6 1.1 copy.36
  117.7 2.4 reshape.398
  120.3 0.2 convolution_convert_fusion.2
  120.5 0.2 fusion.44
  120.8 0.2 dynamic_update_slice.18
  121.8 0.2 dynamic_update_slice.22
  122.2 2.7 convolution_convert_fusion.3
  124.9 4.1 convolution_convert_fusion.4
  129.0 2.2 copy.39
  131.3 34.0 %all-gather = bf16[16,192,64]{1,2,0:T(8,128)(2,1)S(1)} all-gather(bf16[1,192,64]{1,2,0:T(8,128)(2,1)S(1)} %bitcast.83), channel_id=1, replica_groups=mesh['fsdp'=16,'dp'=16] {'fsdp'}, dimensions={0}, use_global_device_ids=true | all-gather | bytes 417792 | tf_op jit(solution)/shard_map/all_gather | solution.py:125
  165.3 1.1 copy.35
  166.3 2.4 reshape.396
  168.8 2.2 convolution_convert_fusion.7
  171.0 1.1 fusion.3
  172.1 2.1 copy.37
  174.3 0.7 all-gather.4.cloned.1.call-update
  175.0 34.5 %reduce-scatter.9.cloned.1.call-done = bf16[192,64]{1,0:T(8,128)(2,1)} async-done(((bf16[3072,64]{1,0:T(8,128)(2,1)}), bf16[192,64]{1,0:T(8,128)(2,1)}) %reduce-scatter.9.cloned.1.call-update) | async-done | bytes 24592
  209.5 0.9 copy.40
  210.4 82.8 %reduce-scatter.7.cloned.1.call-done = bf16[192,64]{1,0:T(8,128)(2,1)} async-done(((bf16[3072,64]{1,0:T(8,128)(2,1)}), bf16[192,64]{1,0:T(8,128)(2,1)}) %reduce-scatter.7.cloned.1.call-update) | async-done | bytes 24592
  293.2 0.9 copy.38
  294.0 262.4 %all-reduce = (bf16[192,64]{0,1:T(8,128)(2,1)S(1)}, bf16[64,192]{1,0:T(8,128)(2,1)S(1)}) all-reduce(bf16[192,64]{0,1:T(8,128)(2,1)S(1)} %copy.38, bf16[64,192]{1,0:T(8,128)(2,1)S(1)} %copy.40), channel_id=1, replica_groups=mesh['fsdp'=16,'dp'=16] {'dp'}, use_global_device_ids=true, to_apply=%region_5.6 | all-reduce | flops 24576 | bytes 98304 | tf_op jit(solution)/shard_map/psum | solution.py:148
  556.4 0.6 convert_multiply_fusion.1
  557.0 0.6 convert_multiply_fusion
  557.7 9.9 %convolution_add_fusion.1 = f32[256,3072]{1,0:T(8,128)S(1)} fusion(bf16[256,3072]{1,0:T(8,128)(2,1)} %convolution_convert_fusion.3, bf16[3072,3072]{1,0:T(8,128)(2,1)} %all-gather.4.cloned.1.call-done), kind=kOutput, calls=%fused_computation.6 | convolution fusion | flops 4833411072 | bytes 23592960 | tf_op jit(solution)/shard_map/dot_general | solution.py:130
  567.6 1.7 fusion.2
  (53 shorter events, 2.9 us)
Async XLA Ops:
  7.2 64.6 %copy-start = (bf16[3136,512]{1,0:T(8,128)(2,1)S(1)}, bf16[3136,512]{1,0:T(8,128)(2,1)}, u32[]{:S(2)}) copy-start(bf16[3136,512]{1,0:T(8,128)(2,1)} %param.19) | copy-start | bytes 9633796
  10.5 40.1 %all-to-all-start = ((s32[16,1,1]{2,1,0:T(1,128)}), s32[16,1,1]{2,1,0:T(1,128)S(1)}, u32[]{:S(2)}, u32[]{:S(2)}) async-start(s32[16,1,1]{2,1,0:T(1,128)} %copy.31), calls=%async_computation | async-start | bytes 16384 | tf_op jit(solution)/shard_map/all_to_all | solution.py:100
  50.6 21.1 %all-to-all-start.1 = ((bf16[16,2,1568]{2,1,0:T(2,128)(2,1)}), bf16[16,2,1568]{2,1,0:T(2,128)(2,1)S(1)}, u32[]{:S(2)}, u32[]{:S(2)}) async-start(bf16[16,2,1568]{2,1,0:T(2,128)(2,1)} %reshape.410), calls=%async_computation.1 | async-start | bytes 212992 | tf_op jit(solution)/shard_map/all_to_all | solution.py:104
  71.8 1.0 copy-start.3
  71.8 1.2 copy-start.4
  73.4 7.3 %copy-start.5 = (bf16[192,64]{0,1:T(8,128)(2,1)S(1)}, bf16[192,64]{0,1:T(8,128)(2,1)}, u32[]{:S(2)}) copy-start(bf16[192,64]{0,1:T(8,128)(2,1)} %param.16) | copy-start | bytes 73732
  77.1 43.0 %all-to-all-start.2 = ((bf16[16,2,1568]{2,1,0:T(2,128)(2,1)}), bf16[16,2,1568]{2,1,0:T(2,128)(2,1)S(1)}, u32[]{:S(2)}, u32[]{:S(2)}) async-start(bf16[16,2,1568]{2,1,0:T(2,128)(2,1)} %reshape.412), calls=%async_computation.2 | async-start | bytes 212992 | tf_op jit(solution)/shard_map/all_to_all | solution.py:109
  80.6 128.9 %reduce-scatter.9.cloned.1.call-start = ((), (), s32[]{:S(2)}) async-start(), calls=%async_computation.7 | async-start | bytes 835584
  129.0 2.3 copy-start.6
  131.2 161.9 %reduce-scatter.7.cloned.1.call-start = ((), (), s32[]{:S(2)}) async-start(), calls=%async_computation.6 | async-start | bytes 835584
  168.8 2.2 copy-start.1
  174.3 383.4 %all-gather.4.cloned.1.call-start = ((), (), s32[]{:S(2)}) async-start(), calls=%async_computation.5 | async-start | bytes 20054016 | tf_op jit(solution)/shard_map/all_gather | solution.py:132
  557.7 9.9 %copy-start.2 = (bf16[3072,64]{0,1:T(8,128)(2,1)S(1)}, bf16[3072,64]{0,1:T(8,128)(2,1)}, u32[]{:S(2)}) copy-start(bf16[3072,64]{0,1:T(8,128)(2,1)} %reshape.398) | copy-start | bytes 1179652
Sparse Core Ops, SparseCore 0:
  131.3 78.1 reduce-scatter.8
  212.2 80.9 reduce-scatter.6
  295.0 215.6 all-gather.3
where the time goes:
time: 577 us; the launch traced here: 576 us
  blocking collectives  332 us (58%)
  waiting for transfers between devices  129 us (22%)
  between operations  37.3 us (6%)
  matrix products  27.3 us (5%)
  starting transfers between devices  22.5 us (4%)
  local copies, waits for them, and re-layouts  22.2 us (4%)
    psum x1, blocking collectives, local(): lax.psum(term_a.astype(jnp.bfloat16), 'dp').astype(jnp.float32)  262 us
    unnamed x5, waiting for transfers between devices  118 us
    all_gather x1, blocking collectives, local(): lax.all_gather(adapter_a, 'fsdp', axis=0, tiled=True)  35.9 us
    all_gather x1, blocking collectives, local(): lax.all_gather(adapter_b, 'fsdp', axis=1, tiled=True)  34 us
    unnamed x24, local copies, waits for them, and re-layouts  13.4 us
  transfers between devices with their start and end apart: 6, of which 3 were waited for; matrix products, arithmetic and copies ran while one was open for 4% of the time, Pallas kernels for 0%

commit v1 on v0

v1 whole, which is shorter than its diff:
```python
import jax
import jax.numpy as jnp
from jax import lax
from jax.experimental import pallas as pl
from jax.experimental.pallas import tpu as pltpu
from jax.sharding import PartitionSpec as P

D = 3072
CH = 64
RANK = 64
HID = 512
EMB = 512
FACE = 7
MAXF = 6
GW = 16
IDS_DEV = 64
TOK = 256
CROP = 3136
SHARD = 192
HALF = 96
KH = 32
GROUPS = 12
ROWS = GROUPS * 8
SEGS = 12
PAY = HALF + KH

loss_scale = 1024.0
eps_norm = 1e-06
BF = jnp.bfloat16
F32 = jnp.float32
AXES = ("fsdp", "dp")


def coords(index):
    f, d = index // 16, index % 16
    return f // 4, f % 4, d // 8, (d // 2) % 4, d % 2


def number(zl, y, zh, x, c):
    return (zl * 4 + y) * 16 + zh * 8 + x * 2 + c


def pairs(move):
    return [(i, number(*move(*coords(i)))) for i in range(256)]


def shift_z(step):
    def move(zl, y, zh, x, c):
        z = (zh * 4 + zl + step) % 8
        return z % 4, y, z // 4, x, c

    return pairs(move)


CORE = pairs(lambda zl, y, zh, x, c: (zl, y, zh, x, c ^ 1))
X1 = pairs(lambda zl, y, zh, x, c: (zl, y, zh, x ^ 1, c))
X3 = pairs(lambda zl, y, zh, x, c: (zl, y, zh, x ^ 3, c))
Y1 = pairs(lambda zl, y, zh, x, c: (zl, y ^ 1, zh, x, c))
Y3 = pairs(lambda zl, y, zh, x, c: (zl, y ^ 3, zh, x, c))
ZL1 = pairs(lambda zl, y, zh, x, c: (zl ^ 1, y, zh, x, c))
ZL2 = pairs(lambda zl, y, zh, x, c: (zl ^ 2, y, zh, x, c))
ZPAIR = pairs(lambda zl, y, zh, x, c: (zl ^ 2, y, zh ^ 1, x, c))


def swap(value, perm):
    return lax.ppermute(value, AXES, perm)


def dot(a, b, da, db):
    return lax.dot_general(a, b, (((da,), (db,)), ((), ())), preferred_element_type=F32)


def lanes_at(width, offset):
    rows = lax.broadcasted_iota(jnp.int32, (CH, width), 0)
    cols = lax.broadcasted_iota(jnp.int32, (CH, width), 1)
    return (cols == rows + offset).astype(BF)


def params(mib):
    return pltpu.CompilerParams(vmem_limit_bytes=mib << 20)


def vmem(n):
    return [pl.BlockSpec(memory_space=pltpu.VMEM)] * n


SMEM = pl.BlockSpec(memory_space=pltpu.SMEM)


def pack_kernel(place, weight, proj, a_ref, b_ref, pay, own_proj):
    f, c = place[0], place[1]
    top = pl.multiple_of(c * HALF, 32)
    mine = proj[pl.ds(pl.multiple_of(f * SHARD, 64), SHARD), :]
    own_proj[...] = mine
    half = proj[pl.ds(pl.multiple_of(f * SHARD + c * HALF, 32), HALF), :]
    moved = dot(weight[pl.ds(top, HALF), :], proj[...], 1, 0) + half.astype(F32)
    left = dot(moved.astype(BF), lanes_at(128, 0), 1, 0)
    right = dot(a_ref[pl.ds(top, HALF), :], lanes_at(128, CH), 1, 0)
    pay[0:HALF, :] = (left + right).astype(BF)
    cross = dot(mine, b_ref[...], 0, 1).astype(BF)
    wide = dot(cross, lanes_at(128, CH), 1, 0)
    pay[HALF:PAY, :] = jnp.where(c == 0, wide[0:KH], wide[KH : 2 * KH]).astype(BF)


def pack(place, weight, proj, a, b):
    return pl.pallas_call(
        pack_kernel,
        out_shape=(
            jax.ShapeDtypeStruct((PAY, 128), BF),
            jax.ShapeDtypeStruct((SHARD, CH), BF),
        ),
        in_specs=[SMEM] + vmem(4),
        out_specs=tuple(vmem(2)),
        compiler_params=params(16),
        name="pack",
    )(place, weight, proj, a, b)


def corner_of(rows, cols, slot):
    corner = jnp.zeros_like(slot)
    for k in range(MAXF):
        corner = jnp.where(slot == k, rows[0, k] * GW + cols[0, k], corner)
    return corner


def token_of(rows, cols, index, i):
    slot = index & 7
    p = 4 * (index >> 3) + i
    down = (p * 37) >> 8
    token = corner_of(rows, cols, slot) + down * GW + (p - down * FACE)
    return jnp.where((slot < MAXF) & (p < FACE * FACE), token, -1)


def face_kernel(rows, cols, y_ref, proj, w_feature, w_embed, pre_ref, emb_ref):
    latent = dot(y_ref[...], proj[...], 1, 0).astype(BF)
    n = ROWS + 8
    index = lax.broadcasted_iota(jnp.int32, (n, TOK), 0)
    token = lax.broadcasted_iota(jnp.int32, (n, TOK), 1)
    crops = jnp.zeros((n, 256), F32)
    for i in range(4):
        pick = (token_of(rows, cols, index, i) == token).astype(BF)
        wide = dot(latent, lanes_at(256, CH * i), 1, 0).astype(BF)
        crops += dot(pick, wide, 1, 0)
    crops = crops.astype(BF)
    pre = dot(crops[ROWS:n, 0:CH], w_feature[GROUPS * 256 : CROP, :], 1, 0)
    for g in range(GROUPS):
        pre += dot(crops[8 * g : 8 * g + 8, :], w_feature[256 * g : 256 * g + 256, :], 1, 0)
    pre_ref[...] = pre
    feature = jax.nn.gelu(pre).astype(BF)
    emb_ref[...] = dot(feature, w_embed[...], 1, 0)


def face(rows, cols, y, proj, w_feature, w_embed):
    return pl.pallas_call(
        face_kernel,
        out_shape=(
            jax.ShapeDtypeStruct((8, HID), F32),
            jax.ShapeDtypeStruct((8, EMB), F32),
        ),
        in_specs=[SMEM, SMEM] + vmem(4),
        out_specs=tuple(vmem(2)),
        compiler_params=params(24),
        name="face",
    )(rows, cols, y, proj, w_feature, w_embed)


def low_kernel(place, x_ref, mine, other, maps, low, cross):
    f, c = place[0], place[1]
    zl, y = f >> 2, f & 3
    for i in range(16):
        b0, b1, b2, b3 = i & 1, (i >> 1) & 1, (i >> 2) & 1, i >> 3
        j = (zl ^ (2 * b0 + b1)) * 4 + (y ^ (3 * b3) ^ b2)
        for source, half in ((mine, c), (other, 1 - c)):
            start = pl.multiple_of(j * SHARD + half * HALF, 32)
            maps[pl.ds(start, HALF), :] = source[i, 0:HALF, :]
    for source, half in ((mine, c), (other, 1 - c)):
        total = jnp.zeros((KH, 128), F32)
        for i in range(16):
            total += source[i, HALF:PAY, :].astype(F32)
        cross[pl.ds(pl.multiple_of(half * KH, KH), KH), :] = total
    low[...] = dot(x_ref[...], maps[...], 1, 0).astype(BF)


def low_maps(place, x, mine, other):
    return pl.pallas_call(
        low_kernel,
        out_shape=(
            jax.ShapeDtypeStruct((D, 128), BF),
            jax.ShapeDtypeStruct((TOK, 128), BF),
            jax.ShapeDtypeStruct((2 * KH, 128), F32),
        ),
        in_specs=[SMEM] + vmem(3),
        out_specs=tuple(vmem(3)),
        compiler_params=params(24),
        name="low",
    )(place, x, mine, other)


def gelu_slope(preact):
    return jax.jvp(jax.nn.gelu, (preact,), (jnp.ones_like(preact),))[1]


def main_kernel(
    place, rows, cols, ident, count, near, far, pre_ref, emb_ref, w_embed, w_feature,
    x_ref, low, cross, out, wide_ref,
):
    d, c = place[2], place[1]
    slot = lax.broadcasted_iota(jnp.int32, (8, 16), 0)
    lane = lax.broadcasted_iota(jnp.int32, (8, 16), 1)
    refer = jnp.zeros((8, EMB), F32)
    for k in range(MAXF):
        who = ident[0, k]
        block = who >> 6
        flip = block ^ d
        b2 = (flip >> 2) & 1
        b1 = ((flip >> 1) & 1) ^ b2
        spot = (b2 * 4 + b1 * 2 + (flip >> 3)) * IDS_DEV + (who & 63)
        start = pl.multiple_of((spot >> 4) * 16, 16)
        chunk = jnp.where((flip & 1) == 0, near[pl.ds(start, 16), :], far[pl.ds(start, 16), :])
        live = (slot == k) & (lane == (spot & 15)) & (k < count[0])
        refer += dot(live.astype(BF), chunk, 1, 0)
    emb = emb_ref[...]
    norm_e = jnp.sqrt(jnp.sum(emb * emb, axis=-1, keepdims=True) + eps_norm)
    norm_r = jnp.sqrt(jnp.sum(refer * refer, axis=-1, keepdims=True) + eps_norm)
    cosine = jnp.sum(emb * refer, axis=-1, keepdims=True) / (norm_e * norm_r)
    d_embed = (
        loss_scale * (refer / (norm_e * norm_r) - cosine * emb / (norm_e * norm_e))
    ).astype(BF)
    d_feature = dot(d_embed, w_embed[...], 1, 1)
    d_pre = (d_feature * gelu_slope(pre_ref[...])).astype(BF)
    parts = [
        dot(d_pre, w_feature[256 * g : 256 * g + 256, :], 1, 1) for g in range(GROUPS)
    ]
    d_crop = jnp.concatenate(parts, axis=0).astype(BF)
    last = dot(d_pre, w_feature[GROUPS * 256 : CROP, :], 1, 1).astype(BF)
    index = lax.broadcasted_iota(jnp.int32, (TOK, ROWS), 1)
    token = lax.broadcasted_iota(jnp.int32, (TOK, ROWS), 0)
    tail = lax.broadcasted_iota(jnp.int32, (TOK, 8), 1) + ROWS
    pick = (token_of(rows, cols, tail, 0) == token[:, 0:8]).astype(BF)
    d_latent = dot(pick, last, 1, 0)
    for i in range(4):
        pick = (token_of(rows, cols, index, i) == token).astype(BF)
        piece = dot(d_crop, lanes_at(256, CH * i), 1, 1).astype(BF)
        d_latent += dot(pick, piece, 1, 0)
    d_latent = d_latent.astype(BF)
    for g in range(2):
        for z in range(4):
            first = 768 * z + 384 * g
            part = dot(d_latent, x_ref[:, first : first + 384], 0, 0).astype(BF)
            for h in range(2):
                for t in range(3):
                    out[h, SEGS * g + 3 * z + t] = part[
                        KH * h : KH * h + KH, 128 * t : 128 * t + 128
                    ]
    part = dot(d_latent, low[...], 0, 0).astype(BF)
    for h in range(2):
        out[h, 2 * SEGS] = part[KH * h : KH * h + KH, :]
    widen = (lanes_at(128, 0).astype(F32) + cross[...]).astype(BF)
    wide_ref[...] = dot(d_latent, widen, 1, 0).astype(BF)


def main(place, rows, cols, ident, count, *rest):
    return pl.pallas_call(
        main_kernel,
        out_shape=(
            jax.ShapeDtypeStruct((2, 2 * SEGS + 1, KH, 128), BF),
            jax.ShapeDtypeStruct((TOK, 128), BF),
        ),
        in_specs=[SMEM] * 5 + vmem(9),
        out_specs=tuple(vmem(2)),
        compiler_params=params(28),
        name="main",
    )(place, rows, cols, ident, count, *rest)


def through_kernel(wide, maps, out):
    out[...] = dot(wide[...], maps[...], 1, 1).astype(BF)


def through(wide, maps):
    cols = 768
    return pl.pallas_call(
        through_kernel,
        out_shape=jax.ShapeDtypeStruct((TOK, D), BF),
        grid=(D // cols,),
        in_specs=[
            pl.BlockSpec((TOK, 128), lambda i: (0, 0)),
            pl.BlockSpec((cols, 128), lambda i: (i, 0)),
        ],
        out_specs=pl.BlockSpec((TOK, cols), lambda i: (0, i)),
        compiler_params=params(16),
        name="through",
    )(wide, maps)


def last_kernel(place, mine, other, cross, own_proj, grad_a, grad_b, total, rows):
    f, c = place[0], place[1]
    for source, half in ((mine, c), (other, 1 - c)):
        for t in range(4):
            total[pl.ds(pl.multiple_of(half * KH, KH), KH), 128 * t : 128 * t + 128] = source[t]
    cross_t = dot(cross[...].astype(BF), lanes_at(128, CH), 1, 1).astype(BF)
    rows[...] = dot(total[:, 0:384], cross_t, 0, 0)
    start = pl.multiple_of((f & 1) * SHARD, 64)
    grad_a[...] = rows[pl.ds(start, SHARD), :] / loss_scale
    both = dot(total[:, 384:512], own_proj[...], 0, 1)
    grad_b[...] = both[RANK : 2 * RANK, :] / loss_scale


def last(place, mine, other, cross, own_proj):
    return pl.pallas_call(
        last_kernel,
        out_shape=(
            jax.ShapeDtypeStruct((SHARD, RANK), F32),
            jax.ShapeDtypeStruct((RANK, SHARD), F32),
        ),
        in_specs=[SMEM] + vmem(4),
        out_specs=tuple(vmem(2)),
        scratch_shapes=[pltpu.VMEM((2 * KH, 512), BF), pltpu.VMEM((384, CH), F32)],
        compiler_params=params(8),
        name="last",
    )(place, mine, other, cross, own_proj)


def add(*terms):
    return sum(t.astype(F32) for t in terms).astype(BF)


def reduce_all(sums, f, d):
    zl, y, c = f // 4, f % 4, d % 2
    group = y // 2
    pick = lambda v, i, n: lax.dynamic_slice_in_dim(v, i, n, axis=0)
    keep = pick(sums, c, 1)[0]
    v = add(keep, swap(pick(sums, 1 - c, 1)[0], CORE))
    tail = v[2 * SEGS :]
    side = lambda g: jnp.concatenate([pick(v, SEGS * g, SEGS), tail])
    v = add(side(group), swap(side(1 - group), Y3))
    up, down = swap(v, shift_z(-1)), swap(v, shift_z(1))
    three, two = add(v, up, down), add(v, up)
    chunk = lambda w, i: jnp.concatenate([pick(w, 3 * (i % 4), 3), w[SEGS:]])
    far_up = swap(chunk(three, zl + 1), shift_z(-3))
    far_down = swap(chunk(two, zl + 3), shift_z(3))
    v = add(chunk(three, zl), far_up, far_down)
    v = add(v, swap(v, Y1))
    v = add(v, swap(v, X1))
    v = add(v, swap(v, X3))
    return v, swap(v, CORE)


def local(
    block_in,
    block_out,
    weight,
    adapter_a,
    adapter_b,
    proj,
    w_feature,
    w_embed,
    id_table,
    box_rows,
    box_cols,
    identity,
    face_count,
):
    f, d = lax.axis_index("fsdp"), lax.axis_index("dp")
    place = jnp.stack([f, d % 2, d]).astype(jnp.int32)

    near = id_table
    for perm in (ZPAIR, X1, X3):
        near = jnp.concatenate([near, swap(near, perm)])
    far = swap(near, CORE)

    pay, own_proj = pack(place, weight, proj, adapter_a, adapter_b)
    mine = pay[None]
    for perm in (ZL2, ZL1, Y1, Y3):
        mine = jnp.concatenate([mine, swap(mine, perm)])
    other = swap(mine, CORE)

    pre, emb = face(box_rows, box_cols, block_out, proj, w_feature, w_embed)
    maps, low, cross = low_maps(place, block_in, mine, other)
    sums, wide = main(
        place, box_rows, box_cols, identity, face_count,
        near, far, pre, emb, w_embed, w_feature, block_in, low, cross,
    )
    total, total_far = reduce_all(sums, f, d)
    grad_in = through(wide, maps)
    grad_a, grad_b = last(place, total, total_far, cross, own_proj)
    return grad_in, grad_a, grad_b


def solution(mesh):
    return jax.shard_map(
        local,
        mesh=mesh,
        in_specs=(
            P(("fsdp", "dp"), None),
            P(("fsdp", "dp"), None),
            P("fsdp", None),
            P("fsdp", None),
            P(None, "fsdp"),
            P(),
            P(),
            P(),
            P("dp", None),
            P(("fsdp", "dp"), None),
            P(("fsdp", "dp"), None),
            P(("fsdp", "dp"), None),
            P(("fsdp", "dp")),
        ),
        out_specs=(P(("fsdp", "dp"), None), P("fsdp", None), P(None, "fsdp")),
        check_vma=False,
    )
```

time: 577 us -> 94.7 us (0.16)
  the two profiles are of different devices: /device:TPU:64 before, /device:TPU:1 now
where the time goes in v1:
time: 94.7 us; the launch traced here: 94.2 us
  starting transfers between devices  39.4 us (42%)
  waiting for transfers between devices  23.8 us (25%)
  local copies, waits for them, and re-layouts  15.2 us (16%)
  Pallas kernels  13 us (14%)
  between operations  1.64 us (2%)
  other arithmetic  1.32 us (1%)
    ppermute x19, starting transfers between devices, swap(): return lax.ppermute(value, AXES, perm)  39.4 us
    ppermute x19, waiting for transfers between devices, swap(): return lax.ppermute(value, AXES, perm)  23.8 us
    unnamed x40, local copies, waits for them, and re-layouts  12.7 us
    pallas_call x1, Pallas kernels, main(): pl.pallas_call(main_kernel, out_shape=(jax.ShapeDtypeStruct((2, 2 * SEGS...  4.16 us
    pallas_call x1, Pallas kernels, through(): pl.pallas_call(through_kernel, out_shape=jax.ShapeDtypeStruct((TOK, D), B...  2.31 us
    pallas_call x1, Pallas kernels, face(): pl.pallas_call(face_kernel, out_shape=(jax.ShapeDtypeStruct((8, HID), F32...  2.14 us
    pallas_call x1, Pallas kernels, low_maps(): pl.pallas_call(low_kernel, out_shape=(jax.ShapeDtypeStruct((D, 128), BF),...  1.9 us
  transfers between devices with their start and end apart: 19, of which 11 were waited for; matrix products, arithmetic and copies ran while one was open for 6% of the time, Pallas kernels for 7%

profile of v1, /device:TPU:1, one launch (start us, length us, event | category | flops | bytes accessed | tf_op | source)
XLA Modules:
  0.0 94.2 jit_solution(16328921408264624905)
XLA Ops:
  0.7 1.5 %copy.16.proj = bf16[3072,64]{1,0:T(8,128)(2,1)S(1)} copy(bf16[3072,64]{0,1:T(8,128)(2,1)} %param.18) | data formatting | bytes 786432 | tf_op args[5]
  2.1 0.9 copy.18.a_ref
  3.1 0.8 copy-done.10
  3.9 1.0 %pack.1 = (bf16[128,128]{1,0:T(8,128)(2,1)S(1)}, bf16[192,64]{1,0:T(8,128)(2,1)S(1)}) custom-call(s32[3]{0:T(128)S(1)} %pad_add_fusion.place, bf16[192,3072]{1,0:T(8,128)(2,1)S(1)} %copy-done.7, bf16[3072,64]{1,0:T(8,128)(2,1)S(1)} %copy.16.proj, bf16[192,64]{1,0:T(8,128)(2,1)S(1)} %copy.18.a_ref, bf16[64,192]{1,0:T(8,128)(2,1)S(1)} %copy-done.10), custom_call_target="tpu_custom_call" | custom-call | tf_op jit(solution)/shard_map/pack/pallas_call | solution.py:106
  4.9 3.9 %collective-permute-start.4 = (bf16[1,128,128]{2,1,0:T(8,128)(2,1)S(1)}, bf16[1,128,128]{2,1,0:T(8,128)(2,1)S(1)}, u32[]{:S(2)}, u32[]{:S(2)}) collective-permute-start(bf16[1,128,128]{2,1,0:T(8,128)(2,1)S(1)} %bitcast.10), channel_id=1, source_target_pairs={{0,128},{1,129},{2,130},{3,131},{4,132},{5,133},{6,134},{7,135},{8... | collective-permute-start | bytes 98312 | tf_op jit(solution)/shard_map/ppermute | solution.py:66
  8.8 4.2 %collective-permute-start = (bf16[64,512]{1,0:T(8,128)(2,1)S(1)}, bf16[64,512]{1,0:T(8,128)(2,1)S(1)}, u32[]{:S(2)}, u32[]{:S(2)}) collective-permute-start(bf16[64,512]{1,0:T(8,128)(2,1)S(1)} %copy-done.14), channel_id=1, source_target_pairs={{0,136},{1,137},{2,138},{3,139},{4,140},{5,141},{6,142},{7,143},{8... | collective-permute-start | bytes 196616 | tf_op jit(solution)/shard_map/ppermute | solution.py:66
  13.0 0.6 constant_dynamic-update-slice_fusion.8
  13.6 0.6 constant_dynamic-update-slice_fusion.3
  14.2 0.8 collective-permute-start.5
  15.7 1.3 %collective-permute-start.1 = (bf16[128,512]{1,0:T(8,128)(2,1)S(1)}, bf16[128,512]{1,0:T(8,128)(2,1)S(1)}, u32[]{:S(2)}, u32[]{:S(2)}) collective-permute-start(bf16[128,512]{1,0:T(8,128)(2,1)S(1)} %pad_maximum_fusion.4), channel_id=1, source_target_pairs={{0,2},{1,3},{2,0},{3,1},{4,6},{5,7},{6,4},{7,5},{8,10},{9,11},{10,... | collective-permute-start | bytes 393224 | tf_op jit(solution)/shard_map/ppermute | solution.py:66
  17.5 1.4 %collective-permute-start.6 = (bf16[4,128,128]{2,1,0:T(8,128)(2,1)S(1)}, bf16[4,128,128]{2,1,0:T(8,128)(2,1)S(1)}, u32[]{:S(2)}, u32[]{:S(2)}) collective-permute-start(bf16[4,128,128]{2,1,0:T(8,128)(2,1)S(1)} %pad_maximum_fusion.5), channel_id=1, source_target_pairs={{0,16},{1,17},{2,18},{3,19},{4,20},{5,21},{6,22},{7,23},{8,24},{9,... | collective-permute-start | bytes 393224 | tf_op jit(solution)/shard_map/ppermute | solution.py:66
  18.9 0.6 constant_dynamic-update-slice_fusion.2
  19.5 0.6 constant_dynamic-update-slice_fusion.6
  20.1 1.6 %collective-permute-done.6 = bf16[4,128,128]{2,1,0:T(8,128)(2,1)S(1)} collective-permute-done((bf16[4,128,128]{2,1,0:T(8,128)(2,1)S(1)}, bf16[4,128,128]{2,1,0:T(8,128)(2,1)S(1)}, u32[]{:S(2)}, u32[]{:S(2)}) %collective-permute-start.6) | collective-permute-done | bytes 131104 | tf_op jit(solution)/shard_map/ppermute | solution.py:66
  21.7 2.8 %collective-permute-start.7 = (bf16[8,128,128]{2,1,0:T(8,128)(2,1)S(1)}, bf16[8,128,128]{2,1,0:T(8,128)(2,1)S(1)}, u32[]{:S(2)}, u32[]{:S(2)}) collective-permute-start(bf16[8,128,128]{2,1,0:T(8,128)(2,1)S(1)} %pad_maximum_fusion.1), channel_id=1, source_target_pairs={{0,48},{1,49},{2,50},{3,51},{4,52},{5,53},{6,54},{7,55},{8,56},{9,... | collective-permute-start | bytes 786440 | tf_op jit(solution)/shard_map/ppermute | solution.py:66
  24.6 2.6 %collective-permute-start.2 = (bf16[256,512]{1,0:T(8,128)(2,1)S(1)}, bf16[256,512]{1,0:T(8,128)(2,1)S(1)}, u32[]{:S(2)}, u32[]{:S(2)}) collective-permute-start(bf16[256,512]{1,0:T(8,128)(2,1)S(1)} %pad_maximum_fusion), channel_id=1, source_target_pairs={{0,6},{1,7},{2,4},{3,5},{4,2},{5,3},{6,0},{7,1},{8,14},{9,15},{10,... | collective-permute-start | bytes 786440 | tf_op jit(solution)/shard_map/ppermute | solution.py:66
  27.1 0.7 constant_dynamic-update-slice_fusion.1
  27.8 0.7 constant_dynamic-update-slice_fusion.5
  28.5 0.7 constant_dynamic-update-slice_fusion.4.mine
  29.2 4.1 %collective-permute-start.8 = (bf16[16,128,128]{2,1,0:T(8,128)(2,1)}, bf16[16,128,128]{2,1,0:T(8,128)(2,1)}, u32[]{:S(2)}, u32[]{:S(2)}) collective-permute-start(bf16[16,128,128]{2,1,0:T(8,128)(2,1)} %constant_dynamic-update-slice_fusion.4.mine), channel_id=1, source_target_pairs={{0,1},{1,0},{2,3},{3,2},{4,5},{5,4},{6,7},{7,6},{8,9},{9,8},{10,11... | collective-permute-start | bytes 1572872 | tf_op jit(solution)/shard_map/ppermute | solution.py:66
  33.3 0.7 constant_dynamic-update-slice_fusion.near
  34.0 2.4 %collective-permute-start.3 = (bf16[512,512]{1,0:T(8,128)(2,1)}, bf16[512,512]{1,0:T(8,128)(2,1)}, u32[]{:S(2)}, u32[]{:S(2)}) collective-permute-start(bf16[512,512]{1,0:T(8,128)(2,1)} %constant_dynamic-update-slice_fusion.near), channel_id=1, source_target_pairs={{0,1},{1,0},{2,3},{3,2},{4,5},{5,4},{6,7},{7,6},{8,9},{9,8},{10,11... | collective-permute-start | bytes 1572872 | tf_op jit(solution)/shard_map/ppermute | solution.py:66
  37.1 1.1 %copy-done.2 = bf16[3072,64]{1,0:T(8,128)(2,1)S(1)} copy-done((bf16[3072,64]{1,0:T(8,128)(2,1)S(1)}, bf16[3072,64]{1,0:T(8,128)(2,1)}, u32[]{:S(2)}) %copy-start.2) | copy-done | bytes 393240
  38.3 1.0 %copy-done.4 = bf16[512,512]{1,0:T(8,128)(2,1)S(1)} copy-done((bf16[512,512]{1,0:T(8,128)(2,1)S(1)}, bf16[512,512]{1,0:T(8,128)(2,1)}, u32[]{:S(2)}) %copy-start.4) | copy-done | bytes 524312
  39.3 1.4 %copy-done.6 = bf16[256,3072]{1,0:T(8,128)(2,1)S(1)} copy-done((bf16[256,3072]{1,0:T(8,128)(2,1)S(1)}, bf16[256,3072]{1,0:T(8,128)(2,1)}, u32[]{:S(2)}) %copy-start.6) | copy-done | bytes 1572888
  40.7 2.1 %face.1 = (f32[8,512]{1,0:T(8,128)S(1)}, f32[8,512]{1,0:T(8,128)S(1)}) custom-call(s32[1,6]{1,0:T(1,128)S(1)} %copy-done.11, s32[1,6]{1,0:T(1,128)S(1)} %copy-done.12, bf16[256,3072]{1,0:T(8,128)(2,1)S(1)} %copy-done.6, bf16[3072,64]{1,0:T(8,128)(2,1)S(1)} %copy-done.2, bf16[3136,512]{1,0:T(8,128)(2,1)S(1)} %copy-done, bf16[512,512]{1,0:T(8,128)(2,1)S(1)} %copy-done.4), custom_call_target="tpu_custom_call" | custom-call | tf_op jit(solution)/shard_map/face/pallas_call | solution.py:154
  42.9 1.9 %low.1 = (bf16[3072,128]{1,0:T(8,128)(2,1)S(1)}, bf16[256,128]{1,0:T(8,128)(2,1)S(1)}, f32[64,128]{1,0:T(8,128)S(1)}) custom-call(s32[3]{0:T(128)S(1)} %pad_add_fusion.place, bf16[256,3072]{1,0:T(8,128)(2,1)S(1)} %copy-done.3, bf16[16,128,128]{2,1,0:T(8,128)(2,1)} %constant_dynamic-update-slice_fusion.4.mine, bf16[16,128,128]{2,1,0:T(8,128)(2,1)} %collective-permute-done.8.other), custom_call_target="tpu_custom_call" | custom-call | tf_op jit(solution)/shard_map/low/pallas_call | solution.py:185
  44.8 0.9 copy-done.8
  45.7 4.2 %main.1 = (bf16[2,25,32,128]{3,2,1,0:T(8,128)(2,1)}, bf16[256,128]{1,0:T(8,128)(2,1)S(1)}) custom-call(s32[3]{0:T(128)S(1)} %pad_add_fusion.place, s32[1,6]{1,0:T(1,128)S(1)} %copy-done.11, s32[1,6]{1,0:T(1,128)S(1)} %copy-done.12, s32[1,6]{1,0:T(1,128)S(1)} %copy-done.13, s32[1]{0:T(128)S(6)} %copy.27.count, ...), custom_call_target="tpu_custom_call" | custom-call | tf_op jit(solution)/shard_map/main/pallas_call | solution.py:263
  49.9 0.9 %dynamic-slice_bitcast_fusion = bf16[25,32,128]{2,1,0:T(8,128)(2,1)S(1)} fusion(bf16[2,25,32,128]{3,2,1,0:T(8,128)(2,1)} %get-tuple-element.21, s32[]{:T(128)S(6)} %select_n.55), kind=kLoop, calls=%fused_computation.7 | loop fusion | bytes 409604 | tf_op jit(solution)/shard_map/squeeze | solution.py:333
  51.0 1.4 %collective-permute-done.9 = bf16[25,32,128]{2,1,0:T(8,128)(2,1)S(1)} collective-permute-done((bf16[25,32,128]{2,1,0:T(8,128)(2,1)S(1)}, bf16[25,32,128]{2,1,0:T(8,128)(2,1)S(1)}, u32[]{:S(2)}, u32[]{:S(2)}) %collective-permute-start.9) | collective-permute-done | bytes 204832 | tf_op jit(solution)/shard_map/ppermute | solution.py:66
  52.4 1.0 %fusion = bf16[25,32,128]{2,1,0:T(8,128)(2,1)S(1)} fusion(bf16[25,32,128]{2,1,0:T(8,128)(2,1)S(1)} %collective-permute-done.9, bf16[2,25,32,128]{3,2,1,0:T(8,128)(2,1)} %get-tuple-element.21, s32[]{:T(128)S(6)} %select_n.54), kind=kLoop, calls=%fused_computation.1 | loop fusion | flops 409600 | bytes 614404 | tf_op jit(solution)/shard_map/convert_element_type | solution.py:325
  54.0 5.2 %collective-permute-done.10 = bf16[13,32,128]{2,1,0:T(8,128)(2,1)S(1)} collective-permute-done((bf16[13,32,128]{2,1,0:T(8,128)(2,1)S(1)}, bf16[13,32,128]{2,1,0:T(8,128)(2,1)S(1)}, u32[]{:S(2)}, u32[]{:S(2)}) %collective-permute-start.10) | collective-permute-done | bytes 106528 | tf_op jit(solution)/shard_map/ppermute | solution.py:66
  59.2 1.8 %collective-permute-start.11 = (bf16[13,32,128]{2,1,0:T(8,128)(2,1)S(1)}, bf16[13,32,128]{2,1,0:T(8,128)(2,1)S(1)}, u32[]{:S(2)}, u32[]{:S(2)}) collective-permute-start(bf16[13,32,128]{2,1,0:T(8,128)(2,1)S(1)} %add_convert_fusion.1), channel_id=1, source_target_pairs={{0,200},{1,201},{2,202},{3,203},{4,204},{5,205},{6,206},{7,207},{8... | collective-permute-start | bytes 319496 | tf_op jit(solution)/shard_map/ppermute | solution.py:66
  61.0 1.8 %collective-permute-done.11 = bf16[13,32,128]{2,1,0:T(8,128)(2,1)S(1)} collective-permute-done((bf16[13,32,128]{2,1,0:T(8,128)(2,1)S(1)}, bf16[13,32,128]{2,1,0:T(8,128)(2,1)S(1)}, u32[]{:S(2)}, u32[]{:S(2)}) %collective-permute-start.11) | collective-permute-done | bytes 106528 | tf_op jit(solution)/shard_map/ppermute | solution.py:66
  62.8 3.0 %collective-permute-done.12 = bf16[13,32,128]{2,1,0:T(8,128)(2,1)S(1)} collective-permute-done((bf16[13,32,128]{2,1,0:T(8,128)(2,1)S(1)}, bf16[13,32,128]{2,1,0:T(8,128)(2,1)S(1)}, u32[]{:S(2)}, u32[]{:S(2)}) %collective-permute-start.12) | collective-permute-done | bytes 106528 | tf_op jit(solution)/shard_map/ppermute | solution.py:66
  65.9 0.7 collective-permute-start.13
  66.6 2.9 %collective-permute-start.14 = (bf16[4,32,128]{2,1,0:T(8,128)(2,1)S(1)}, bf16[4,32,128]{2,1,0:T(8,128)(2,1)S(1)}, u32[]{:S(2)}, u32[]{:S(2)}) collective-permute-start(bf16[4,32,128]{2,1,0:T(8,128)(2,1)S(1)} %pad_maximum_fusion.9), channel_id=1, source_target_pairs={{0,192},{1,193},{2,194},{3,195},{4,196},{5,197},{6,198},{7,199},{8... | collective-permute-start | bytes 98312 | tf_op jit(solution)/shard_map/ppermute | solution.py:66
  69.5 1.9 %collective-permute-done.13 = bf16[4,32,128]{2,1,0:T(8,128)(2,1)S(1)} collective-permute-done((bf16[4,32,128]{2,1,0:T(8,128)(2,1)S(1)}, bf16[4,32,128]{2,1,0:T(8,128)(2,1)S(1)}, u32[]{:S(2)}, u32[]{:S(2)}) %collective-permute-start.13) | collective-permute-done | bytes 32800 | tf_op jit(solution)/shard_map/ppermute | solution.py:66
  71.4 1.1 %collective-permute-done.14 = bf16[4,32,128]{2,1,0:T(8,128)(2,1)S(1)} collective-permute-done((bf16[4,32,128]{2,1,0:T(8,128)(2,1)S(1)}, bf16[4,32,128]{2,1,0:T(8,128)(2,1)S(1)}, u32[]{:S(2)}, u32[]{:S(2)}) %collective-permute-start.14) | collective-permute-done | bytes 32800 | tf_op jit(solution)/shard_map/ppermute | solution.py:66
  72.6 3.0 %collective-permute-done.15 = bf16[4,32,128]{2,1,0:T(8,128)(2,1)S(1)} collective-permute-done((bf16[4,32,128]{2,1,0:T(8,128)(2,1)S(1)}, bf16[4,32,128]{2,1,0:T(8,128)(2,1)S(1)}, u32[]{:S(2)}, u32[]{:S(2)}) %collective-permute-start.15) | collective-permute-done | bytes 32800 | tf_op jit(solution)/shard_map/ppermute | solution.py:66
  75.8 2.8 %collective-permute-done.16 = bf16[4,32,128]{2,1,0:T(8,128)(2,1)S(1)} collective-permute-done((bf16[4,32,128]{2,1,0:T(8,128)(2,1)S(1)}, bf16[4,32,128]{2,1,0:T(8,128)(2,1)S(1)}, u32[]{:S(2)}, u32[]{:S(2)}) %collective-permute-start.16) | collective-permute-done | bytes 32800 | tf_op jit(solution)/shard_map/ppermute | solution.py:66
  78.5 2.5 %collective-permute-start.17 = (bf16[4,32,128]{2,1,0:T(8,128)(2,1)S(1)}, bf16[4,32,128]{2,1,0:T(8,128)(2,1)S(1)}, u32[]{:S(2)}, u32[]{:S(2)}) collective-permute-start(bf16[4,32,128]{2,1,0:T(8,128)(2,1)S(1)} %add_convert_fusion.3), channel_id=1, source_target_pairs={{0,6},{1,7},{2,4},{3,5},{4,2},{5,3},{6,0},{7,1},{8,14},{9,15},{10,... | collective-permute-start | bytes 98312 | tf_op jit(solution)/shard_map/ppermute | solution.py:66
  81.0 1.6 %collective-permute-done.17 = bf16[4,32,128]{2,1,0:T(8,128)(2,1)S(1)} collective-permute-done((bf16[4,32,128]{2,1,0:T(8,128)(2,1)S(1)}, bf16[4,32,128]{2,1,0:T(8,128)(2,1)S(1)}, u32[]{:S(2)}, u32[]{:S(2)}) %collective-permute-start.17) | collective-permute-done | bytes 32800 | tf_op jit(solution)/shard_map/ppermute | solution.py:66
  82.6 7.1 %collective-permute-start.18 = (bf16[4,32,128]{2,1,0:T(8,128)(2,1)S(1)}, bf16[4,32,128]{2,1,0:T(8,128)(2,1)S(1)}, u32[]{:S(2)}, u32[]{:S(2)}) collective-permute-start(bf16[4,32,128]{2,1,0:T(8,128)(2,1)S(1)} %add_convert_fusion.2.mine), channel_id=1, source_target_pairs={{0,1},{1,0},{2,3},{3,2},{4,5},{5,4},{6,7},{7,6},{8,9},{9,8},{10,11... | collective-permute-start | bytes 98312 | tf_op jit(solution)/shard_map/ppermute | solution.py:66
  89.7 2.3 %through.1 = bf16[256,3072]{1,0:T(8,128)(2,1)} custom-call(bf16[256,128]{1,0:T(8,128)(2,1)S(1)} %get-tuple-element.19.wide, bf16[3072,128]{1,0:T(8,128)(2,1)S(1)} %copy-done.9), custom_call_target="tpu_custom_call" | custom-call | tf_op jit(solution)/shard_map/through/pallas_call | solution.py:282
  92.0 1.5 %last.1 = (f32[192,64]{1,0:T(8,128)S(1)}, f32[64,192]{1,0:T(8,128)}) custom-call(s32[3]{0:T(128)S(1)} %pad_add_fusion.place, bf16[4,32,128]{2,1,0:T(8,128)(2,1)S(1)} %add_convert_fusion.2.mine, bf16[4,32,128]{2,1,0:T(8,128)(2,1)S(1)} %collective-permute-done.18.other, f32[64,128]{1,0:T(8,128)S(1)} %get-tuple-element.18.cross, ...), custom_call_target="tpu_custom_call" | custom-call | tf_op jit(solution)/shard_map/last/pallas_call | solution.py:310
  93.5 0.7 copy.19
  (61 shorter events, 2.4 us)
Async XLA Ops:
  0.6 2.5 %copy-start.7 = (bf16[192,3072]{1,0:T(8,128)(2,1)S(1)}, bf16[192,3072]{1,0:T(8,128)(2,1)}, u32[]{:S(2)}) copy-start(bf16[192,3072]{1,0:T(8,128)(2,1)} %weight.1) | copy-start | bytes 3538948
  0.7 8.1 %copy-start.14 = (bf16[64,512]{1,0:T(8,128)(2,1)S(1)}, bf16[64,512]{1,0:T(8,128)(2,1)}, u32[]{:S(2)}) copy-start(bf16[64,512]{1,0:T(8,128)(2,1)} %param.21) | copy-start | bytes 196612
  2.1 13.5 %copy-start.1 = (bf16[3072,64]{1,0:T(8,128)(2,1)}, bf16[3072,64]{1,0:T(8,128)(2,1)S(1)}, u32[]{:S(2)}) copy-start(bf16[3072,64]{1,0:T(8,128)(2,1)S(1)} %copy.16.proj) | copy-start | bytes 1179652
  3.1 0.8 copy-start.10
  4.9 9.3 %collective-permute-start.4 = (bf16[1,128,128]{2,1,0:T(8,128)(2,1)S(1)}, bf16[1,128,128]{2,1,0:T(8,128)(2,1)S(1)}, u32[]{:S(2)}, u32[]{:S(2)}) collective-permute-start(bf16[1,128,128]{2,1,0:T(8,128)(2,1)S(1)} %bitcast.10), channel_id=1, source_target_pairs={{0,128},{1,129},{2,130},{3,131},{4,132},{5,133},{6,134},{7,135},{8... | collective-permute-start | bytes 98312 | tf_op jit(solution)/shard_map/ppermute | solution.py:66
  8.8 6.9 %collective-permute-start = (bf16[64,512]{1,0:T(8,128)(2,1)S(1)}, bf16[64,512]{1,0:T(8,128)(2,1)S(1)}, u32[]{:S(2)}, u32[]{:S(2)}) collective-permute-start(bf16[64,512]{1,0:T(8,128)(2,1)S(1)} %copy-done.14), channel_id=1, source_target_pairs={{0,136},{1,137},{2,138},{3,139},{4,140},{5,141},{6,142},{7,143},{8... | collective-permute-start | bytes 196616 | tf_op jit(solution)/shard_map/ppermute | solution.py:66
  14.2 3.3 %collective-permute-start.5 = (bf16[2,128,128]{2,1,0:T(8,128)(2,1)S(1)}, bf16[2,128,128]{2,1,0:T(8,128)(2,1)S(1)}, u32[]{:S(2)}, u32[]{:S(2)}) collective-permute-start(bf16[2,128,128]{2,1,0:T(8,128)(2,1)S(1)} %pad_maximum_fusion.6), channel_id=1, source_target_pairs={{0,64},{1,65},{2,66},{3,67},{4,68},{5,69},{6,70},{7,71},{8,72},{9,... | collective-permute-start | bytes 196616 | tf_op jit(solution)/shard_map/ppermute | solution.py:66
  15.7 21.4 %copy-start = (bf16[3136,512]{1,0:T(8,128)(2,1)S(1)}, bf16[3136,512]{1,0:T(8,128)(2,1)}, u32[]{:S(2)}) copy-start(bf16[3136,512]{1,0:T(8,128)(2,1)} %w_feature.3) | copy-start | bytes 9633796
  15.7 21.4 %copy-start.11 = (s32[1,6]{1,0:T(1,128)S(1)}, s32[1,6]{1,0:T(1,128)}, u32[]{:S(2)}) copy-start(s32[1,6]{1,0:T(1,128)} %rows.3) | copy-start | bytes 76
  15.7 21.4 %copy-start.12 = (s32[1,6]{1,0:T(1,128)S(1)}, s32[1,6]{1,0:T(1,128)}, u32[]{:S(2)}) copy-start(s32[1,6]{1,0:T(1,128)} %cols.3) | copy-start | bytes 76
  15.7 8.9 %collective-permute-start.1 = (bf16[128,512]{1,0:T(8,128)(2,1)S(1)}, bf16[128,512]{1,0:T(8,128)(2,1)S(1)}, u32[]{:S(2)}, u32[]{:S(2)}) collective-permute-start(bf16[128,512]{1,0:T(8,128)(2,1)S(1)} %pad_maximum_fusion.4), channel_id=1, source_target_pairs={{0,2},{1,3},{2,0},{3,1},{4,6},{5,7},{6,4},{7,5},{8,10},{9,11},{10,... | collective-permute-start | bytes 393224 | tf_op jit(solution)/shard_map/ppermute | solution.py:66
  17.5 4.2 %collective-permute-start.6 = (bf16[4,128,128]{2,1,0:T(8,128)(2,1)S(1)}, bf16[4,128,128]{2,1,0:T(8,128)(2,1)S(1)}, u32[]{:S(2)}, u32[]{:S(2)}) collective-permute-start(bf16[4,128,128]{2,1,0:T(8,128)(2,1)S(1)} %pad_maximum_fusion.5), channel_id=1, source_target_pairs={{0,16},{1,17},{2,18},{3,19},{4,20},{5,21},{6,22},{7,23},{8,24},{9,... | collective-permute-start | bytes 393224 | tf_op jit(solution)/shard_map/ppermute | solution.py:66
  21.7 6.7 %collective-permute-start.7 = (bf16[8,128,128]{2,1,0:T(8,128)(2,1)S(1)}, bf16[8,128,128]{2,1,0:T(8,128)(2,1)S(1)}, u32[]{:S(2)}, u32[]{:S(2)}) collective-permute-start(bf16[8,128,128]{2,1,0:T(8,128)(2,1)S(1)} %pad_maximum_fusion.1), channel_id=1, source_target_pairs={{0,48},{1,49},{2,50},{3,51},{4,52},{5,53},{6,54},{7,55},{8,56},{9,... | collective-permute-start | bytes 786440 | tf_op jit(solution)/shard_map/ppermute | solution.py:66
  24.6 8.7 %collective-permute-start.2 = (bf16[256,512]{1,0:T(8,128)(2,1)S(1)}, bf16[256,512]{1,0:T(8,128)(2,1)S(1)}, u32[]{:S(2)}, u32[]{:S(2)}) collective-permute-start(bf16[256,512]{1,0:T(8,128)(2,1)S(1)} %pad_maximum_fusion), channel_id=1, source_target_pairs={{0,6},{1,7},{2,4},{3,5},{4,2},{5,3},{6,0},{7,1},{8,14},{9,15},{10,... | collective-permute-start | bytes 786440 | tf_op jit(solution)/shard_map/ppermute | solution.py:66
  29.2 13.7 %collective-permute-start.8 = (bf16[16,128,128]{2,1,0:T(8,128)(2,1)}, bf16[16,128,128]{2,1,0:T(8,128)(2,1)}, u32[]{:S(2)}, u32[]{:S(2)}) collective-permute-start(bf16[16,128,128]{2,1,0:T(8,128)(2,1)} %constant_dynamic-update-slice_fusion.4.mine), channel_id=1, source_target_pairs={{0,1},{1,0},{2,3},{3,2},{4,5},{5,4},{6,7},{7,6},{8,9},{9,8},{10,11... | collective-permute-start | bytes 1572872 | tf_op jit(solution)/shard_map/ppermute | solution.py:66
  34.0 11.6 %collective-permute-start.3 = (bf16[512,512]{1,0:T(8,128)(2,1)}, bf16[512,512]{1,0:T(8,128)(2,1)}, u32[]{:S(2)}, u32[]{:S(2)}) collective-permute-start(bf16[512,512]{1,0:T(8,128)(2,1)} %constant_dynamic-update-slice_fusion.near), channel_id=1, source_target_pairs={{0,1},{1,0},{2,3},{3,2},{4,5},{5,4},{6,7},{7,6},{8,9},{9,8},{10,11... | collective-permute-start | bytes 1572872 | tf_op jit(solution)/shard_map/ppermute | solution.py:66
  37.1 1.1 %copy-start.2 = (bf16[3072,64]{1,0:T(8,128)(2,1)S(1)}, bf16[3072,64]{1,0:T(8,128)(2,1)}, u32[]{:S(2)}) copy-start(bf16[3072,64]{1,0:T(8,128)(2,1)} %copy-done.1) | copy-start | bytes 1179652
  38.3 1.0 %copy-start.4 = (bf16[512,512]{1,0:T(8,128)(2,1)S(1)}, bf16[512,512]{1,0:T(8,128)(2,1)}, u32[]{:S(2)}) copy-start(bf16[512,512]{1,0:T(8,128)(2,1)} %w_embed.3) | copy-start | bytes 1572868
  39.3 1.4 %copy-start.6 = (bf16[256,3072]{1,0:T(8,128)(2,1)S(1)}, bf16[256,3072]{1,0:T(8,128)(2,1)}, u32[]{:S(2)}) copy-start(bf16[256,3072]{1,0:T(8,128)(2,1)} %y_ref.1) | copy-start | bytes 4718596
  40.7 2.2 %copy-start.3 = (bf16[256,3072]{1,0:T(8,128)(2,1)S(1)}, bf16[256,3072]{1,0:T(8,128)(2,1)}, u32[]{:S(2)}) copy-start(bf16[256,3072]{1,0:T(8,128)(2,1)} %x_ref.3) | copy-start | bytes 4718596
  42.9 2.8 %copy-start.5 = (bf16[512,512]{1,0:T(8,128)(2,1)S(1)}, bf16[512,512]{1,0:T(8,128)(2,1)}, u32[]{:S(2)}) copy-start(bf16[512,512]{1,0:T(8,128)(2,1)} %w_embed.3) | copy-start | bytes 1572868
  42.9 2.8 %copy-start.13 = (s32[1,6]{1,0:T(1,128)S(1)}, s32[1,6]{1,0:T(1,128)}, u32[]{:S(2)}) copy-start(s32[1,6]{1,0:T(1,128)} %ident.1) | copy-start | bytes 76
  44.8 0.9 copy-start.8
  50.8 38.9 %copy-start.9 = (bf16[3072,128]{1,0:T(8,128)(2,1)S(1)}, bf16[3072,128]{1,0:T(8,128)(2,1)}, u32[]{:S(2)}) copy-start(bf16[3072,128]{1,0:T(8,128)(2,1)} %copy-done.8) | copy-start | bytes 2359300
  50.8 1.5 %collective-permute-start.9 = (bf16[25,32,128]{2,1,0:T(8,128)(2,1)S(1)}, bf16[25,32,128]{2,1,0:T(8,128)(2,1)S(1)}, u32[]{:S(2)}, u32[]{:S(2)}) collective-permute-start(bf16[25,32,128]{2,1,0:T(8,128)(2,1)S(1)} %dynamic-slice_bitcast_fusion), channel_id=1, source_target_pairs={{0,1},{1,0},{2,3},{3,2},{4,5},{5,4},{6,7},{7,6},{8,9},{9,8},{10,11... | collective-permute-start | bytes 614408 | tf_op jit(solution)/shard_map/ppermute | solution.py:66
  53.4 5.7 %collective-permute-start.10 = (bf16[13,32,128]{2,1,0:T(8,128)(2,1)S(1)}, bf16[13,32,128]{2,1,0:T(8,128)(2,1)S(1)}, u32[]{:S(2)}, u32[]{:S(2)}) collective-permute-start(bf16[13,32,128]{2,1,0:T(8,128)(2,1)S(1)} %pad_maximum_fusion.2), channel_id=1, source_target_pairs={{0,48},{1,49},{2,50},{3,51},{4,52},{5,53},{6,54},{7,55},{8,56},{9,... | collective-permute-start | bytes 319496 | tf_op jit(solution)/shard_map/ppermute | solution.py:66
  59.2 3.6 %collective-permute-start.11 = (bf16[13,32,128]{2,1,0:T(8,128)(2,1)S(1)}, bf16[13,32,128]{2,1,0:T(8,128)(2,1)S(1)}, u32[]{:S(2)}, u32[]{:S(2)}) collective-permute-start(bf16[13,32,128]{2,1,0:T(8,128)(2,1)S(1)} %add_convert_fusion.1), channel_id=1, source_target_pairs={{0,200},{1,201},{2,202},{3,203},{4,204},{5,205},{6,206},{7,207},{8... | collective-permute-start | bytes 319496 | tf_op jit(solution)/shard_map/ppermute | solution.py:66
  61.0 4.8 %collective-permute-start.12 = (bf16[13,32,128]{2,1,0:T(8,128)(2,1)S(1)}, bf16[13,32,128]{2,1,0:T(8,128)(2,1)S(1)}, u32[]{:S(2)}, u32[]{:S(2)}) collective-permute-start(bf16[13,32,128]{2,1,0:T(8,128)(2,1)S(1)} %add_convert_fusion.1), channel_id=1, source_target_pairs={{0,64},{1,65},{2,66},{3,67},{4,68},{5,69},{6,70},{7,71},{8,72},{9,... | collective-permute-start | bytes 319496 | tf_op jit(solution)/shard_map/ppermute | solution.py:66
  65.9 5.5 %collective-permute-start.13 = (bf16[4,32,128]{2,1,0:T(8,128)(2,1)S(1)}, bf16[4,32,128]{2,1,0:T(8,128)(2,1)S(1)}, u32[]{:S(2)}, u32[]{:S(2)}) collective-permute-start(bf16[4,32,128]{2,1,0:T(8,128)(2,1)S(1)} %pad_maximum_fusion.7), channel_id=1, source_target_pairs={{0,72},{1,73},{2,74},{3,75},{4,76},{5,77},{6,78},{7,79},{8,64},{9,... | collective-permute-start | bytes 98312 | tf_op jit(solution)/shard_map/ppermute | solution.py:66
  66.6 5.9 %collective-permute-start.14 = (bf16[4,32,128]{2,1,0:T(8,128)(2,1)S(1)}, bf16[4,32,128]{2,1,0:T(8,128)(2,1)S(1)}, u32[]{:S(2)}, u32[]{:S(2)}) collective-permute-start(bf16[4,32,128]{2,1,0:T(8,128)(2,1)S(1)} %pad_maximum_fusion.9), channel_id=1, source_target_pairs={{0,192},{1,193},{2,194},{3,195},{4,196},{5,197},{6,198},{7,199},{8... | collective-permute-start | bytes 98312 | tf_op jit(solution)/shard_map/ppermute | solution.py:66
  72.5 3.1 %collective-permute-start.15 = (bf16[4,32,128]{2,1,0:T(8,128)(2,1)S(1)}, bf16[4,32,128]{2,1,0:T(8,128)(2,1)S(1)}, u32[]{:S(2)}, u32[]{:S(2)}) collective-permute-start(bf16[4,32,128]{2,1,0:T(8,128)(2,1)S(1)} %add_convert_fusion.5), channel_id=1, source_target_pairs={{0,16},{1,17},{2,18},{3,19},{4,20},{5,21},{6,22},{7,23},{8,24},{9,... | collective-permute-start | bytes 98312 | tf_op jit(solution)/shard_map/ppermute | solution.py:66
  75.7 2.9 %collective-permute-start.16 = (bf16[4,32,128]{2,1,0:T(8,128)(2,1)S(1)}, bf16[4,32,128]{2,1,0:T(8,128)(2,1)S(1)}, u32[]{:S(2)}, u32[]{:S(2)}) collective-permute-start(bf16[4,32,128]{2,1,0:T(8,128)(2,1)S(1)} %add_convert_fusion.4), channel_id=1, source_target_pairs={{0,2},{1,3},{2,0},{3,1},{4,6},{5,7},{6,4},{7,5},{8,10},{9,11},{10,... | collective-permute-start | bytes 98312 | tf_op jit(solution)/shard_map/ppermute | solution.py:66
  78.5 4.1 %collective-permute-start.17 = (bf16[4,32,128]{2,1,0:T(8,128)(2,1)S(1)}, bf16[4,32,128]{2,1,0:T(8,128)(2,1)S(1)}, u32[]{:S(2)}, u32[]{:S(2)}) collective-permute-start(bf16[4,32,128]{2,1,0:T(8,128)(2,1)S(1)} %add_convert_fusion.3), channel_id=1, source_target_pairs={{0,6},{1,7},{2,4},{3,5},{4,2},{5,3},{6,0},{7,1},{8,14},{9,15},{10,... | collective-permute-start | bytes 98312 | tf_op jit(solution)/shard_map/ppermute | solution.py:66
  82.6 9.4 %collective-permute-start.18 = (bf16[4,32,128]{2,1,0:T(8,128)(2,1)S(1)}, bf16[4,32,128]{2,1,0:T(8,128)(2,1)S(1)}, u32[]{:S(2)}, u32[]{:S(2)}) collective-permute-start(bf16[4,32,128]{2,1,0:T(8,128)(2,1)S(1)} %add_convert_fusion.2.mine), channel_id=1, source_target_pairs={{0,1},{1,0},{2,3},{3,2},{4,5},{5,4},{6,7},{7,6},{8,9},{9,8},{10,11... | collective-permute-start | bytes 98312 | tf_op jit(solution)/shard_map/ppermute | solution.py:66

commit v2 on v1

v2 whole, which is shorter than its diff:
```python
import jax
import jax.numpy as jnp
from jax import lax
from jax.experimental import pallas as pl
from jax.experimental.pallas import tpu as pltpu
from jax.sharding import PartitionSpec as P

D = 3072
CH = 64
RANK = 64
HID = 512
EMB = 512
FACE = 7
MAXF = 6
GW = 16
IDS_DEV = 64
TOK = 256
CROP = 3136
SHARD = 192
PAIR = 2 * SHARD
KH = 32
GROUPS = 12
ROWS = GROUPS * 8
UNITS = 48
BLOCK = 512

loss_scale = 1024.0
eps_norm = 1e-06
BF = jnp.bfloat16
F32 = jnp.float32
AXES = ("fsdp", "dp")


def coords(index):
    f, d = index // 16, index % 16
    return f // 4, f % 4, d // 8, (d // 2) % 4, d % 2


def number(zl, y, zh, x, c):
    return (zl * 4 + y) * 16 + zh * 8 + x * 2 + c


def flip(zl=0, y=0, zh=0, x=0, c=0):
    move = lambda l, b, h, a, e: (l ^ zl, b ^ y, h ^ zh, a ^ x, e ^ c)
    return [(i, number(*move(*coords(i)))) for i in range(256)]


def send(value, perm):
    return lax.ppermute(value, AXES, perm)


def after(value, *others):
    return lax.optimization_barrier((value,) + others)[0]


def dot(a, b, da, db):
    return lax.dot_general(a, b, (((da,), (db,)), ((), ())), preferred_element_type=F32)


def shifted(rows, width, offset):
    r = lax.broadcasted_iota(jnp.int32, (rows, width), 0)
    c = lax.broadcasted_iota(jnp.int32, (rows, width), 1)
    return (c == r + offset).astype(BF)


def params(mib):
    return pltpu.CompilerParams(vmem_limit_bytes=mib << 20)


def cost(us):
    return pl.CostEstimate(flops=us, bytes_accessed=us, transcendentals=0)


def vmem(n):
    return [pl.BlockSpec(memory_space=pltpu.VMEM)] * n


SMEM = pl.BlockSpec(memory_space=pltpu.SMEM)


HBM = pl.BlockSpec(memory_space=pl.ANY)


def load_all(pairs_of, sems):
    copies = [pltpu.make_async_copy(a, b, sems.at[n]) for n, (a, b) in enumerate(pairs_of)]
    for copy in copies:
        copy.start()
    return copies


def corner_of(rows, cols, slot):
    corner = jnp.zeros_like(slot)
    for k in range(MAXF):
        corner = jnp.where(slot == k, rows[0, k] * GW + cols[0, k], corner)
    return corner


def token_of(rows, cols, index, i):
    slot = index & 7
    p = 4 * (index >> 3) + i
    down = (p * 37) >> 8
    token = corner_of(rows, cols, slot) + down * GW + (p - down * FACE)
    return jnp.where((slot < MAXF) & (p < FACE * FACE), token, -1)


def load_all(moves, sems):
    copies = [pltpu.make_async_copy(a, b, sems.at[n]) for n, (a, b) in enumerate(moves)]
    for copy in copies:
        copy.start()
    return copies


def pack_kernel(
    place, proj_hbm, weight_hbm, a_hbm, b_hbm, pay, own_ref,
    proj_t, weight, a_ref, b_ref, sems,
):
    f, c = place[0], place[1]
    copies = load_all(
        (
            (proj_hbm, proj_t),
            (weight_hbm, weight),
            (a_hbm, a_ref),
            (b_hbm, b_ref),
        ),
        sems,
    )
    for copy in copies:
        copy.wait()
    window = proj_t[:, pl.ds(pl.multiple_of((f >> 1) * PAIR, 128), PAIR)]
    own = dot(window, shifted(SHARD, PAIR, (f & 1) * SHARD), 1, 1).astype(BF)
    own_ref[...] = own

    @pl.when(c == 0)
    def _():
        pay[0] = dot(a_ref[...], shifted(SHARD, 256, 0), 1, 0).astype(BF)

    @pl.when(c == 1)
    def _():
        moved = (dot(proj_t[...], weight[...], 1, 1) + own.astype(F32)).astype(BF)
        cross = dot(own, b_ref[...], 1, 1).astype(BF)
        wide = dot(moved, shifted(SHARD, 256, 0), 1, 0)
        pay[0] = (wide + dot(cross, shifted(CH, 256, SHARD), 1, 0)).astype(BF)


def pack(*args):
    return pl.pallas_call(
        pack_kernel,
        out_shape=(
            jax.ShapeDtypeStruct((1, CH, 256), BF),
            jax.ShapeDtypeStruct((CH, SHARD), BF),
        ),
        in_specs=[SMEM] + [HBM] * 4,
        out_specs=tuple(vmem(2)),
        scratch_shapes=[
            pltpu.VMEM((CH, D), BF),
            pltpu.VMEM((SHARD, D), BF),
            pltpu.VMEM((RANK, SHARD), BF),
            pltpu.VMEM((RANK, SHARD), BF),
            pltpu.SemaphoreType.DMA((4,)),
        ],
        compiler_params=params(52),
        cost_estimate=cost(2),
        name="pack",
    )(*args)


def face_kernel(
    rows, cols, y_hbm, proj_hbm, feature_hbm, embed_hbm, pre_ref, emb_ref,
    y_ref, proj_t, w_feature, w_embed, sems,
):
    copies = load_all(
        (
            (proj_hbm, proj_t),
            (y_hbm, y_ref),
            (feature_hbm, w_feature),
            (embed_hbm, w_embed),
        ),
        sems,
    )
    n = ROWS + 8
    index = lax.broadcasted_iota(jnp.int32, (n, TOK), 0)
    token = lax.broadcasted_iota(jnp.int32, (n, TOK), 1)
    picks = [(token_of(rows, cols, index, i) == token).astype(BF) for i in range(4)]
    copies[0].wait()
    copies[1].wait()
    latent = dot(y_ref[...], proj_t[...], 1, 1).astype(BF)
    crops = jnp.zeros((n, 256), F32)
    for i in range(4):
        wide = dot(latent, shifted(CH, 256, CH * i), 1, 0).astype(BF)
        crops += dot(picks[i], wide, 1, 0)
    crops = crops.astype(BF)
    copies[2].wait()
    pre = dot(crops[ROWS:n, 0:CH], w_feature[GROUPS * 256 : CROP, :], 1, 0)
    for g in range(GROUPS):
        pre += dot(crops[8 * g : 8 * g + 8, :], w_feature[256 * g : 256 * g + 256, :], 1, 0)
    pre_ref[...] = pre
    feature = jax.nn.gelu(pre).astype(BF)
    copies[3].wait()
    emb_ref[...] = dot(feature, w_embed[...], 1, 0)


def face(*args):
    return pl.pallas_call(
        face_kernel,
        out_shape=(
            jax.ShapeDtypeStruct((8, HID), F32),
            jax.ShapeDtypeStruct((8, EMB), F32),
        ),
        in_specs=[SMEM, SMEM] + [HBM] * 4,
        out_specs=tuple(vmem(2)),
        scratch_shapes=[
            pltpu.VMEM((TOK, D), BF),
            pltpu.VMEM((CH, D), BF),
            pltpu.VMEM((CROP, HID), BF),
            pltpu.VMEM((HID, EMB), BF),
            pltpu.SemaphoreType.DMA((4,)),
        ],
        compiler_params=params(52),
        cost_estimate=cost(4),
        name="face",
    )(*args)


def side_by_side(f, c, kind, near, far, near_2, far_2):
    zl, y = f >> 2, f & 3
    even = (y & 1) == 0
    lane = lax.broadcasted_iota(jnp.int32, (CH, 128), 1)
    for step, (a_ref, b_ref) in enumerate(((near, near_2), (far, far_2))):
        own_y = y ^ (3 * step)
        first = even if step == 0 else jnp.logical_not(even)
        for i in range(4):
            crossed = (i & 1) + (i >> 1) + step
            here = (c ^ (crossed & 1)) == kind
            a = jnp.where(here, a_ref[i], b_ref[i])
            b = jnp.where(here, b_ref[i + 4], a_ref[i + 4])
            left = jnp.where(first, a, b).astype(F32)
            right = jnp.where(first, b, a).astype(F32)
            turned = pltpu.roll(right[:, 0:128], 64, 1)
            tiles = (
                left[:, 0:128],
                jnp.where(lane < 64, left[:, 128:256], turned),
                jnp.where(lane < 64, turned, pltpu.roll(right[:, 128:256], 64, 1)),
            )
            p = (zl ^ (2 * (i & 1) + (i >> 1))) * 2 + (own_y >> 1)
            yield p, [t.astype(BF) for t in tiles], left[:, 128:256] + right[:, 128:256]


def low_kernel(place, x_ref, latent, near, far, near_2, far_2, maps, keep, give):
    f, c = place[0], place[1]
    total = jnp.zeros((TOK, RANK), F32)
    for p, tiles, _ in side_by_side(f, c, 0, near, far, near_2, far_2):
        for t in range(3):
            spot = pl.ds(pl.multiple_of(p * PAIR + 128 * t, 128), 128)
            maps[:, spot] = tiles[t]
        spot = pl.ds(pl.multiple_of(p * PAIR, 128), PAIR)
        total += dot(x_ref[:, spot], maps[:, spot], 1, 1)
    part = dot(latent[...], dot(total.astype(BF), shifted(RANK, 128, 0), 1, 0).astype(BF), 0, 0)
    lane = lax.broadcasted_iota(jnp.int32, (KH, 128), 1)
    unit = jnp.where(lane < 64, part[0:KH], pltpu.roll(part[KH : 2 * KH], 64, 1)).astype(BF)
    top, bottom = unit[0 : KH // 2], unit[KH // 2 : KH]
    keep[0] = jnp.where(c == 0, top, bottom)
    give[0] = jnp.where(c == 0, bottom, top)


def low_maps(*args):
    share = jax.ShapeDtypeStruct((1, KH // 2, 128), BF)
    return pl.pallas_call(
        low_kernel,
        out_shape=(jax.ShapeDtypeStruct((RANK, D), BF), share, share),
        in_specs=[SMEM] + vmem(6),
        out_specs=tuple(vmem(3)),
        compiler_params=params(16),
        cost_estimate=cost(2),
        name="low",
    )(*args)


def gelu_slope(preact):
    return jax.jvp(jax.nn.gelu, (preact,), (jnp.ones_like(preact),))[1]


def main_kernel(
    place, rows, cols, ident, count, near_0, near_1, far_0, far_1,
    pre_ref, emb_ref, w_embed, w_feature, x_ref, keep, give, latent_ref,
):
    c, d = place[1], place[2]
    slot = lax.broadcasted_iota(jnp.int32, (8, 16), 0)
    lane = lax.broadcasted_iota(jnp.int32, (8, 16), 1)
    refer = jnp.zeros((8, EMB), F32)
    for k in range(MAXF):
        who = ident[0, k]
        apart = (who >> 6) ^ d
        dz, dx = apart >> 3, (apart >> 1) & 3
        here = ((apart ^ dz ^ dx) & 1) == 0
        spot = ((dx ^ (dx >> 1)) & 1) * 128 + dz * IDS_DEV + (who & 63)
        at = pl.ds(pl.multiple_of((spot >> 4) * 16, 16), 16)
        near = jnp.where(dx < 2, near_0[at, :], near_1[at, :])
        far = jnp.where(dx < 2, far_0[at, :], far_1[at, :])
        live = (slot == k) & (lane == (spot & 15)) & (k < count[0])
        refer += dot(live.astype(BF), jnp.where(here, near, far), 1, 0)
    emb = emb_ref[...]
    norm_e = jnp.sqrt(jnp.sum(emb * emb, axis=-1, keepdims=True) + eps_norm)
    norm_r = jnp.sqrt(jnp.sum(refer * refer, axis=-1, keepdims=True) + eps_norm)
    cosine = jnp.sum(emb * refer, axis=-1, keepdims=True) / (norm_e * norm_r)
    d_embed = (
        loss_scale * (refer / (norm_e * norm_r) - cosine * emb / (norm_e * norm_e))
    ).astype(BF)
    d_feature = dot(d_embed, w_embed[...], 1, 1)
    d_pre = (d_feature * gelu_slope(pre_ref[...])).astype(BF)
    parts = [
        dot(d_pre, w_feature[256 * g : 256 * g + 256, :], 1, 1) for g in range(GROUPS)
    ]
    d_crop = jnp.concatenate(parts, axis=0).astype(BF)
    last = dot(d_pre, w_feature[GROUPS * 256 : CROP, :], 1, 1).astype(BF)
    index = lax.broadcasted_iota(jnp.int32, (TOK, ROWS), 1)
    token = lax.broadcasted_iota(jnp.int32, (TOK, ROWS), 0)
    tail = lax.broadcasted_iota(jnp.int32, (TOK, 8), 1) + ROWS
    pick = (token_of(rows, cols, tail, 0) == token[:, 0:8]).astype(BF)
    d_latent = dot(pick, last, 1, 0)
    for i in range(4):
        pick = (token_of(rows, cols, index, i) == token).astype(BF)
        piece = dot(d_crop, shifted(CH, 256, CH * i), 1, 1).astype(BF)
        d_latent += dot(pick, piece, 1, 0)
    d_latent = d_latent.astype(BF)
    latent_ref[...] = d_latent
    lane = lax.broadcasted_iota(jnp.int32, (KH, 128), 1)
    for p in range(8):
        part = dot(d_latent, x_ref[:, p * PAIR : p * PAIR + PAIR], 0, 0)
        for u in range(6):
            top = part[0:KH, 128 * (u // 2) : 128 * (u // 2) + 128]
            bottom = part[KH : 2 * KH, 128 * (u // 2) : 128 * (u // 2) + 128]
            if u % 2 == 0:
                unit = jnp.where(lane < 64, top, pltpu.roll(bottom, 64, 1))
            else:
                unit = jnp.where(lane < 64, pltpu.roll(top, 64, 1), bottom)
            j = 2 * p + u // 3
            share(c, unit.astype(BF), keep, give, 4 * (j % 4) + j // 4, u % 3)


def share(c, unit, keep, give, j, u):
    top, bottom = unit[0 : KH // 2], unit[KH // 2 : KH]
    keep[j, u] = jnp.where(c == 0, top, bottom)
    give[j, u] = jnp.where(c == 0, bottom, top)


def main(*args):
    shares = jax.ShapeDtypeStruct((16, 3, KH // 2, 128), BF)
    return pl.pallas_call(
        main_kernel,
        out_shape=(shares, shares, jax.ShapeDtypeStruct((TOK, CH), BF)),
        in_specs=[SMEM] * 5 + vmem(9),
        out_specs=tuple(vmem(3)),
        compiler_params=params(24),
        cost_estimate=cost(3),
        name="main",
    )(*args)


def through_kernel(
    place, near, far, near_2, far_2, latent, maps, out, cross_ref, stack, slab, sems
):
    f, c = place[0], place[1]
    total = jnp.zeros((CH, 128), F32)
    for p, tiles, beside in side_by_side(f, c, 1, near, far, near_2, far_2):
        total += beside
        for t in range(3):
            stack[0:CH, pl.ds(pl.multiple_of(p * PAIR + 128 * t, 128), 128)] = tiles[t]
    cross_ref[...] = dot(total.astype(BF), shifted(CH, 128, 64), 1, 1).astype(BF)
    stack[CH : CH + RANK, :] = maps[...]
    widen = shifted(CH, 128, 0).astype(F32) + dot(cross_ref[...], shifted(RANK, 128, CH), 1, 0)
    wide = dot(latent[...], widen.astype(BF), 1, 0).astype(BF)
    copies = []
    for i in range(D // BLOCK):
        slab[i] = dot(wide, stack[:, BLOCK * i : BLOCK * i + BLOCK], 1, 0).astype(BF)
        copy = pltpu.make_async_copy(
            slab.at[i], out.at[:, pl.ds(BLOCK * i, BLOCK)], sems.at[i]
        )
        copy.start()
        copies.append(copy)
    for copy in copies:
        copy.wait()


def through(*args):
    return pl.pallas_call(
        through_kernel,
        out_shape=(
            jax.ShapeDtypeStruct((TOK, D), BF),
            jax.ShapeDtypeStruct((CH, RANK), BF),
        ),
        in_specs=[SMEM] + vmem(6),
        out_specs=(pl.BlockSpec(memory_space=pl.ANY), pl.BlockSpec(memory_space=pltpu.VMEM)),
        scratch_shapes=[
            pltpu.VMEM((CH + RANK, D), BF),
            pltpu.VMEM((D // BLOCK, TOK, BLOCK), BF),
            pltpu.SemaphoreType.DMA((D // BLOCK,)),
        ],
        compiler_params=params(16),
        cost_estimate=cost(3),
        name="through",
    )(*args)


def last_kernel(units, cross, own_proj, grad_a, grad_b):
    unit = [units[u] for u in range(4)]

    def rows(right):
        total = jnp.zeros((KH, SHARD), F32)
        for u in range(3):
            r = lax.broadcasted_iota(jnp.int32, (128, SHARD), 0) - 64 * right
            col = lax.broadcasted_iota(jnp.int32, (128, SHARD), 1) - 64 * u
            place_at = ((r == col) & (col >= 0) & (col < 64)).astype(BF)
            total += dot(unit[u], place_at, 1, 0)
        return total

    sums = jnp.concatenate([rows(0), rows(1)], axis=0).astype(BF)
    low = jnp.concatenate(
        [dot(unit[3], shifted(RANK, 128, 64 * h), 1, 1) for h in range(2)], axis=0
    ).astype(BF)
    grad_a[...] = dot(cross[...], sums, 0, 0) / loss_scale
    grad_b[...] = dot(low, own_proj[...], 0, 0) / loss_scale


def last(*args):
    return pl.pallas_call(
        last_kernel,
        out_shape=(
            jax.ShapeDtypeStruct((RANK, SHARD), F32),
            jax.ShapeDtypeStruct((RANK, SHARD), F32),
        ),
        in_specs=vmem(3),
        out_specs=tuple(vmem(2)),
        compiler_params=params(8),
        cost_estimate=cost(1),
        name="last",
    )(*args)


def add(*terms):
    return sum(t.astype(F32) for t in terms).astype(BF)


def widen(near, perm):
    return jnp.concatenate([near, send(near, perm)])


def exchange(v, groups):
    v = lax.all_to_all(v, AXES, 0, 0, axis_index_groups=groups, tiled=True)
    return jnp.sum(v.astype(F32), axis=0).astype(BF)


def beside(v, low):
    return jnp.concatenate([v, jnp.broadcast_to(low[None], v.shape[:1] + low.shape)], axis=1)


def shift_z(step):
    def move(zl, y, zh, x, c):
        z = (zh * 4 + zl + step) % 8
        return z % 4, y, z // 4, x, c

    return [(i, number(*move(*coords(i)))) for i in range(256)]


def slab_of(value, start, size):
    return lax.dynamic_slice_in_dim(value, start, size, axis=0)


def members(key):
    groups = {}
    for i in range(256):
        groups.setdefault(key(*coords(i)), []).append(i)
    return list(groups.values())


def reduce_all(keep, give, keep_low, give_low, f, c):
    zl, y = f // 4, f % 4
    v = add(keep, send(give, flip(c=1)))
    low = add(keep_low, send(give_low, flip(c=1)))
    v = beside(v.reshape((4, 12) + v.shape[2:]), low)
    v = exchange(v, members(lambda zl, y, zh, x, c: (zl, zh, x, c)))
    v, low = v[:12].reshape((4, 3) + v.shape[1:]), v[12:]
    v = beside(v, low)
    v = jnp.broadcast_to(v[:, None], (4, 2) + v.shape[1:]).reshape((8,) + v.shape[1:])
    v = exchange(v, members(lambda zl, y, zh, x, c: (y, x, c)))
    other = send(v, flip(c=1))
    v = jnp.concatenate([jnp.where(c == 0, v, other), jnp.where(c == 0, other, v)], axis=1)
    v = add(v, send(v, flip(x=1, c=1)))
    return add(v, send(v, flip(x=3, c=1)))


def local(
    block_in,
    block_out,
    weight,
    adapter_a,
    adapter_b,
    proj,
    w_feature,
    w_embed,
    id_table,
    box_rows,
    box_cols,
    identity,
    face_count,
):
    f, d = lax.axis_index("fsdp"), lax.axis_index("dp")
    place = jnp.stack([f, d % 2, d]).astype(jnp.int32)
    proj_t = proj.T

    table = widen(id_table, flip(zl=2, zh=1, c=1))
    maps, own_proj = pack(place, proj_t, weight, adapter_a.T, adapter_b)
    maps = widen(maps, flip(zl=2, c=1))
    table = widen(table, flip(x=1, c=1))
    maps = widen(maps, flip(zl=1, c=1))
    maps = widen(maps, flip(y=1, c=1))
    table = after(table, maps)
    pre, emb = face(
        after(box_rows, table, maps), box_cols, block_out, proj_t, w_feature, w_embed
    )
    table_2 = after(send(table, flip(x=3, c=1)), pre)
    maps_2 = after(send(maps, flip(y=3, c=1)), pre)
    table_far = (send(table, flip(c=1)), send(table_2, flip(c=1)))
    blocks = (maps, maps_2, send(maps, flip(c=1)), send(maps_2, flip(c=1)))
    keep, give, d_latent = main(
        place, box_rows, box_cols, identity, face_count,
        table, table_2, *table_far, pre, emb, w_embed, w_feature, block_in,
    )
    whole_a, keep_low, give_low = low_maps(place, block_in, d_latent, *blocks)
    total = reduce_all(keep, give, keep_low, give_low, f, d % 2)
    grad_in, cross = through(place, *blocks, d_latent, whole_a)
    grad_a, grad_b = last(total, cross, own_proj)
    return grad_in, grad_a.T, grad_b


def solution(mesh):
    return jax.shard_map(
        local,
        mesh=mesh,
        in_specs=(
            P(("fsdp", "dp"), None),
            P(("fsdp", "dp"), None),
            P("fsdp", None),
            P("fsdp", None),
            P(None, "fsdp"),
            P(),
            P(),
            P(),
            P("dp", None),
            P(("fsdp", "dp"), None),
            P(("fsdp", "dp"), None),
            P(("fsdp", "dp"), None),
            P(("fsdp", "dp")),
        ),
        out_specs=(P(("fsdp", "dp"), None), P("fsdp", None), P(None, "fsdp")),
        check_vma=False,
    )
```

time: 94.7 us -> 79.3 us (0.84)
  blocking collectives: 0 us -> 21 us
  starting transfers between devices: 39.4 us -> 25.1 us
  local copies, waits for them, and re-layouts: 15.2 us -> 3.88 us
  waiting for transfers between devices: 23.8 us -> 12.5 us
  Pallas kernels: 13 us -> 14.5 us
  other arithmetic: 1.32 us -> 0.32 us
    all_to_all x0 -> x2, blocking collectives: none -> 21 us  [exchange(): v = lax.all_to_all(v, AXES, 0, 0, axis_index_groups=groups, tiled=True)]
    ppermute x19 -> x16, starting transfers between devices: 39.4 us -> 25.1 us  [send(): return lax.ppermute(value, AXES, perm)]
    ppermute x19 -> x16, waiting for transfers between devices: 23.8 us -> 12.5 us  [send(): return lax.ppermute(value, AXES, perm)]
    unnamed x40 -> x27, local copies, waits for them, and re-layouts: 12.7 us -> 3.83 us
    pallas_call x1, Pallas kernels: 2.14 us -> 4.87 us  [face(): pl.pallas_call(face_kernel, out_shape=(jax.ShapeDtypeStruct((8, HID), F32...]
    concatenate x2 -> x1, local copies, waits for them, and re-layouts: 1.44 us -> 0.01 us  [widen(): return jnp.concatenate([near, send(near, perm)])]
    pallas_call x5, Pallas kernels: 10.9 us -> 9.67 us  [the longest x1 2.8 us: main(): pl.pallas_call(main_kernel, out_shape=(shares, shares, jax.ShapeDtypeStru...]
    convert_element_type x7 -> x3, other arithmetic: 1.13 us -> 0.08 us  [add(): return sum((t.astype(F32) for t in terms)).astype(BF)]
  transfers between devices with their start and end apart: 19 -> 16, of which waited for: 11 -> 9; matrix products, arithmetic and copies ran while one was open for 6% -> 0% of each run, Pallas kernels for 7% -> 13%
where the time goes in v2:
time: 79.3 us; the launch traced here: 78.9 us
  starting transfers between devices  25.1 us (32%)
  blocking collectives  21 us (26%)
  Pallas kernels  14.5 us (18%)
  waiting for transfers between devices  12.5 us (16%)
  local copies, waits for them, and re-layouts  3.88 us (5%)
  between operations  1.54 us (2%)
    ppermute x16, starting transfers between devices, send(): return lax.ppermute(value, AXES, perm)  25.1 us
    all_to_all x2, blocking collectives, exchange(): v = lax.all_to_all(v, AXES, 0, 0, axis_index_groups=groups, tiled=True)  21 us
    ppermute x16, waiting for transfers between devices, send(): return lax.ppermute(value, AXES, perm)  12.5 us
    pallas_call x1, Pallas kernels, face(): pl.pallas_call(face_kernel, out_shape=(jax.ShapeDtypeStruct((8, HID), F32...  4.87 us
    unnamed x27, local copies, waits for them, and re-layouts  3.83 us
    pallas_call x1, Pallas kernels, main(): pl.pallas_call(main_kernel, out_shape=(shares, shares, jax.ShapeDtypeStru...  2.8 us
    pallas_call x1, Pallas kernels, through(): pl.pallas_call(through_kernel, out_shape=(jax.ShapeDtypeStruct((TOK, D),...  2.36 us
    pallas_call x1, Pallas kernels, pack(): pl.pallas_call(pack_kernel, out_shape=(jax.ShapeDtypeStruct((1, CH, 256),...  1.95 us
  transfers between devices with their start and end apart: 16, of which 9 were waited for; matrix products, arithmetic and copies ran while one was open for 0% of the time, Pallas kernels for 13%

profile of v2, /device:TPU:1, one launch (start us, length us, event | category | flops | bytes accessed | tf_op | source)
XLA Modules:
  0.0 78.9 jit_solution(7093110654326931792)
XLA Ops:
  0.6 0.1 pad_add_fusion.place
  0.7 1.0 %copy-done.3 = bf16[3072,64]{0,1:T(8,128)(2,1)S(1)} copy-done((bf16[3072,64]{0,1:T(8,128)(2,1)S(1)}, bf16[3072,64]{0,1:T(8,128)(2,1)}, u32[]{:S(2)}) %copy-start.3) | copy-done | bytes 393240
  1.7 1.3 %copy-done.5 = bf16[192,3072]{1,0:T(8,128)(2,1)S(1)} copy-done((bf16[192,3072]{1,0:T(8,128)(2,1)S(1)}, bf16[192,3072]{1,0:T(8,128)(2,1)}, u32[]{:S(2)}) %copy-start.5) | copy-done | bytes 1179672
  3.0 0.8 copy-done.6
  3.7 0.8 copy-done.7
  4.5 0.0 copy-start.9
  4.5 1.9 %pack.1 = (bf16[1,64,256]{2,1,0:T(8,128)(2,1)S(1)}, bf16[64,192]{1,0:T(8,128)(2,1)S(1)}) custom-call(s32[3]{0:T(128)S(1)} %pad_add_fusion.place, bf16[64,3072]{1,0:T(8,128)(2,1)S(1)} %bitcast.13, bf16[192,3072]{1,0:T(8,128)(2,1)S(1)} %copy-done.5, bf16[64,192]{1,0:T(8,128)(2,1)S(1)} %bitcast.15, bf16[64,192]{1,0:T(8,128)(2,1)S(1)} %copy-done.7), custom_call_target="tpu_custom_call" | custom-call | flops 2 | bytes 2 | tf_op jit(solution)/shard_map/pack/pallas_call | solution.py:146
  6.5 4.0 %collective-permute-start = (bf16[1,64,256]{2,1,0:T(8,128)(2,1)S(1)}, bf16[1,64,256]{2,1,0:T(8,128)(2,1)S(1)}, u32[]{:S(2)}, u32[]{:S(2)}) collective-permute-start(bf16[1,64,256]{2,1,0:T(8,128)(2,1)S(1)} %get-tuple-element.21), channel_id=1, source_target_pairs={{0,129},{1,128},{2,131},{3,130},{4,133},{5,132},{6,135},{7,134},{8... | collective-permute-start | bytes 98312 | tf_op jit(solution)/shard_map/ppermute | solution.py:49
  10.4 4.4 %collective-permute-start.4 = (bf16[64,512]{1,0:T(8,128)(2,1)S(1)}, bf16[64,512]{1,0:T(8,128)(2,1)S(1)}, u32[]{:S(2)}, u32[]{:S(2)}) collective-permute-start(bf16[64,512]{1,0:T(8,128)(2,1)S(1)} %copy-done.11), channel_id=1, source_target_pairs={{0,137},{1,136},{2,139},{3,138},{4,141},{5,140},{6,143},{7,142},{8... | collective-permute-start | bytes 196616 | tf_op jit(solution)/shard_map/ppermute | solution.py:49
  14.9 0.0 collective-permute-done
  14.9 0.9 %collective-permute-start.1 = (bf16[2,64,256]{2,1,0:T(8,128)(2,1)S(1)}, bf16[2,64,256]{2,1,0:T(8,128)(2,1)S(1)}, u32[]{:S(2)}, u32[]{:S(2)}) collective-permute-start(bf16[2,64,256]{2,1,0:T(8,128)(2,1)S(1)} %pad_maximum_fusion.4), channel_id=1, source_target_pairs={{0,65},{1,64},{2,67},{3,66},{4,69},{5,68},{6,71},{7,70},{8,73},{9,... | collective-permute-start | bytes 196616 | tf_op jit(solution)/shard_map/ppermute | solution.py:49
  15.8 1.9 %collective-permute-done.4 = bf16[64,512]{1,0:T(8,128)(2,1)S(1)} collective-permute-done((bf16[64,512]{1,0:T(8,128)(2,1)S(1)}, bf16[64,512]{1,0:T(8,128)(2,1)S(1)}, u32[]{:S(2)}, u32[]{:S(2)}) %collective-permute-start.4) | collective-permute-done | bytes 65568 | tf_op jit(solution)/shard_map/ppermute | solution.py:49
  17.7 2.1 %collective-permute-start.5 = (bf16[128,512]{1,0:T(8,128)(2,1)S(1)}, bf16[128,512]{1,0:T(8,128)(2,1)S(1)}, u32[]{:S(2)}, u32[]{:S(2)}) collective-permute-start(bf16[128,512]{1,0:T(8,128)(2,1)S(1)} %pad_maximum_fusion.3), channel_id=1, source_target_pairs={{0,3},{1,2},{2,1},{3,0},{4,7},{5,6},{6,5},{7,4},{8,11},{9,10},{10,... | collective-permute-start | bytes 393224 | tf_op jit(solution)/shard_map/ppermute | solution.py:49
  19.8 0.0 collective-permute-done.1
  19.8 1.3 %collective-permute-start.2 = (bf16[4,64,256]{2,1,0:T(8,128)(2,1)S(1)}, bf16[4,64,256]{2,1,0:T(8,128)(2,1)S(1)}, u32[]{:S(2)}, u32[]{:S(2)}) collective-permute-start(bf16[4,64,256]{2,1,0:T(8,128)(2,1)S(1)} %pad_maximum_fusion.2), channel_id=1, source_target_pairs={{0,17},{1,16},{2,19},{3,18},{4,21},{5,20},{6,23},{7,22},{8,25},{9,... | collective-permute-start | bytes 393224 | tf_op jit(solution)/shard_map/ppermute | solution.py:49
  21.1 3.0 %collective-permute-done.5 = bf16[128,512]{1,0:T(8,128)(2,1)S(1)} collective-permute-done((bf16[128,512]{1,0:T(8,128)(2,1)S(1)}, bf16[128,512]{1,0:T(8,128)(2,1)S(1)}, u32[]{:S(2)}, u32[]{:S(2)}) %collective-permute-start.5) | collective-permute-done | bytes 131104 | tf_op jit(solution)/shard_map/ppermute | solution.py:49
  24.1 0.8 %collective-permute-done.2 = bf16[4,64,256]{2,1,0:T(8,128)(2,1)S(1)} collective-permute-done((bf16[4,64,256]{2,1,0:T(8,128)(2,1)S(1)}, bf16[4,64,256]{2,1,0:T(8,128)(2,1)S(1)}, u32[]{:S(2)}, u32[]{:S(2)}) %collective-permute-start.2) | collective-permute-done | bytes 131104 | tf_op jit(solution)/shard_map/ppermute | solution.py:49
  25.0 0.0 copy-start
  25.0 0.0 copy-start.1
  25.0 0.0 copy-start.10
  25.0 2.9 %collective-permute-start.8 = (bf16[256,512]{1,0:T(8,128)(2,1)S(1)}, bf16[256,512]{1,0:T(8,128)(2,1)S(1)}, u32[]{:S(2)}, u32[]{:S(2)}) collective-permute-start(bf16[256,512]{1,0:T(8,128)(2,1)S(1)} %pad_maximum_fusion.near_0), channel_id=1, source_target_pairs={{0,7},{1,6},{2,5},{3,4},{4,3},{5,2},{6,1},{7,0},{8,15},{9,14},{10,... | collective-permute-start | bytes 786440 | tf_op jit(solution)/shard_map/ppermute | solution.py:49
  28.0 2.7 %collective-permute-start.3 = (bf16[8,64,256]{2,1,0:T(8,128)(2,1)S(1)}, bf16[8,64,256]{2,1,0:T(8,128)(2,1)S(1)}, u32[]{:S(2)}, u32[]{:S(2)}) collective-permute-start(bf16[8,64,256]{2,1,0:T(8,128)(2,1)S(1)} %constant_dynamic-update-slice_fusion.near), channel_id=1, source_target_pairs={{0,49},{1,48},{2,51},{3,50},{4,53},{5,52},{6,55},{7,54},{8,57},{9,... | collective-permute-start | bytes 786440 | tf_op jit(solution)/shard_map/ppermute | solution.py:49
  30.6 0.3 collective-permute-start.9
  31.0 4.9 %face.1 = (f32[8,512]{1,0:T(8,128)S(1)}, f32[8,512]{1,0:T(8,128)S(1)}) custom-call(s32[1,6]{1,0:T(1,128)S(1)} %copy-done.8, s32[1,6]{1,0:T(1,128)S(1)} %copy-done.9, bf16[256,3072]{1,0:T(8,128)(2,1)} %y_hbm.1, bf16[64,3072]{1,0:T(8,128)(2,1)S(1)} %bitcast.14, bf16[3136,512]{1,0:T(8,128)(2,1)} %w_feature.1, bf16[512,512]{1,0:T(8,128)(2,1)S(1)} %copy-done.2), custom_call_target="tpu_custom_call" | custom-call | flops 4 | bytes 4 | tf_op jit(solution)/shard_map/face/pallas_call | solution.py:203
  35.9 0.0 collective-permute-done.8.near_1
  35.9 0.2 collective-permute-start.10
  36.1 0.3 collective-permute-start.6
  36.5 0.8 collective-permute-done.3.far
  37.2 0.2 collective-permute-start.7
  38.1 0.0 collective-permute-done.9.far_0
  38.1 2.8 %main.1 = (bf16[16,3,16,128]{3,2,1,0:T(8,128)(2,1)S(1)}, bf16[16,3,16,128]{3,2,1,0:T(8,128)(2,1)S(1)}, bf16[256,64]{1,0:T(8,128)(2,1)S(1)}) custom-call(s32[3]{0:T(128)S(1)} %pad_add_fusion.place, s32[1,6]{1,0:T(1,128)S(1)} %copy-done.8, s32[1,6]{1,0:T(1,128)S(1)} %copy-done.9, s32[1,6]{1,0:T(1,128)S(1)} %copy-done.10, s32[1]{0:T(128)S(6)} %copy.19.count, ...), custom_call_target="tpu_custom_call" | custom-call | flops 3 | bytes 3 | tf_op jit(solution)/shard_map/main/pallas_call | solution.py:348
  40.9 0.0 collective-permute-done.6.near_2
  41.0 1.6 %low.1 = (bf16[64,3072]{1,0:T(8,128)(2,1)S(1)}, bf16[1,16,128]{2,1,0:T(8,128)(2,1)S(1)}, bf16[1,16,128]{2,1,0:T(8,128)(2,1)S(1)}) custom-call(s32[3]{0:T(128)S(1)} %pad_add_fusion.place, bf16[256,3072]{1,0:T(8,128)(2,1)S(1)} %copy-done.1, bf16[256,64]{1,0:T(8,128)(2,1)S(1)} %get-tuple-element.28.latent, ...), custom_call_target="tpu_custom_call" | custom-call | flops 2 | bytes 2 | tf_op jit(solution)/shard_map/low/pallas_call | solution.py:267
  42.5 0.3 collective-permute-start.12
  42.9 0.2 collective-permute-start.11
  43.1 0.7 collective-permute-done.12
  43.7 0.6 collective-permute-done.11
  44.3 0.1 add_convert_fusion
  44.4 9.1 %all_to_all.10 = bf16[4,13,16,128]{3,2,1,0:T(8,128)(2,1)S(1)} all-to-all(bf16[4,13,16,128]{3,2,1,0:T(8,128)(2,1)S(1)} %pad_maximum_fusion.1), channel_id=1, replica_groups={{0,16,32,48},{1,17,33,49},{2,18,34,50},{3,19,35,51},{4,20,36,52},{5,21,..., dimensions={0} | all-to-all | bytes 425984 | tf_op jit(solution)/shard_map/all_to_all | solution.py:448
  53.7 11.9 %all_to_all.11 = bf16[8,4,16,128]{3,2,1,0:T(8,128)(2,1)S(1)} all-to-all(bf16[8,4,16,128]{3,2,1,0:T(8,128)(2,1)S(1)} %bitcast.17), channel_id=1, replica_groups={{0,8,64,72,128,136,192,200},{1,9,65,73,129,137,193,201},{2,10,66,74,130..., dimensions={0} | all-to-all | bytes 262144 | tf_op jit(solution)/shard_map/all_to_all | solution.py:448
  65.6 3.4 %collective-permute-start.13 = (bf16[4,16,128]{2,1,0:T(8,128)(2,1)S(1)}, bf16[4,16,128]{2,1,0:T(8,128)(2,1)S(1)}, u32[]{:S(2)}, u32[]{:S(2)}) collective-permute-start(bf16[4,16,128]{2,1,0:T(8,128)(2,1)S(1)} %reduce_sum.25), channel_id=1, source_target_pairs={{0,1},{1,0},{2,3},{3,2},{4,5},{5,4},{6,7},{7,6},{8,9},{9,8},{10,11... | collective-permute-start | bytes 49160 | tf_op jit(solution)/shard_map/ppermute | solution.py:49
  68.9 0.8 %collective-permute-done.13 = bf16[4,16,128]{2,1,0:T(8,128)(2,1)S(1)} collective-permute-done((bf16[4,16,128]{2,1,0:T(8,128)(2,1)S(1)}, bf16[4,16,128]{2,1,0:T(8,128)(2,1)S(1)}, u32[]{:S(2)}, u32[]{:S(2)}) %collective-permute-start.13) | collective-permute-done | bytes 16416 | tf_op jit(solution)/shard_map/ppermute | solution.py:49
  69.8 0.6 collective-permute-start.14
  70.4 2.8 %collective-permute-done.14 = bf16[4,32,128]{2,1,0:T(8,128)(2,1)S(1)} collective-permute-done((bf16[4,32,128]{2,1,0:T(8,128)(2,1)S(1)}, bf16[4,32,128]{2,1,0:T(8,128)(2,1)S(1)}, u32[]{:S(2)}, u32[]{:S(2)}) %collective-permute-start.14) | collective-permute-done | bytes 32800 | tf_op jit(solution)/shard_map/ppermute | solution.py:49
  73.2 1.2 %collective-permute-start.15 = (bf16[4,32,128]{2,1,0:T(8,128)(2,1)S(1)}, bf16[4,32,128]{2,1,0:T(8,128)(2,1)S(1)}, u32[]{:S(2)}, u32[]{:S(2)}) collective-permute-start(bf16[4,32,128]{2,1,0:T(8,128)(2,1)S(1)} %add_convert_fusion.2), channel_id=1, source_target_pairs={{0,7},{1,6},{2,5},{3,4},{4,3},{5,2},{6,1},{7,0},{8,15},{9,14},{10,... | collective-permute-start | bytes 98312 | tf_op jit(solution)/shard_map/ppermute | solution.py:49
  74.4 2.4 %through.1 = (bf16[256,3072]{1,0:T(8,128)(2,1)}, bf16[64,64]{1,0:T(8,128)(2,1)S(1)}) custom-call(s32[3]{0:T(128)S(1)} %pad_add_fusion.place, bf16[8,64,256]{2,1,0:T(8,128)(2,1)S(1)} %constant_dynamic-update-slice_fusion.near, bf16[8,64,256]{2,1,0:T(8,128)(2,1)S(1)} %collective-permute-done.3.far, bf16[8,64,256]{2,1,0:T(8,128)(2,1)S(1)} %collective-permute-done.6.near_2, ...), custom_call_target="tpu_custom_call" | custom-call | flops 3 | bytes 3 | tf_op jit(solution)/shard_map/through/pallas_call | solution.py:385
  76.8 1.1 %collective-permute-done.15 = bf16[4,32,128]{2,1,0:T(8,128)(2,1)S(1)} collective-permute-done((bf16[4,32,128]{2,1,0:T(8,128)(2,1)S(1)}, bf16[4,32,128]{2,1,0:T(8,128)(2,1)S(1)}, u32[]{:S(2)}, u32[]{:S(2)}) %collective-permute-start.15) | collective-permute-done | bytes 32800 | tf_op jit(solution)/shard_map/ppermute | solution.py:49
  77.9 1.0 %last.1 = (f32[64,192]{1,0:T(8,128)}, f32[64,192]{1,0:T(8,128)}) custom-call(bf16[4,32,128]{2,1,0:T(8,128)(2,1)S(1)} %add_convert_fusion.1.units, bf16[64,64]{1,0:T(8,128)(2,1)S(1)} %get-tuple-element.35.cross, bf16[64,192]{1,0:T(8,128)(2,1)S(1)} %get-tuple-element.36.own_proj), custom_call_target="tpu_custom_call" | custom-call | flops 1 | bytes 1 | tf_op jit(solution)/shard_map/last/pallas_call | solution.py:425
  (40 shorter events, 0.3 us)
Async XLA Ops:
  0.7 1.0 %copy-start.3 = (bf16[3072,64]{0,1:T(8,128)(2,1)S(1)}, bf16[3072,64]{0,1:T(8,128)(2,1)}, u32[]{:S(2)}) copy-start(bf16[3072,64]{0,1:T(8,128)(2,1)} %param.18) | copy-start | bytes 1179652
  1.7 1.3 %copy-start.5 = (bf16[192,3072]{1,0:T(8,128)(2,1)S(1)}, bf16[192,3072]{1,0:T(8,128)(2,1)}, u32[]{:S(2)}) copy-start(bf16[192,3072]{1,0:T(8,128)(2,1)} %weight_hbm.1) | copy-start | bytes 3538948
  3.0 0.8 copy-start.6
  3.7 0.8 copy-start.7
  4.5 5.9 %copy-start.11 = (bf16[64,512]{1,0:T(8,128)(2,1)S(1)}, bf16[64,512]{1,0:T(8,128)(2,1)}, u32[]{:S(2)}) copy-start(bf16[64,512]{1,0:T(8,128)(2,1)} %param.21) | copy-start | bytes 196612
  4.5 26.5 %copy-start.2 = (bf16[512,512]{1,0:T(8,128)(2,1)S(1)}, bf16[512,512]{1,0:T(8,128)(2,1)}, u32[]{:S(2)}) copy-start(bf16[512,512]{1,0:T(8,128)(2,1)} %w_embed.1) | copy-start | bytes 1572868
  4.5 26.5 %copy-start.4 = (bf16[3072,64]{0,1:T(8,128)(2,1)S(1)}, bf16[3072,64]{0,1:T(8,128)(2,1)}, u32[]{:S(2)}) copy-start(bf16[3072,64]{0,1:T(8,128)(2,1)} %param.18) | copy-start | bytes 1179652
  4.5 26.5 %copy-start.8 = (s32[1,6]{1,0:T(1,128)S(1)}, s32[1,6]{1,0:T(1,128)}, u32[]{:S(2)}) copy-start(s32[1,6]{1,0:T(1,128)} %rows.2) | copy-start | bytes 76
  4.5 26.5 %copy-start.9 = (s32[1,6]{1,0:T(1,128)S(1)}, s32[1,6]{1,0:T(1,128)}, u32[]{:S(2)}) copy-start(s32[1,6]{1,0:T(1,128)} %cols.3) | copy-start | bytes 76
  6.5 8.4 %collective-permute-start = (bf16[1,64,256]{2,1,0:T(8,128)(2,1)S(1)}, bf16[1,64,256]{2,1,0:T(8,128)(2,1)S(1)}, u32[]{:S(2)}, u32[]{:S(2)}) collective-permute-start(bf16[1,64,256]{2,1,0:T(8,128)(2,1)S(1)} %get-tuple-element.21), channel_id=1, source_target_pairs={{0,129},{1,128},{2,131},{3,130},{4,133},{5,132},{6,135},{7,134},{8... | collective-permute-start | bytes 98312 | tf_op jit(solution)/shard_map/ppermute | solution.py:49
  10.4 7.2 %collective-permute-start.4 = (bf16[64,512]{1,0:T(8,128)(2,1)S(1)}, bf16[64,512]{1,0:T(8,128)(2,1)S(1)}, u32[]{:S(2)}, u32[]{:S(2)}) collective-permute-start(bf16[64,512]{1,0:T(8,128)(2,1)S(1)} %copy-done.11), channel_id=1, source_target_pairs={{0,137},{1,136},{2,139},{3,138},{4,141},{5,140},{6,143},{7,142},{8... | collective-permute-start | bytes 196616 | tf_op jit(solution)/shard_map/ppermute | solution.py:49
  14.9 4.9 %collective-permute-start.1 = (bf16[2,64,256]{2,1,0:T(8,128)(2,1)S(1)}, bf16[2,64,256]{2,1,0:T(8,128)(2,1)S(1)}, u32[]{:S(2)}, u32[]{:S(2)}) collective-permute-start(bf16[2,64,256]{2,1,0:T(8,128)(2,1)S(1)} %pad_maximum_fusion.4), channel_id=1, source_target_pairs={{0,65},{1,64},{2,67},{3,66},{4,69},{5,68},{6,71},{7,70},{8,73},{9,... | collective-permute-start | bytes 196616 | tf_op jit(solution)/shard_map/ppermute | solution.py:49
  17.7 6.4 %collective-permute-start.5 = (bf16[128,512]{1,0:T(8,128)(2,1)S(1)}, bf16[128,512]{1,0:T(8,128)(2,1)S(1)}, u32[]{:S(2)}, u32[]{:S(2)}) collective-permute-start(bf16[128,512]{1,0:T(8,128)(2,1)S(1)} %pad_maximum_fusion.3), channel_id=1, source_target_pairs={{0,3},{1,2},{2,1},{3,0},{4,7},{5,6},{6,5},{7,4},{8,11},{9,10},{10,... | collective-permute-start | bytes 393224 | tf_op jit(solution)/shard_map/ppermute | solution.py:49
  19.8 5.1 %collective-permute-start.2 = (bf16[4,64,256]{2,1,0:T(8,128)(2,1)S(1)}, bf16[4,64,256]{2,1,0:T(8,128)(2,1)S(1)}, u32[]{:S(2)}, u32[]{:S(2)}) collective-permute-start(bf16[4,64,256]{2,1,0:T(8,128)(2,1)S(1)} %pad_maximum_fusion.2), channel_id=1, source_target_pairs={{0,17},{1,16},{2,19},{3,18},{4,21},{5,20},{6,23},{7,22},{8,25},{9,... | collective-permute-start | bytes 393224 | tf_op jit(solution)/shard_map/ppermute | solution.py:49
  25.0 13.1 %copy-start = (bf16[3136,512]{1,0:T(8,128)(2,1)S(1)}, bf16[3136,512]{1,0:T(8,128)(2,1)}, u32[]{:S(2)}) copy-start(bf16[3136,512]{1,0:T(8,128)(2,1)} %w_feature.1) | copy-start | bytes 9633796
  25.0 13.1 %copy-start.1 = (bf16[256,3072]{1,0:T(8,128)(2,1)S(1)}, bf16[256,3072]{1,0:T(8,128)(2,1)}, u32[]{:S(2)}) copy-start(bf16[256,3072]{1,0:T(8,128)(2,1)} %x_ref.3) | copy-start | bytes 4718596
  25.0 13.1 %copy-start.10 = (s32[1,6]{1,0:T(1,128)S(1)}, s32[1,6]{1,0:T(1,128)}, u32[]{:S(2)}) copy-start(s32[1,6]{1,0:T(1,128)} %ident.1) | copy-start | bytes 76
  25.0 10.8 %collective-permute-start.8 = (bf16[256,512]{1,0:T(8,128)(2,1)S(1)}, bf16[256,512]{1,0:T(8,128)(2,1)S(1)}, u32[]{:S(2)}, u32[]{:S(2)}) collective-permute-start(bf16[256,512]{1,0:T(8,128)(2,1)S(1)} %pad_maximum_fusion.near_0), channel_id=1, source_target_pairs={{0,7},{1,6},{2,5},{3,4},{4,3},{5,2},{6,1},{7,0},{8,15},{9,14},{10,... | collective-permute-start | bytes 786440 | tf_op jit(solution)/shard_map/ppermute | solution.py:49
  28.0 9.3 %collective-permute-start.3 = (bf16[8,64,256]{2,1,0:T(8,128)(2,1)S(1)}, bf16[8,64,256]{2,1,0:T(8,128)(2,1)S(1)}, u32[]{:S(2)}, u32[]{:S(2)}) collective-permute-start(bf16[8,64,256]{2,1,0:T(8,128)(2,1)S(1)} %constant_dynamic-update-slice_fusion.near), channel_id=1, source_target_pairs={{0,49},{1,48},{2,51},{3,50},{4,53},{5,52},{6,55},{7,54},{8,57},{9,... | collective-permute-start | bytes 786440 | tf_op jit(solution)/shard_map/ppermute | solution.py:49
  30.6 7.5 %collective-permute-start.9 = (bf16[256,512]{1,0:T(8,128)(2,1)S(1)}, bf16[256,512]{1,0:T(8,128)(2,1)S(1)}, u32[]{:S(2)}, u32[]{:S(2)}) collective-permute-start(bf16[256,512]{1,0:T(8,128)(2,1)S(1)} %pad_maximum_fusion.near_0), channel_id=1, source_target_pairs={{0,1},{1,0},{2,3},{3,2},{4,5},{5,4},{6,7},{7,6},{8,9},{9,8},{10,11... | collective-permute-start | bytes 786440 | tf_op jit(solution)/shard_map/ppermute | solution.py:49
  35.9 2.2 %collective-permute-start.10 = (bf16[256,512]{1,0:T(8,128)(2,1)S(1)}, bf16[256,512]{1,0:T(8,128)(2,1)S(1)}, u32[]{:S(2)}, u32[]{:S(2)}) collective-permute-start(bf16[256,512]{1,0:T(8,128)(2,1)S(1)} %collective-permute-done.8.near_1), channel_id=1, source_target_pairs={{0,1},{1,0},{2,3},{3,2},{4,5},{5,4},{6,7},{7,6},{8,9},{9,8},{10,11... | collective-permute-start | bytes 786440 | tf_op jit(solution)/shard_map/ppermute | solution.py:49
  36.1 4.8 %collective-permute-start.6 = (bf16[8,64,256]{2,1,0:T(8,128)(2,1)S(1)}, bf16[8,64,256]{2,1,0:T(8,128)(2,1)S(1)}, u32[]{:S(2)}, u32[]{:S(2)}) collective-permute-start(bf16[8,64,256]{2,1,0:T(8,128)(2,1)S(1)} %constant_dynamic-update-slice_fusion.near), channel_id=1, source_target_pairs={{0,1},{1,0},{2,3},{3,2},{4,5},{5,4},{6,7},{7,6},{8,9},{9,8},{10,11... | collective-permute-start | bytes 786440 | tf_op jit(solution)/shard_map/ppermute | solution.py:49
  37.2 3.7 %collective-permute-start.7 = (bf16[8,64,256]{2,1,0:T(8,128)(2,1)S(1)}, bf16[8,64,256]{2,1,0:T(8,128)(2,1)S(1)}, u32[]{:S(2)}, u32[]{:S(2)}) collective-permute-start(bf16[8,64,256]{2,1,0:T(8,128)(2,1)S(1)} %collective-permute-done.3.far), channel_id=1, source_target_pairs={{0,1},{1,0},{2,3},{3,2},{4,5},{5,4},{6,7},{7,6},{8,9},{9,8},{10,11... | collective-permute-start | bytes 786440 | tf_op jit(solution)/shard_map/ppermute | solution.py:49
  42.5 1.2 %collective-permute-start.12 = (bf16[1,16,128]{2,1,0:T(8,128)(2,1)S(1)}, bf16[1,16,128]{2,1,0:T(8,128)(2,1)S(1)}, u32[]{:S(2)}, u32[]{:S(2)}) collective-permute-start(bf16[1,16,128]{2,1,0:T(8,128)(2,1)S(1)} %get-tuple-element.34), channel_id=1, source_target_pairs={{0,1},{1,0},{2,3},{3,2},{4,5},{5,4},{6,7},{7,6},{8,9},{9,8},{10,11... | collective-permute-start | bytes 12296 | tf_op jit(solution)/shard_map/ppermute | solution.py:49
  42.9 1.4 %collective-permute-start.11 = (bf16[16,3,16,128]{3,2,1,0:T(8,128)(2,1)S(1)}, bf16[16,3,16,128]{3,2,1,0:T(8,128)(2,1)S(1)}, u32[]{:S(2)}, u32[]{:S(2)}) collective-permute-start(bf16[16,3,16,128]{3,2,1,0:T(8,128)(2,1)S(1)} %get-tuple-element.32), channel_id=1, source_target_pairs={{0,1},{1,0},{2,3},{3,2},{4,5},{5,4},{6,7},{7,6},{8,9},{9,8},{10,11... | collective-permute-start | bytes 589832 | tf_op jit(solution)/shard_map/ppermute | solution.py:49
  65.6 4.2 %collective-permute-start.13 = (bf16[4,16,128]{2,1,0:T(8,128)(2,1)S(1)}, bf16[4,16,128]{2,1,0:T(8,128)(2,1)S(1)}, u32[]{:S(2)}, u32[]{:S(2)}) collective-permute-start(bf16[4,16,128]{2,1,0:T(8,128)(2,1)S(1)} %reduce_sum.25), channel_id=1, source_target_pairs={{0,1},{1,0},{2,3},{3,2},{4,5},{5,4},{6,7},{7,6},{8,9},{9,8},{10,11... | collective-permute-start | bytes 49160 | tf_op jit(solution)/shard_map/ppermute | solution.py:49
  69.8 3.4 %collective-permute-start.14 = (bf16[4,32,128]{2,1,0:T(8,128)(2,1)S(1)}, bf16[4,32,128]{2,1,0:T(8,128)(2,1)S(1)}, u32[]{:S(2)}, u32[]{:S(2)}) collective-permute-start(bf16[4,32,128]{2,1,0:T(8,128)(2,1)S(1)} %pad_maximum_fusion.6), channel_id=1, source_target_pairs={{0,3},{1,2},{2,1},{3,0},{4,7},{5,6},{6,5},{7,4},{8,11},{9,10},{10,... | collective-permute-start | bytes 98312 | tf_op jit(solution)/shard_map/ppermute | solution.py:49
  73.2 4.6 %collective-permute-start.15 = (bf16[4,32,128]{2,1,0:T(8,128)(2,1)S(1)}, bf16[4,32,128]{2,1,0:T(8,128)(2,1)S(1)}, u32[]{:S(2)}, u32[]{:S(2)}) collective-permute-start(bf16[4,32,128]{2,1,0:T(8,128)(2,1)S(1)} %add_convert_fusion.2), channel_id=1, source_target_pairs={{0,7},{1,6},{2,5},{3,4},{4,3},{5,2},{6,1},{7,0},{8,15},{9,14},{10,... | collective-permute-start | bytes 98312 | tf_op jit(solution)/shard_map/ppermute | solution.py:49

commit v3 on v2

v3 whole, which is shorter than its diff:
```python
import jax
import jax.numpy as jnp
from jax import lax
from jax.experimental import pallas as pl
from jax.experimental.pallas import tpu as pltpu
from jax.sharding import PartitionSpec as P

D = 3072
CH = 64
RANK = 64
HID = 512
EMB = 512
FACE = 7
MAXF = 6
GW = 16
IDS_DEV = 64
TOK = 256
CROP = 3136
SHARD = 192
PAIR = 2 * SHARD
KH = 32
GROUPS = 12
ROWS = GROUPS * 8
UNITS = 48
BLOCK = 512

loss_scale = 1024.0
eps_norm = 1e-06
BF = jnp.bfloat16
F32 = jnp.float32
AXES = ("fsdp", "dp")


def coords(index):
    f, d = index // 16, index % 16
    return f // 4, f % 4, d // 8, (d // 2) % 4, d % 2


def number(zl, y, zh, x, c):
    return (zl * 4 + y) * 16 + zh * 8 + x * 2 + c


def flip(zl=0, y=0, zh=0, x=0, c=0):
    move = lambda l, b, h, a, e: (l ^ zl, b ^ y, h ^ zh, a ^ x, e ^ c)
    return [(i, number(*move(*coords(i)))) for i in range(256)]


def send(value, perm):
    return lax.ppermute(value, AXES, perm)


def after(value, *others):
    return lax.optimization_barrier((value,) + others)[0]


def dot(a, b, da, db):
    return lax.dot_general(a, b, (((da,), (db,)), ((), ())), preferred_element_type=F32)


def shifted(rows, width, offset):
    r = lax.broadcasted_iota(jnp.int32, (rows, width), 0)
    c = lax.broadcasted_iota(jnp.int32, (rows, width), 1)
    return (c == r + offset).astype(BF)


def params(mib):
    return pltpu.CompilerParams(vmem_limit_bytes=mib << 20)


def cost(us):
    return pl.CostEstimate(flops=us, bytes_accessed=us, transcendentals=0)


def vmem(n):
    return [pl.BlockSpec(memory_space=pltpu.VMEM)] * n


SMEM = pl.BlockSpec(memory_space=pltpu.SMEM)


HBM = pl.BlockSpec(memory_space=pl.ANY)


def corner_of(rows, cols, slot):
    corner = jnp.zeros_like(slot)
    for k in range(MAXF):
        corner = jnp.where(slot == k, rows[0, k] * GW + cols[0, k], corner)
    return corner


def token_of(rows, cols, index, i):
    slot = index & 7
    p = 4 * (index >> 3) + i
    down = (p * 37) >> 8
    token = corner_of(rows, cols, slot) + down * GW + (p - down * FACE)
    return jnp.where((slot < MAXF) & (p < FACE * FACE), token, -1)


def load_all(moves, sems):
    waits, n = [], 0
    for source, target, parts in moves:
        rows = source.shape[0] // parts
        copies = []
        for p in range(parts):
            at = pl.ds(p * rows, rows)
            copies.append(pltpu.make_async_copy(source.at[at], target.at[at], sems.at[n]))
            copies[-1].start()
            n += 1
        waits.append(copies)
    return waits


def arrived(*groups):
    for copies in groups:
        for copy in copies:
            copy.wait()


def front_kernel(
    rows, cols, proj_hbm, weight_hbm, a_hbm, b_hbm, y_hbm, feature_hbm, embed_hbm,
    pay, own_ref, face_ref,
    proj_t, weight, a_ref, b_ref, y_ref, w_feature, w_embed, sems,
):
    f, c = lax.axis_index("fsdp"), lax.axis_index("dp") & 1
    small, heavy, faces, feature_w, embed_w = (slice(0, 3), slice(3, 4), 4, 5, 6)
    copies = load_all(
        (
            (proj_hbm, proj_t, 2),
            (a_hbm, a_ref, 1),
            (b_hbm, b_ref, 1),
            (weight_hbm, weight, 4),
            (y_hbm, y_ref, 4),
            (feature_hbm, w_feature, 7),
            (embed_hbm, w_embed, 2),
        ),
        sems,
    )
    n = ROWS + 8
    index = lax.broadcasted_iota(jnp.int32, (n, TOK), 0)
    token = lax.broadcasted_iota(jnp.int32, (n, TOK), 1)
    picks = [(token_of(rows, cols, index, i) == token).astype(BF) for i in range(4)]
    arrived(*copies[small])
    window = proj_t[:, pl.ds(pl.multiple_of((f >> 1) * PAIR, 128), PAIR)]
    own = dot(window, shifted(SHARD, PAIR, (f & 1) * SHARD), 1, 1).astype(BF)
    own_ref[...] = own
    arrived(*copies[heavy])

    @pl.when(c == 0)
    def _():
        pay[0] = dot(a_ref[...], shifted(SHARD, 256, 0), 1, 0).astype(BF)

    @pl.when(c == 1)
    def _():
        moved = (dot(proj_t[...], weight[...], 1, 1) + own.astype(F32)).astype(BF)
        cross = dot(own, b_ref[...], 1, 1).astype(BF)
        wide = dot(moved, shifted(SHARD, 256, 0), 1, 0)
        pay[0] = (wide + dot(cross, shifted(CH, 256, SHARD), 1, 0)).astype(BF)

    arrived(copies[faces])
    latent = dot(y_ref[...], proj_t[...], 1, 1).astype(BF)
    crops = jnp.zeros((n, 256), F32)
    for i in range(4):
        wide = dot(latent, shifted(CH, 256, CH * i), 1, 0).astype(BF)
        crops += dot(picks[i], wide, 1, 0)
    crops = crops.astype(BF)
    arrived(copies[feature_w])
    pre = dot(crops[ROWS:n, 0:CH], w_feature[GROUPS * 256 : CROP, :], 1, 0)
    for g in range(GROUPS):
        pre += dot(crops[8 * g : 8 * g + 8, :], w_feature[256 * g : 256 * g + 256, :], 1, 0)
    face_ref[0:8] = pre
    feature = jax.nn.gelu(pre).astype(BF)
    arrived(copies[embed_w])
    face_ref[8:16] = dot(feature, w_embed[...], 1, 0)


def front(*args):
    return pl.pallas_call(
        front_kernel,
        out_shape=(
            jax.ShapeDtypeStruct((1, CH, 256), BF),
            jax.ShapeDtypeStruct((CH, SHARD), BF),
            jax.ShapeDtypeStruct((16, EMB), F32),
        ),
        in_specs=[SMEM] * 2 + [HBM] * 7,
        out_specs=tuple(vmem(3)),
        scratch_shapes=[
            pltpu.VMEM((CH, D), BF),
            pltpu.VMEM((SHARD, D), BF),
            pltpu.VMEM((RANK, SHARD), BF),
            pltpu.VMEM((RANK, SHARD), BF),
            pltpu.VMEM((TOK, D), BF),
            pltpu.VMEM((CROP, HID), BF),
            pltpu.VMEM((HID, EMB), BF),
            pltpu.SemaphoreType.DMA((21,)),
        ],
        compiler_params=params(56),
        cost_estimate=cost(4),
        name="front",
    )(*args)


def side_by_side(f, c, kind, maps):
    zl, y = f >> 2, f & 3
    even = (y & 1) == 0
    lane = lax.broadcasted_iota(jnp.int32, (CH, 128), 1)

    def block(k, i):
        crossed = int(k != 0) ^ int(i != 0)
        return jnp.where((c ^ crossed) == kind, maps[k][i], maps[k + 4][i])

    for k in (0, 2):
        for i in range(4):
            a, b = block(k, i), block(k + 1, i)
            left = jnp.where(even, a, b).astype(F32)
            right = jnp.where(even, b, a).astype(F32)
            turned = pltpu.roll(right[:, 0:128], 64, 1)
            tiles = (
                left[:, 0:128],
                jnp.where(lane < 64, left[:, 128:256], turned),
                jnp.where(lane < 64, turned, pltpu.roll(right[:, 128:256], 64, 1)),
            )
            p = (zl ^ i) * 2 + ((y ^ k) >> 1)
            yield p, [t.astype(BF) for t in tiles], left[:, 128:256] + right[:, 128:256]


def low_kernel(x_ref, latent, *refs):
    blocks, (maps, keep, give) = refs[0:8], refs[8:]
    f, c = lax.axis_index("fsdp"), lax.axis_index("dp") & 1
    total = jnp.zeros((TOK, RANK), F32)
    for p, tiles, _ in side_by_side(f, c, 0, blocks):
        for t in range(3):
            spot = pl.ds(pl.multiple_of(p * PAIR + 128 * t, 128), 128)
            maps[:, spot] = tiles[t]
        spot = pl.ds(pl.multiple_of(p * PAIR, 128), PAIR)
        total += dot(x_ref[:, spot], maps[:, spot], 1, 1)
    part = dot(latent[...], dot(total.astype(BF), shifted(RANK, 128, 0), 1, 0).astype(BF), 0, 0)
    lane = lax.broadcasted_iota(jnp.int32, (KH, 128), 1)
    unit = jnp.where(lane < 64, part[0:KH], pltpu.roll(part[KH : 2 * KH], 64, 1)).astype(BF)
    top, bottom = unit[0 : KH // 2], unit[KH // 2 : KH]
    half = parity(f, lax.axis_index("dp"))
    keep[0] = jnp.where(half == 0, top, bottom)
    give[0] = jnp.where(half == 0, bottom, top)


def low_maps(*args):
    share = jax.ShapeDtypeStruct((1, KH // 2, 128), BF)
    return pl.pallas_call(
        low_kernel,
        out_shape=(jax.ShapeDtypeStruct((RANK, D), BF), share, share),
        in_specs=vmem(10),
        out_specs=tuple(vmem(3)),
        compiler_params=params(16),
        cost_estimate=cost(2),
        name="low",
    )(*args)


def gelu_slope(preact):
    return jax.jvp(jax.nn.gelu, (preact,), (jnp.ones_like(preact),))[1]


def main_kernel(
    rows, cols, ident, count, *refs,
):
    near, far = refs[0:4], refs[4:8]
    face_ref, w_embed, w_feature, x_ref, keep, give, latent_ref = refs[8:]
    d = lax.axis_index("dp")
    half = parity(lax.axis_index("fsdp"), d)
    slot = lax.broadcasted_iota(jnp.int32, (8, 16), 0)
    lane = lax.broadcasted_iota(jnp.int32, (8, 16), 1)
    refer = jnp.zeros((8, EMB), F32)
    for k_slot in range(MAXF):
        who = ident[0, k_slot]
        apart = (who >> 6) ^ d
        dz, dx = apart >> 3, (apart >> 1) & 3
        crossed = dz ^ jnp.where(dx == 0, 0, 1)
        here = ((apart ^ crossed) & 1) == 0
        spot = dz * IDS_DEV + (who & 63)
        at = pl.ds(pl.multiple_of((spot >> 4) * 16, 16), 16)
        found = jnp.zeros((16, EMB), BF)
        for k in range(4):
            found = jnp.where(dx == k, jnp.where(here, near[k][at, :], far[k][at, :]), found)
        live = (slot == k_slot) & (lane == (spot & 15)) & (k_slot < count[0])
        refer += dot(live.astype(BF), found, 1, 0)
    emb = face_ref[8:16]
    norm_e = jnp.sqrt(jnp.sum(emb * emb, axis=-1, keepdims=True) + eps_norm)
    norm_r = jnp.sqrt(jnp.sum(refer * refer, axis=-1, keepdims=True) + eps_norm)
    cosine = jnp.sum(emb * refer, axis=-1, keepdims=True) / (norm_e * norm_r)
    d_embed = (
        loss_scale * (refer / (norm_e * norm_r) - cosine * emb / (norm_e * norm_e))
    ).astype(BF)
    d_feature = dot(d_embed, w_embed[...], 1, 1)
    d_pre = (d_feature * gelu_slope(face_ref[0:8])).astype(BF)
    parts = [
        dot(d_pre, w_feature[256 * g : 256 * g + 256, :], 1, 1) for g in range(GROUPS)
    ]
    d_crop = jnp.concatenate(parts, axis=0).astype(BF)
    last = dot(d_pre, w_feature[GROUPS * 256 : CROP, :], 1, 1).astype(BF)
    index = lax.broadcasted_iota(jnp.int32, (TOK, ROWS), 1)
    token = lax.broadcasted_iota(jnp.int32, (TOK, ROWS), 0)
    tail = lax.broadcasted_iota(jnp.int32, (TOK, 8), 1) + ROWS
    pick = (token_of(rows, cols, tail, 0) == token[:, 0:8]).astype(BF)
    d_latent = dot(pick, last, 1, 0)
    for i in range(4):
        pick = (token_of(rows, cols, index, i) == token).astype(BF)
        piece = dot(d_crop, shifted(CH, 256, CH * i), 1, 1).astype(BF)
        d_latent += dot(pick, piece, 1, 0)
    d_latent = d_latent.astype(BF)
    latent_ref[...] = d_latent
    lane = lax.broadcasted_iota(jnp.int32, (KH, 128), 1)
    for p in range(8):
        part = dot(d_latent, x_ref[:, p * PAIR : p * PAIR + PAIR], 0, 0)
        for u in range(6):
            top = part[0:KH, 128 * (u // 2) : 128 * (u // 2) + 128]
            bottom = part[KH : 2 * KH, 128 * (u // 2) : 128 * (u // 2) + 128]
            if u % 2 == 0:
                unit = jnp.where(lane < 64, top, pltpu.roll(bottom, 64, 1))
            else:
                unit = jnp.where(lane < 64, pltpu.roll(top, 64, 1), bottom)
            j = 2 * p + u // 3
            share(half, unit.astype(BF), keep, give, 4 * (j % 4) + j // 4, u % 3)


def share(half, unit, keep, give, j, u):
    top, bottom = unit[0 : KH // 2], unit[KH // 2 : KH]
    keep[j, u] = jnp.where(half == 0, top, bottom)
    give[j, u] = jnp.where(half == 0, bottom, top)


def main(*args):
    shares = jax.ShapeDtypeStruct((16, 3, KH // 2, 128), BF)
    return pl.pallas_call(
        main_kernel,
        out_shape=(shares, shares, jax.ShapeDtypeStruct((TOK, CH), BF)),
        in_specs=[SMEM] * 4 + vmem(12),
        out_specs=tuple(vmem(3)),
        compiler_params=params(24),
        cost_estimate=cost(3),
        name="main",
    )(*args)


def through_kernel(latent, maps, *refs):
    blocks, (out, cross_ref, stack, slab, sems) = refs[0:8], refs[8:]
    f, c = lax.axis_index("fsdp"), lax.axis_index("dp") & 1
    total = jnp.zeros((CH, 128), F32)
    for p, tiles, beside in side_by_side(f, c, 1, blocks):
        total += beside
        for t in range(3):
            stack[0:CH, pl.ds(pl.multiple_of(p * PAIR + 128 * t, 128), 128)] = tiles[t]
    cross_ref[...] = dot(total.astype(BF), shifted(CH, 128, 64), 1, 1).astype(BF)
    stack[CH : CH + RANK, :] = maps[...]
    widen = shifted(CH, 128, 0).astype(F32) + dot(cross_ref[...], shifted(RANK, 128, CH), 1, 0)
    wide = dot(latent[...], widen.astype(BF), 1, 0).astype(BF)
    copies = []
    for i in range(D // BLOCK):
        slab[i] = dot(wide, stack[:, BLOCK * i : BLOCK * i + BLOCK], 1, 0).astype(BF)
        copy = pltpu.make_async_copy(
            slab.at[i], out.at[:, pl.ds(BLOCK * i, BLOCK)], sems.at[i]
        )
        copy.start()
        copies.append(copy)
    for copy in copies:
        copy.wait()


def through(*args):
    return pl.pallas_call(
        through_kernel,
        out_shape=(
            jax.ShapeDtypeStruct((TOK, D), BF),
            jax.ShapeDtypeStruct((CH, RANK), BF),
        ),
        in_specs=vmem(10),
        out_specs=(pl.BlockSpec(memory_space=pl.ANY), pl.BlockSpec(memory_space=pltpu.VMEM)),
        scratch_shapes=[
            pltpu.VMEM((CH + RANK, D), BF),
            pltpu.VMEM((D // BLOCK, TOK, BLOCK), BF),
            pltpu.SemaphoreType.DMA((D // BLOCK,)),
        ],
        compiler_params=params(16),
        cost_estimate=cost(3),
        name="through",
    )(*args)


def last_kernel(units, cross, own_proj, grad_a, grad_b):
    unit = [units[u] for u in range(4)]

    def rows(right):
        total = jnp.zeros((KH, SHARD), F32)
        for u in range(3):
            r = lax.broadcasted_iota(jnp.int32, (128, SHARD), 0) - 64 * right
            col = lax.broadcasted_iota(jnp.int32, (128, SHARD), 1) - 64 * u
            place_at = ((r == col) & (col >= 0) & (col < 64)).astype(BF)
            total += dot(unit[u], place_at, 1, 0)
        return total

    sums = jnp.concatenate([rows(0), rows(1)], axis=0).astype(BF)
    low = jnp.concatenate(
        [dot(unit[3], shifted(RANK, 128, 64 * h), 1, 1) for h in range(2)], axis=0
    ).astype(BF)
    grad_a[...] = dot(cross[...], sums, 0, 0) / loss_scale
    grad_b[...] = dot(low, own_proj[...], 0, 0) / loss_scale


def last(*args):
    return pl.pallas_call(
        last_kernel,
        out_shape=(
            jax.ShapeDtypeStruct((RANK, SHARD), F32),
            jax.ShapeDtypeStruct((RANK, SHARD), F32),
        ),
        in_specs=vmem(3),
        out_specs=tuple(vmem(2)),
        compiler_params=params(8),
        cost_estimate=cost(1),
        name="last",
    )(*args)


def add(*terms):
    return sum(t.astype(F32) for t in terms).astype(BF)


def fan(value, **axis):
    ((name, _),) = axis.items()
    return [send(value, flip(**{name: k, "c": 1})) for k in (1, 2, 3)]


def parity(f, d):
    return (d ^ (d >> 1) ^ f ^ (f >> 2)) & 1


def exchange(v, groups):
    v = lax.all_to_all(v, AXES, 0, 0, axis_index_groups=groups, tiled=True)
    return jnp.sum(v.astype(F32), axis=0).astype(BF)


def beside(v, low):
    return jnp.concatenate([v, jnp.broadcast_to(low[None], v.shape[:1] + low.shape)], axis=1)


def shift_z(step):
    def move(zl, y, zh, x, c):
        z = (zh * 4 + zl + step) % 8
        return z % 4, y, z // 4, x, c

    return [(i, number(*move(*coords(i)))) for i in range(256)]


def slab_of(value, start, size):
    return lax.dynamic_slice_in_dim(value, start, size, axis=0)


def members(key):
    groups = {}
    for i in range(256):
        groups.setdefault(key(*coords(i)), []).append(i)
    return list(groups.values())


def reduce_all(keep, give, keep_low, give_low, f, half):
    zl, y = f // 4, f % 4
    v = add(keep, send(give, flip(c=1)))
    low = add(keep_low, send(give_low, flip(c=1)))
    v = v.reshape((4, 12) + v.shape[2:])
    part = lambda k: jnp.concatenate([slab_of(v, y ^ k, 1)[0], low])
    v = add(part(0), *[send(part(k), flip(y=k, c=k & 1)) for k in (2, 1, 3)])
    v, low = v[:12].reshape((4, 3) + v.shape[1:]), v[12:]
    v = beside(v, low)
    v = jnp.broadcast_to(v[:, None], (4, 2) + v.shape[1:]).reshape((8,) + v.shape[1:])
    v = exchange(v, members(lambda zl, y, zh, x, c: (y, x, c ^ (zl & 1))))
    other = send(v, flip(c=1))
    v = jnp.concatenate([jnp.where(half == 0, v, other), jnp.where(half == 0, other, v)], axis=1)
    return add(v, *fan(v, x=0))


def local(
    block_in,
    block_out,
    weight,
    adapter_a,
    adapter_b,
    proj,
    w_feature,
    w_embed,
    id_table,
    box_rows,
    box_cols,
    identity,
    face_count,
):
    f, d = lax.axis_index("fsdp"), lax.axis_index("dp")
    proj_t = proj.T

    table = jnp.concatenate([id_table, send(id_table, flip(zl=2, zh=1, c=1))])
    maps, own_proj, faces = front(
        box_rows, box_cols, proj_t, weight, adapter_a.T, adapter_b,
        block_out, w_feature, w_embed,
    )
    maps = after(maps, table)
    tables = fan(table, x=0)
    maps = jnp.concatenate([maps] + fan(maps, zl=0))
    tables = [table] + tables
    blocks = [maps] + fan(maps, y=0)
    tables += [send(part, flip(c=1)) for part in tables]
    blocks += [send(part, flip(c=1)) for part in blocks]
    keep, give, d_latent = main(
        box_rows, box_cols, identity, face_count,
        *tables, faces, w_embed, w_feature, block_in,
    )
    whole_a, keep_low, give_low = low_maps(block_in, d_latent, *blocks)
    total = reduce_all(keep, give, keep_low, give_low, f, parity(f, d))
    grad_in, cross = through(d_latent, whole_a, *blocks)
    grad_a, grad_b = last(total, cross, own_proj)
    return grad_in, grad_a.T, grad_b


def solution(mesh):
    return jax.shard_map(
        local,
        mesh=mesh,
        in_specs=(
            P(("fsdp", "dp"), None),
            P(("fsdp", "dp"), None),
            P("fsdp", None),
            P("fsdp", None),
            P(None, "fsdp"),
            P(),
            P(),
            P(),
            P("dp", None),
            P(("fsdp", "dp"), None),
            P(("fsdp", "dp"), None),
            P(("fsdp", "dp"), None),
            P(("fsdp", "dp")),
        ),
        out_specs=(P(("fsdp", "dp"), None), P("fsdp", None), P(None, "fsdp")),
        check_vma=False,
    )
```

time: 79.3 us -> 72.3 us (0.912)
  blocking collectives: 21 us -> 9.43 us
  starting transfers between devices: 25.1 us -> 34.4 us
  local copies, waits for them, and re-layouts: 3.88 us -> 1.66 us
  waiting for transfers between devices: 12.5 us -> 11.3 us
  Pallas kernels: 14.5 us -> 13.5 us
    all_to_all x2 -> x1, blocking collectives: 21 us -> 9.43 us  [exchange(): v = lax.all_to_all(v, AXES, 0, 0, axis_index_groups=groups, tiled=True)]
    ppermute x16 -> x27, starting transfers between devices: 25.1 us -> 34.4 us  [send(): return lax.ppermute(value, AXES, perm)]
    unnamed x27 -> x22, local copies, waits for them, and re-layouts: 3.83 us -> 1.59 us
    ppermute x16 -> x27, waiting for transfers between devices: 12.5 us -> 11.3 us  [send(): return lax.ppermute(value, AXES, perm)]
    pallas_call x2 -> x1, Pallas kernels: 6.82 us -> 6.85 us  [front(): pl.pallas_call(front_kernel, out_shape=(jax.ShapeDtypeStruct((1, CH, 256)...]
  transfers between devices with their start and end apart: 16 -> 27, of which waited for: 9 -> 10; matrix products, arithmetic and copies ran while one was open for 0% -> 1% of each run, Pallas kernels for 13% -> 16%
where the time goes in v3:
time: 72.3 us; the launch traced here: 72.1 us
  starting transfers between devices  34.4 us (48%)
  Pallas kernels  13.5 us (19%)
  waiting for transfers between devices  11.3 us (16%)
  blocking collectives  9.43 us (13%)
  local copies, waits for them, and re-layouts  1.66 us (2%)
  between operations  1.59 us (2%)
    ppermute x27, starting transfers between devices, send(): return lax.ppermute(value, AXES, perm)  34.4 us
    ppermute x27, waiting for transfers between devices, send(): return lax.ppermute(value, AXES, perm)  11.3 us
    all_to_all x1, blocking collectives, exchange(): v = lax.all_to_all(v, AXES, 0, 0, axis_index_groups=groups, tiled=True)  9.43 us
    pallas_call x1, Pallas kernels, front(): pl.pallas_call(front_kernel, out_shape=(jax.ShapeDtypeStruct((1, CH, 256)...  6.85 us
    pallas_call x1, Pallas kernels, main(): pl.pallas_call(main_kernel, out_shape=(shares, shares, jax.ShapeDtypeStru...  2.8 us
    pallas_call x1, Pallas kernels, through(): pl.pallas_call(through_kernel, out_shape=(jax.ShapeDtypeStruct((TOK, D),...  1.83 us
    unnamed x22, local copies, waits for them, and re-layouts  1.59 us
  transfers between devices with their start and end apart: 27, of which 10 were waited for; matrix products, arithmetic and copies ran while one was open for 1% of the time, Pallas kernels for 16%

profile of v3, /device:TPU:1, one launch (start us, length us, event | category | flops | bytes accessed | tf_op | source)
XLA Modules:
  0.0 72.1 jit_solution(2315440990152004906)
XLA Ops:
  0.6 7.5 %collective-permute-start = (bf16[64,512]{1,0:T(8,128)(2,1)}, bf16[64,512]{1,0:T(8,128)(2,1)S(1)}, u32[]{:S(2)}, u32[]{:S(2)}) collective-permute-start(bf16[64,512]{1,0:T(8,128)(2,1)} %param.21), channel_id=1, source_target_pairs={{0,137},{1,136},{2,139},{3,138},{4,141},{5,140},{6,143},{7,142},{8... | collective-permute-start | bytes 196616 | tf_op jit(solution)/shard_map/ppermute | solution.py:49
  8.2 6.8 %front.1 = (bf16[1,64,256]{2,1,0:T(8,128)(2,1)}, bf16[64,192]{1,0:T(8,128)(2,1)}, f32[16,512]{1,0:T(8,128)}) custom-call(s32[1,6]{1,0:T(1,128)} %rows.3, s32[1,6]{1,0:T(1,128)} %cols.3, bf16[64,3072]{1,0:T(8,128)(2,1)} %bitcast.18, bf16[192,3072]{1,0:T(8,128)(2,1)} %weight_hbm.1, bf16[64,192]{1,0:T(8,128)(2,1)} %bitcast.20, bf16[64,192]{1,0:T(8,128)(2,1)} %b_hbm.1, ...), custom_call_target="tpu_custom_call" | custom-call | flops 4 | bytes 4 | tf_op jit(solution)/shard_map/front/pallas_call | solution.py:177
  15.1 0.0 collective-permute-done
  15.1 1.2 %collective-permute-start.10 = (bf16[1,64,256]{2,1,0:T(8,128)(2,1)}, bf16[1,64,256]{2,1,0:T(8,128)(2,1)S(1)}, u32[]{:S(2)}, u32[]{:S(2)}) collective-permute-start(bf16[1,64,256]{2,1,0:T(8,128)(2,1)} %get-tuple-element.20), channel_id=1, source_target_pairs={{0,193},{1,192},{2,195},{3,194},{4,197},{5,196},{6,199},{7,198},{8... | collective-permute-start | bytes 98312 | tf_op jit(solution)/shard_map/ppermute | solution.py:49
  16.3 1.0 %collective-permute-start.9 = (bf16[1,64,256]{2,1,0:T(8,128)(2,1)}, bf16[1,64,256]{2,1,0:T(8,128)(2,1)S(1)}, u32[]{:S(2)}, u32[]{:S(2)}) collective-permute-start(bf16[1,64,256]{2,1,0:T(8,128)(2,1)} %get-tuple-element.20), channel_id=1, source_target_pairs={{0,129},{1,128},{2,131},{3,130},{4,133},{5,132},{6,135},{7,134},{8... | collective-permute-start | bytes 98312 | tf_op jit(solution)/shard_map/ppermute | solution.py:49
  17.4 1.2 %collective-permute-start.8 = (bf16[1,64,256]{2,1,0:T(8,128)(2,1)}, bf16[1,64,256]{2,1,0:T(8,128)(2,1)S(1)}, u32[]{:S(2)}, u32[]{:S(2)}) collective-permute-start(bf16[1,64,256]{2,1,0:T(8,128)(2,1)} %get-tuple-element.20), channel_id=1, source_target_pairs={{0,65},{1,64},{2,67},{3,66},{4,69},{5,68},{6,71},{7,70},{8,73},{9,... | collective-permute-start | bytes 98312 | tf_op jit(solution)/shard_map/ppermute | solution.py:49
  18.5 0.8 %constant_dynamic-update-slice_fusion.5 = bf16[4,64,256]{2,1,0:T(8,128)(2,1)S(1)} fusion(bf16[1,64,256]{2,1,0:T(8,128)(2,1)} %get-tuple-element.20), kind=kLoop, calls=%fused_computation.20 | loop fusion | bytes 65536
  19.3 0.9 %collective-permute-start.4 = (bf16[128,512]{1,0:T(8,128)(2,1)S(1)}, bf16[128,512]{1,0:T(8,128)(2,1)S(1)}, u32[]{:S(2)}, u32[]{:S(2)}) collective-permute-start(bf16[128,512]{1,0:T(8,128)(2,1)S(1)} %constant_dynamic-update-slice_fusion.refs_0_), channel_id=1, source_target_pairs={{0,1},{1,0},{2,3},{3,2},{4,5},{5,4},{6,7},{7,6},{8,9},{9,8},{10,11... | collective-permute-start | bytes 393224 | tf_op jit(solution)/shard_map/ppermute | solution.py:49
  20.2 2.4 %collective-permute-start.3 = (bf16[128,512]{1,0:T(8,128)(2,1)S(1)}, bf16[128,512]{1,0:T(8,128)(2,1)S(1)}, u32[]{:S(2)}, u32[]{:S(2)}) collective-permute-start(bf16[128,512]{1,0:T(8,128)(2,1)S(1)} %constant_dynamic-update-slice_fusion.refs_0_), channel_id=1, source_target_pairs={{0,7},{1,6},{2,5},{3,4},{4,3},{5,2},{6,1},{7,0},{8,15},{9,14},{10,... | collective-permute-start | bytes 393224 | tf_op jit(solution)/shard_map/ppermute | solution.py:49
  22.6 1.8 %collective-permute-start.2 = (bf16[128,512]{1,0:T(8,128)(2,1)S(1)}, bf16[128,512]{1,0:T(8,128)(2,1)S(1)}, u32[]{:S(2)}, u32[]{:S(2)}) collective-permute-start(bf16[128,512]{1,0:T(8,128)(2,1)S(1)} %constant_dynamic-update-slice_fusion.refs_0_), channel_id=1, source_target_pairs={{0,5},{1,4},{2,7},{3,6},{4,1},{5,0},{6,3},{7,2},{8,13},{9,12},{10,... | collective-permute-start | bytes 393224 | tf_op jit(solution)/shard_map/ppermute | solution.py:49
  24.4 0.8 %collective-permute-start.1 = (bf16[128,512]{1,0:T(8,128)(2,1)S(1)}, bf16[128,512]{1,0:T(8,128)(2,1)S(1)}, u32[]{:S(2)}, u32[]{:S(2)}) collective-permute-start(bf16[128,512]{1,0:T(8,128)(2,1)S(1)} %constant_dynamic-update-slice_fusion.refs_0_), channel_id=1, source_target_pairs={{0,3},{1,2},{2,1},{3,0},{4,7},{5,6},{6,5},{7,4},{8,11},{9,10},{10,... | collective-permute-start | bytes 393224 | tf_op jit(solution)/shard_map/ppermute | solution.py:49
  25.2 2.6 %collective-permute-start.13 = (bf16[4,64,256]{2,1,0:T(8,128)(2,1)S(1)}, bf16[4,64,256]{2,1,0:T(8,128)(2,1)S(1)}, u32[]{:S(2)}, u32[]{:S(2)}) collective-permute-start(bf16[4,64,256]{2,1,0:T(8,128)(2,1)S(1)} %constant_dynamic-update-slice_fusion.2.refs_0_), channel_id=1, source_target_pairs={{0,49},{1,48},{2,51},{3,50},{4,53},{5,52},{6,55},{7,54},{8,57},{9,... | collective-permute-start | bytes 393224 | tf_op jit(solution)/shard_map/ppermute | solution.py:49
  27.8 0.0 collective-permute-done.4.refs_4_
  27.8 0.9 %collective-permute-start.12 = (bf16[4,64,256]{2,1,0:T(8,128)(2,1)S(1)}, bf16[4,64,256]{2,1,0:T(8,128)(2,1)S(1)}, u32[]{:S(2)}, u32[]{:S(2)}) collective-permute-start(bf16[4,64,256]{2,1,0:T(8,128)(2,1)S(1)} %constant_dynamic-update-slice_fusion.2.refs_0_), channel_id=1, source_target_pairs={{0,33},{1,32},{2,35},{3,34},{4,37},{5,36},{6,39},{7,38},{8,41},{9,... | collective-permute-start | bytes 393224 | tf_op jit(solution)/shard_map/ppermute | solution.py:49
  28.7 1.5 %collective-permute-start.11 = (bf16[4,64,256]{2,1,0:T(8,128)(2,1)S(1)}, bf16[4,64,256]{2,1,0:T(8,128)(2,1)S(1)}, u32[]{:S(2)}, u32[]{:S(2)}) collective-permute-start(bf16[4,64,256]{2,1,0:T(8,128)(2,1)S(1)} %constant_dynamic-update-slice_fusion.2.refs_0_), channel_id=1, source_target_pairs={{0,17},{1,16},{2,19},{3,18},{4,21},{5,20},{6,23},{7,22},{8,25},{9,... | collective-permute-start | bytes 393224 | tf_op jit(solution)/shard_map/ppermute | solution.py:49
  30.2 1.4 %collective-permute-done.1.refs_1_ = bf16[128,512]{1,0:T(8,128)(2,1)S(1)} collective-permute-done((bf16[128,512]{1,0:T(8,128)(2,1)S(1)}, bf16[128,512]{1,0:T(8,128)(2,1)S(1)}, u32[]{:S(2)}, u32[]{:S(2)}) %collective-permute-start.1) | collective-permute-done | bytes 131104 | tf_op jit(solution)/shard_map/ppermute | solution.py:49
  31.6 1.4 %collective-permute-done.13.refs_3_ = bf16[4,64,256]{2,1,0:T(8,128)(2,1)S(1)} collective-permute-done((bf16[4,64,256]{2,1,0:T(8,128)(2,1)S(1)}, bf16[4,64,256]{2,1,0:T(8,128)(2,1)S(1)}, u32[]{:S(2)}, u32[]{:S(2)}) %collective-permute-start.13) | collective-permute-done | bytes 131104 | tf_op jit(solution)/shard_map/ppermute | solution.py:49
  33.0 1.3 %collective-permute-start.5 = (bf16[128,512]{1,0:T(8,128)(2,1)S(1)}, bf16[128,512]{1,0:T(8,128)(2,1)S(1)}, u32[]{:S(2)}, u32[]{:S(2)}) collective-permute-start(bf16[128,512]{1,0:T(8,128)(2,1)S(1)} %collective-permute-done.1.refs_1_), channel_id=1, source_target_pairs={{0,1},{1,0},{2,3},{3,2},{4,5},{5,4},{6,7},{7,6},{8,9},{9,8},{10,11... | collective-permute-start | bytes 393224 | tf_op jit(solution)/shard_map/ppermute | solution.py:49
  34.3 1.0 %collective-permute-done.12.refs_2_ = bf16[4,64,256]{2,1,0:T(8,128)(2,1)S(1)} collective-permute-done((bf16[4,64,256]{2,1,0:T(8,128)(2,1)S(1)}, bf16[4,64,256]{2,1,0:T(8,128)(2,1)S(1)}, u32[]{:S(2)}, u32[]{:S(2)}) %collective-permute-start.12) | collective-permute-done | bytes 131104 | tf_op jit(solution)/shard_map/ppermute | solution.py:49
  35.4 0.4 collective-permute-start.14
  35.8 0.1 collective-permute-start.17
  35.9 0.4 collective-permute-start.16
  36.3 0.3 collective-permute-start.15
  37.3 0.0 copy-start.3
  37.3 0.7 %copy-done.3 = f32[16,512]{1,0:T(8,128)S(1)} copy-done((f32[16,512]{1,0:T(8,128)S(1)}, f32[16,512]{1,0:T(8,128)}, u32[]{:S(2)}) %copy-start.3) | copy-done | bytes 32792
  38.0 2.8 %main.1 = (bf16[16,3,16,128]{3,2,1,0:T(8,128)(2,1)S(1)}, bf16[16,3,16,128]{3,2,1,0:T(8,128)(2,1)S(1)}, bf16[256,64]{1,0:T(8,128)(2,1)S(1)}) custom-call(s32[1,6]{1,0:T(1,128)S(1)} %copy-done.5, s32[1,6]{1,0:T(1,128)S(1)} %copy-done.6, s32[1,6]{1,0:T(1,128)S(1)} %copy-done.7, s32[1]{0:T(128)S(6)} %copy.20.count, ...), custom_call_target="tpu_custom_call" | custom-call | flops 3 | bytes 3 | tf_op jit(solution)/shard_map/main/pallas_call | solution.py:332
  40.9 1.0 %low.1 = (bf16[64,3072]{1,0:T(8,128)(2,1)S(1)}, bf16[1,16,128]{2,1,0:T(8,128)(2,1)S(1)}, bf16[1,16,128]{2,1,0:T(8,128)(2,1)S(1)}) custom-call(bf16[256,3072]{1,0:T(8,128)(2,1)S(1)} %copy-done.1, bf16[256,64]{1,0:T(8,128)(2,1)S(1)} %get-tuple-element.18.latent, bf16[4,64,256]{2,1,0:T(8,128)(2,1)S(1)} %constant_dynamic-update-slice_fusion.2.refs_0_, ...), custom_call_target="tpu_custom_call" | custom-call | flops 2 | bytes 2 | tf_op jit(solution)/shard_map/low/pallas_call | solution.py:247
  41.9 0.3 collective-permute-start.19
  42.2 0.3 collective-permute-start.18
  42.5 0.7 collective-permute-done.19
  43.1 0.5 collective-permute-done.18
  43.6 0.1 add_convert_fusion
  43.7 0.0 copy-start.4
  43.8 3.1 %collective-permute-start.20 = (bf16[13,16,128]{2,1,0:T(8,128)(2,1)S(1)}, bf16[13,16,128]{2,1,0:T(8,128)(2,1)S(1)}, u32[]{:S(2)}, u32[]{:S(2)}) collective-permute-start(bf16[13,16,128]{2,1,0:T(8,128)(2,1)S(1)} %get-tuple-element.37), channel_id=1, source_target_pairs={{0,32},{1,33},{2,34},{3,35},{4,36},{5,37},{6,38},{7,39},{8,40},{9,... | collective-permute-start | bytes 159752 | tf_op jit(solution)/shard_map/ppermute | solution.py:49
  46.9 0.8 %collective-permute-start.21 = (bf16[13,16,128]{2,1,0:T(8,128)(2,1)S(1)}, bf16[13,16,128]{2,1,0:T(8,128)(2,1)S(1)}, u32[]{:S(2)}, u32[]{:S(2)}) collective-permute-start(bf16[13,16,128]{2,1,0:T(8,128)(2,1)S(1)} %get-tuple-element.38), channel_id=1, source_target_pairs={{0,17},{1,16},{2,19},{3,18},{4,21},{5,20},{6,23},{7,22},{8,25},{9,... | collective-permute-start | bytes 159752 | tf_op jit(solution)/shard_map/ppermute | solution.py:49
  47.7 0.2 collective-permute-start.22
  47.9 0.5 collective-permute-done.20
  48.4 2.6 %collective-permute-done.21 = bf16[13,16,128]{2,1,0:T(8,128)(2,1)S(1)} collective-permute-done((bf16[13,16,128]{2,1,0:T(8,128)(2,1)S(1)}, bf16[13,16,128]{2,1,0:T(8,128)(2,1)S(1)}, u32[]{:S(2)}, u32[]{:S(2)}) %collective-permute-start.21) | collective-permute-done | bytes 53280 | tf_op jit(solution)/shard_map/ppermute | solution.py:49
  51.0 1.5 %collective-permute-done.22 = bf16[13,16,128]{2,1,0:T(8,128)(2,1)S(1)} collective-permute-done((bf16[13,16,128]{2,1,0:T(8,128)(2,1)S(1)}, bf16[13,16,128]{2,1,0:T(8,128)(2,1)S(1)}, u32[]{:S(2)}, u32[]{:S(2)}) %collective-permute-start.22) | collective-permute-done | bytes 53280 | tf_op jit(solution)/shard_map/ppermute | solution.py:49
  52.6 9.4 %all_to_all.5 = bf16[8,4,16,128]{3,2,1,0:T(8,128)(2,1)S(1)} all-to-all(bf16[8,4,16,128]{3,2,1,0:T(8,128)(2,1)S(1)} %bitcast.17), channel_id=1, replica_groups={{0,8,65,73,128,136,193,201},{1,9,64,72,129,137,192,200},{2,10,67,75,130..., dimensions={0} | all-to-all | bytes 262144 | tf_op jit(solution)/shard_map/all_to_all | solution.py:436
  62.0 1.5 %collective-permute-start.23 = (bf16[4,16,128]{2,1,0:T(8,128)(2,1)S(1)}, bf16[4,16,128]{2,1,0:T(8,128)(2,1)S(1)}, u32[]{:S(2)}, u32[]{:S(2)}) collective-permute-start(bf16[4,16,128]{2,1,0:T(8,128)(2,1)S(1)} %reduce_sum.12), channel_id=1, source_target_pairs={{0,1},{1,0},{2,3},{3,2},{4,5},{5,4},{6,7},{7,6},{8,9},{9,8},{10,11... | collective-permute-start | bytes 49160 | tf_op jit(solution)/shard_map/ppermute | solution.py:49
  63.5 0.8 %collective-permute-done.23 = bf16[4,16,128]{2,1,0:T(8,128)(2,1)S(1)} collective-permute-done((bf16[4,16,128]{2,1,0:T(8,128)(2,1)S(1)}, bf16[4,16,128]{2,1,0:T(8,128)(2,1)S(1)}, u32[]{:S(2)}, u32[]{:S(2)}) %collective-permute-start.23) | collective-permute-done | bytes 16416 | tf_op jit(solution)/shard_map/ppermute | solution.py:49
  64.4 2.0 %collective-permute-start.25 = (bf16[4,32,128]{2,1,0:T(8,128)(2,1)S(1)}, bf16[4,32,128]{2,1,0:T(8,128)(2,1)S(1)}, u32[]{:S(2)}, u32[]{:S(2)}) collective-permute-start(bf16[4,32,128]{2,1,0:T(8,128)(2,1)S(1)} %pad_maximum_fusion.5), channel_id=1, source_target_pairs={{0,5},{1,4},{2,7},{3,6},{4,1},{5,0},{6,3},{7,2},{8,13},{9,12},{10,... | collective-permute-start | bytes 98312 | tf_op jit(solution)/shard_map/ppermute | solution.py:49
  66.4 0.1 collective-permute-start.24
  66.5 1.8 %collective-permute-start.26 = (bf16[4,32,128]{2,1,0:T(8,128)(2,1)S(1)}, bf16[4,32,128]{2,1,0:T(8,128)(2,1)S(1)}, u32[]{:S(2)}, u32[]{:S(2)}) collective-permute-start(bf16[4,32,128]{2,1,0:T(8,128)(2,1)S(1)} %pad_maximum_fusion.5), channel_id=1, source_target_pairs={{0,7},{1,6},{2,5},{3,4},{4,3},{5,2},{6,1},{7,0},{8,15},{9,14},{10,... | collective-permute-start | bytes 98312 | tf_op jit(solution)/shard_map/ppermute | solution.py:49
  68.3 1.8 %through.1 = (bf16[256,3072]{1,0:T(8,128)(2,1)}, bf16[64,64]{1,0:T(8,128)(2,1)S(1)}) custom-call(bf16[256,64]{1,0:T(8,128)(2,1)S(1)} %get-tuple-element.18.latent, bf16[64,3072]{1,0:T(8,128)(2,1)S(1)} %get-tuple-element.21.maps, bf16[4,64,256]{2,1,0:T(8,128)(2,1)S(1)} %constant_dynamic-update-slice_fusion.2.refs_0_, ...), custom_call_target="tpu_custom_call" | custom-call | flops 3 | bytes 3 | tf_op jit(solution)/shard_map/through/pallas_call | solution.py:368
  70.1 0.9 %collective-permute-done.26 = bf16[4,32,128]{2,1,0:T(8,128)(2,1)S(1)} collective-permute-done((bf16[4,32,128]{2,1,0:T(8,128)(2,1)S(1)}, bf16[4,32,128]{2,1,0:T(8,128)(2,1)S(1)}, u32[]{:S(2)}, u32[]{:S(2)}) %collective-permute-start.26) | collective-permute-done | bytes 32800 | tf_op jit(solution)/shard_map/ppermute | solution.py:49
  71.1 1.0 %last.1 = (f32[64,192]{1,0:T(8,128)}, f32[64,192]{1,0:T(8,128)}) custom-call(bf16[4,32,128]{2,1,0:T(8,128)(2,1)S(1)} %add_convert_fusion.2.units, bf16[64,64]{1,0:T(8,128)(2,1)S(1)} %get-tuple-element.27.cross, bf16[64,192]{1,0:T(8,128)(2,1)S(1)} %copy-done.4), custom_call_target="tpu_custom_call" | custom-call | flops 1 | bytes 1 | tf_op jit(solution)/shard_map/last/pallas_call | solution.py:408
  (50 shorter events, 0.3 us)
Async XLA Ops:
  0.6 14.4 %collective-permute-start = (bf16[64,512]{1,0:T(8,128)(2,1)}, bf16[64,512]{1,0:T(8,128)(2,1)S(1)}, u32[]{:S(2)}, u32[]{:S(2)}) collective-permute-start(bf16[64,512]{1,0:T(8,128)(2,1)} %param.21), channel_id=1, source_target_pairs={{0,137},{1,136},{2,139},{3,138},{4,141},{5,140},{6,143},{7,142},{8... | collective-permute-start | bytes 196616 | tf_op jit(solution)/shard_map/ppermute | solution.py:49
  8.1 6.9 %copy-start.8 = (bf16[64,512]{1,0:T(8,128)(2,1)S(1)}, bf16[64,512]{1,0:T(8,128)(2,1)}, u32[]{:S(2)}) copy-start(bf16[64,512]{1,0:T(8,128)(2,1)} %param.21) | copy-start | bytes 196612
  8.1 29.1 %copy-start = (bf16[3136,512]{1,0:T(8,128)(2,1)S(1)}, bf16[3136,512]{1,0:T(8,128)(2,1)}, u32[]{:S(2)}) copy-start(bf16[3136,512]{1,0:T(8,128)(2,1)} %refs_10_.1) | copy-start | bytes 9633796
  8.1 29.1 %copy-start.1 = (bf16[256,3072]{1,0:T(8,128)(2,1)S(1)}, bf16[256,3072]{1,0:T(8,128)(2,1)}, u32[]{:S(2)}) copy-start(bf16[256,3072]{1,0:T(8,128)(2,1)} %x_ref.1) | copy-start | bytes 4718596
  8.1 29.1 %copy-start.2 = (bf16[512,512]{1,0:T(8,128)(2,1)S(1)}, bf16[512,512]{1,0:T(8,128)(2,1)}, u32[]{:S(2)}) copy-start(bf16[512,512]{1,0:T(8,128)(2,1)} %refs_9_.1) | copy-start | bytes 1572868
  8.1 29.1 %copy-start.5 = (s32[1,6]{1,0:T(1,128)S(1)}, s32[1,6]{1,0:T(1,128)}, u32[]{:S(2)}) copy-start(s32[1,6]{1,0:T(1,128)} %rows.3) | copy-start | bytes 76
  8.2 29.1 %copy-start.6 = (s32[1,6]{1,0:T(1,128)S(1)}, s32[1,6]{1,0:T(1,128)}, u32[]{:S(2)}) copy-start(s32[1,6]{1,0:T(1,128)} %cols.3) | copy-start | bytes 76
  8.2 29.1 %copy-start.7 = (s32[1,6]{1,0:T(1,128)S(1)}, s32[1,6]{1,0:T(1,128)}, u32[]{:S(2)}) copy-start(s32[1,6]{1,0:T(1,128)} %ident.1) | copy-start | bytes 76
  15.1 10.1 %collective-permute-start.10 = (bf16[1,64,256]{2,1,0:T(8,128)(2,1)}, bf16[1,64,256]{2,1,0:T(8,128)(2,1)S(1)}, u32[]{:S(2)}, u32[]{:S(2)}) collective-permute-start(bf16[1,64,256]{2,1,0:T(8,128)(2,1)} %get-tuple-element.20), channel_id=1, source_target_pairs={{0,193},{1,192},{2,195},{3,194},{4,197},{5,196},{6,199},{7,198},{8... | collective-permute-start | bytes 98312 | tf_op jit(solution)/shard_map/ppermute | solution.py:49
  16.3 8.1 %collective-permute-start.9 = (bf16[1,64,256]{2,1,0:T(8,128)(2,1)}, bf16[1,64,256]{2,1,0:T(8,128)(2,1)S(1)}, u32[]{:S(2)}, u32[]{:S(2)}) collective-permute-start(bf16[1,64,256]{2,1,0:T(8,128)(2,1)} %get-tuple-element.20), channel_id=1, source_target_pairs={{0,129},{1,128},{2,131},{3,130},{4,133},{5,132},{6,135},{7,134},{8... | collective-permute-start | bytes 98312 | tf_op jit(solution)/shard_map/ppermute | solution.py:49
  17.4 5.2 %collective-permute-start.8 = (bf16[1,64,256]{2,1,0:T(8,128)(2,1)}, bf16[1,64,256]{2,1,0:T(8,128)(2,1)S(1)}, u32[]{:S(2)}, u32[]{:S(2)}) collective-permute-start(bf16[1,64,256]{2,1,0:T(8,128)(2,1)} %get-tuple-element.20), channel_id=1, source_target_pairs={{0,65},{1,64},{2,67},{3,66},{4,69},{5,68},{6,71},{7,70},{8,73},{9,... | collective-permute-start | bytes 98312 | tf_op jit(solution)/shard_map/ppermute | solution.py:49
  19.3 8.5 %collective-permute-start.4 = (bf16[128,512]{1,0:T(8,128)(2,1)S(1)}, bf16[128,512]{1,0:T(8,128)(2,1)S(1)}, u32[]{:S(2)}, u32[]{:S(2)}) collective-permute-start(bf16[128,512]{1,0:T(8,128)(2,1)S(1)} %constant_dynamic-update-slice_fusion.refs_0_), channel_id=1, source_target_pairs={{0,1},{1,0},{2,3},{3,2},{4,5},{5,4},{6,7},{7,6},{8,9},{9,8},{10,11... | collective-permute-start | bytes 393224 | tf_op jit(solution)/shard_map/ppermute | solution.py:49
  20.2 8.5 %collective-permute-start.3 = (bf16[128,512]{1,0:T(8,128)(2,1)S(1)}, bf16[128,512]{1,0:T(8,128)(2,1)S(1)}, u32[]{:S(2)}, u32[]{:S(2)}) collective-permute-start(bf16[128,512]{1,0:T(8,128)(2,1)S(1)} %constant_dynamic-update-slice_fusion.refs_0_), channel_id=1, source_target_pairs={{0,7},{1,6},{2,5},{3,4},{4,3},{5,2},{6,1},{7,0},{8,15},{9,14},{10,... | collective-permute-start | bytes 393224 | tf_op jit(solution)/shard_map/ppermute | solution.py:49
  22.6 7.6 %collective-permute-start.2 = (bf16[128,512]{1,0:T(8,128)(2,1)S(1)}, bf16[128,512]{1,0:T(8,128)(2,1)S(1)}, u32[]{:S(2)}, u32[]{:S(2)}) collective-permute-start(bf16[128,512]{1,0:T(8,128)(2,1)S(1)} %constant_dynamic-update-slice_fusion.refs_0_), channel_id=1, source_target_pairs={{0,5},{1,4},{2,7},{3,6},{4,1},{5,0},{6,3},{7,2},{8,13},{9,12},{10,... | collective-permute-start | bytes 393224 | tf_op jit(solution)/shard_map/ppermute | solution.py:49
  24.4 7.2 %collective-permute-start.1 = (bf16[128,512]{1,0:T(8,128)(2,1)S(1)}, bf16[128,512]{1,0:T(8,128)(2,1)S(1)}, u32[]{:S(2)}, u32[]{:S(2)}) collective-permute-start(bf16[128,512]{1,0:T(8,128)(2,1)S(1)} %constant_dynamic-update-slice_fusion.refs_0_), channel_id=1, source_target_pairs={{0,3},{1,2},{2,1},{3,0},{4,7},{5,6},{6,5},{7,4},{8,11},{9,10},{10,... | collective-permute-start | bytes 393224 | tf_op jit(solution)/shard_map/ppermute | solution.py:49
  25.2 7.8 %collective-permute-start.13 = (bf16[4,64,256]{2,1,0:T(8,128)(2,1)S(1)}, bf16[4,64,256]{2,1,0:T(8,128)(2,1)S(1)}, u32[]{:S(2)}, u32[]{:S(2)}) collective-permute-start(bf16[4,64,256]{2,1,0:T(8,128)(2,1)S(1)} %constant_dynamic-update-slice_fusion.2.refs_0_), channel_id=1, source_target_pairs={{0,49},{1,48},{2,51},{3,50},{4,53},{5,52},{6,55},{7,54},{8,57},{9,... | collective-permute-start | bytes 393224 | tf_op jit(solution)/shard_map/ppermute | solution.py:49
  27.8 7.5 %collective-permute-start.12 = (bf16[4,64,256]{2,1,0:T(8,128)(2,1)S(1)}, bf16[4,64,256]{2,1,0:T(8,128)(2,1)S(1)}, u32[]{:S(2)}, u32[]{:S(2)}) collective-permute-start(bf16[4,64,256]{2,1,0:T(8,128)(2,1)S(1)} %constant_dynamic-update-slice_fusion.2.refs_0_), channel_id=1, source_target_pairs={{0,33},{1,32},{2,35},{3,34},{4,37},{5,36},{6,39},{7,38},{8,41},{9,... | collective-permute-start | bytes 393224 | tf_op jit(solution)/shard_map/ppermute | solution.py:49
  28.7 7.0 %collective-permute-start.11 = (bf16[4,64,256]{2,1,0:T(8,128)(2,1)S(1)}, bf16[4,64,256]{2,1,0:T(8,128)(2,1)S(1)}, u32[]{:S(2)}, u32[]{:S(2)}) collective-permute-start(bf16[4,64,256]{2,1,0:T(8,128)(2,1)S(1)} %constant_dynamic-update-slice_fusion.2.refs_0_), channel_id=1, source_target_pairs={{0,17},{1,16},{2,19},{3,18},{4,21},{5,20},{6,23},{7,22},{8,25},{9,... | collective-permute-start | bytes 393224 | tf_op jit(solution)/shard_map/ppermute | solution.py:49
  30.2 5.7 %collective-permute-start.7 = (bf16[128,512]{1,0:T(8,128)(2,1)S(1)}, bf16[128,512]{1,0:T(8,128)(2,1)S(1)}, u32[]{:S(2)}, u32[]{:S(2)}) collective-permute-start(bf16[128,512]{1,0:T(8,128)(2,1)S(1)} %collective-permute-done.3.refs_3_), channel_id=1, source_target_pairs={{0,1},{1,0},{2,3},{3,2},{4,5},{5,4},{6,7},{7,6},{8,9},{9,8},{10,11... | collective-permute-start | bytes 393224 | tf_op jit(solution)/shard_map/ppermute | solution.py:49
  31.6 4.7 %collective-permute-start.6 = (bf16[128,512]{1,0:T(8,128)(2,1)S(1)}, bf16[128,512]{1,0:T(8,128)(2,1)S(1)}, u32[]{:S(2)}, u32[]{:S(2)}) collective-permute-start(bf16[128,512]{1,0:T(8,128)(2,1)S(1)} %collective-permute-done.2.refs_2_), channel_id=1, source_target_pairs={{0,1},{1,0},{2,3},{3,2},{4,5},{5,4},{6,7},{7,6},{8,9},{9,8},{10,11... | collective-permute-start | bytes 393224 | tf_op jit(solution)/shard_map/ppermute | solution.py:49
  33.0 4.2 %collective-permute-start.5 = (bf16[128,512]{1,0:T(8,128)(2,1)S(1)}, bf16[128,512]{1,0:T(8,128)(2,1)S(1)}, u32[]{:S(2)}, u32[]{:S(2)}) collective-permute-start(bf16[128,512]{1,0:T(8,128)(2,1)S(1)} %collective-permute-done.1.refs_1_), channel_id=1, source_target_pairs={{0,1},{1,0},{2,3},{3,2},{4,5},{5,4},{6,7},{7,6},{8,9},{9,8},{10,11... | collective-permute-start | bytes 393224 | tf_op jit(solution)/shard_map/ppermute | solution.py:49
  35.4 5.5 %collective-permute-start.14 = (bf16[4,64,256]{2,1,0:T(8,128)(2,1)S(1)}, bf16[4,64,256]{2,1,0:T(8,128)(2,1)S(1)}, u32[]{:S(2)}, u32[]{:S(2)}) collective-permute-start(bf16[4,64,256]{2,1,0:T(8,128)(2,1)S(1)} %constant_dynamic-update-slice_fusion.2.refs_0_), channel_id=1, source_target_pairs={{0,1},{1,0},{2,3},{3,2},{4,5},{5,4},{6,7},{7,6},{8,9},{9,8},{10,11... | collective-permute-start | bytes 393224 | tf_op jit(solution)/shard_map/ppermute | solution.py:49
  35.8 5.1 %collective-permute-start.17 = (bf16[4,64,256]{2,1,0:T(8,128)(2,1)S(1)}, bf16[4,64,256]{2,1,0:T(8,128)(2,1)S(1)}, u32[]{:S(2)}, u32[]{:S(2)}) collective-permute-start(bf16[4,64,256]{2,1,0:T(8,128)(2,1)S(1)} %collective-permute-done.13.refs_3_), channel_id=1, source_target_pairs={{0,1},{1,0},{2,3},{3,2},{4,5},{5,4},{6,7},{7,6},{8,9},{9,8},{10,11... | collective-permute-start | bytes 393224 | tf_op jit(solution)/shard_map/ppermute | solution.py:49
  35.9 5.0 %collective-permute-start.16 = (bf16[4,64,256]{2,1,0:T(8,128)(2,1)S(1)}, bf16[4,64,256]{2,1,0:T(8,128)(2,1)S(1)}, u32[]{:S(2)}, u32[]{:S(2)}) collective-permute-start(bf16[4,64,256]{2,1,0:T(8,128)(2,1)S(1)} %collective-permute-done.12.refs_2_), channel_id=1, source_target_pairs={{0,1},{1,0},{2,3},{3,2},{4,5},{5,4},{6,7},{7,6},{8,9},{9,8},{10,11... | collective-permute-start | bytes 393224 | tf_op jit(solution)/shard_map/ppermute | solution.py:49
  36.3 4.6 %collective-permute-start.15 = (bf16[4,64,256]{2,1,0:T(8,128)(2,1)S(1)}, bf16[4,64,256]{2,1,0:T(8,128)(2,1)S(1)}, u32[]{:S(2)}, u32[]{:S(2)}) collective-permute-start(bf16[4,64,256]{2,1,0:T(8,128)(2,1)S(1)} %collective-permute-done.11.refs_1_), channel_id=1, source_target_pairs={{0,1},{1,0},{2,3},{3,2},{4,5},{5,4},{6,7},{7,6},{8,9},{9,8},{10,11... | collective-permute-start | bytes 393224 | tf_op jit(solution)/shard_map/ppermute | solution.py:49
  37.3 0.8 %copy-start.3 = (f32[16,512]{1,0:T(8,128)S(1)}, f32[16,512]{1,0:T(8,128)}, u32[]{:S(2)}) copy-start(f32[16,512]{1,0:T(8,128)} %get-tuple-element.17.refs_8_) | copy-start | bytes 98308
  41.9 1.2 %collective-permute-start.19 = (bf16[1,16,128]{2,1,0:T(8,128)(2,1)S(1)}, bf16[1,16,128]{2,1,0:T(8,128)(2,1)S(1)}, u32[]{:S(2)}, u32[]{:S(2)}) collective-permute-start(bf16[1,16,128]{2,1,0:T(8,128)(2,1)S(1)} %get-tuple-element.26), channel_id=1, source_target_pairs={{0,1},{1,0},{2,3},{3,2},{4,5},{5,4},{6,7},{7,6},{8,9},{9,8},{10,11... | collective-permute-start | bytes 12296 | tf_op jit(solution)/shard_map/ppermute | solution.py:49
  42.2 1.4 %collective-permute-start.18 = (bf16[16,3,16,128]{3,2,1,0:T(8,128)(2,1)S(1)}, bf16[16,3,16,128]{3,2,1,0:T(8,128)(2,1)S(1)}, u32[]{:S(2)}, u32[]{:S(2)}) collective-permute-start(bf16[16,3,16,128]{3,2,1,0:T(8,128)(2,1)S(1)} %get-tuple-element.24), channel_id=1, source_target_pairs={{0,1},{1,0},{2,3},{3,2},{4,5},{5,4},{6,7},{7,6},{8,9},{9,8},{10,11... | collective-permute-start | bytes 589832 | tf_op jit(solution)/shard_map/ppermute | solution.py:49
  43.7 27.3 %copy-start.4 = (bf16[64,192]{1,0:T(8,128)(2,1)S(1)}, bf16[64,192]{1,0:T(8,128)(2,1)}, u32[]{:S(2)}) copy-start(bf16[64,192]{1,0:T(8,128)(2,1)} %get-tuple-element.28.own_proj) | copy-start | bytes 73732
  43.8 4.6 %collective-permute-start.20 = (bf16[13,16,128]{2,1,0:T(8,128)(2,1)S(1)}, bf16[13,16,128]{2,1,0:T(8,128)(2,1)S(1)}, u32[]{:S(2)}, u32[]{:S(2)}) collective-permute-start(bf16[13,16,128]{2,1,0:T(8,128)(2,1)S(1)} %get-tuple-element.37), channel_id=1, source_target_pairs={{0,32},{1,33},{2,34},{3,35},{4,36},{5,37},{6,38},{7,39},{8,40},{9,... | collective-permute-start | bytes 159752 | tf_op jit(solution)/shard_map/ppermute | solution.py:49
  46.9 4.1 %collective-permute-start.21 = (bf16[13,16,128]{2,1,0:T(8,128)(2,1)S(1)}, bf16[13,16,128]{2,1,0:T(8,128)(2,1)S(1)}, u32[]{:S(2)}, u32[]{:S(2)}) collective-permute-start(bf16[13,16,128]{2,1,0:T(8,128)(2,1)S(1)} %get-tuple-element.38), channel_id=1, source_target_pairs={{0,17},{1,16},{2,19},{3,18},{4,21},{5,20},{6,23},{7,22},{8,25},{9,... | collective-permute-start | bytes 159752 | tf_op jit(solution)/shard_map/ppermute | solution.py:49
  47.7 4.8 %collective-permute-start.22 = (bf16[13,16,128]{2,1,0:T(8,128)(2,1)S(1)}, bf16[13,16,128]{2,1,0:T(8,128)(2,1)S(1)}, u32[]{:S(2)}, u32[]{:S(2)}) collective-permute-start(bf16[13,16,128]{2,1,0:T(8,128)(2,1)S(1)} %get-tuple-element.39), channel_id=1, source_target_pairs={{0,49},{1,48},{2,51},{3,50},{4,53},{5,52},{6,55},{7,54},{8,57},{9,... | collective-permute-start | bytes 159752 | tf_op jit(solution)/shard_map/ppermute | solution.py:49
  62.0 2.3 %collective-permute-start.23 = (bf16[4,16,128]{2,1,0:T(8,128)(2,1)S(1)}, bf16[4,16,128]{2,1,0:T(8,128)(2,1)S(1)}, u32[]{:S(2)}, u32[]{:S(2)}) collective-permute-start(bf16[4,16,128]{2,1,0:T(8,128)(2,1)S(1)} %reduce_sum.12), channel_id=1, source_target_pairs={{0,1},{1,0},{2,3},{3,2},{4,5},{5,4},{6,7},{7,6},{8,9},{9,8},{10,11... | collective-permute-start | bytes 49160 | tf_op jit(solution)/shard_map/ppermute | solution.py:49
  64.4 5.8 %collective-permute-start.25 = (bf16[4,32,128]{2,1,0:T(8,128)(2,1)S(1)}, bf16[4,32,128]{2,1,0:T(8,128)(2,1)S(1)}, u32[]{:S(2)}, u32[]{:S(2)}) collective-permute-start(bf16[4,32,128]{2,1,0:T(8,128)(2,1)S(1)} %pad_maximum_fusion.5), channel_id=1, source_target_pairs={{0,5},{1,4},{2,7},{3,6},{4,1},{5,0},{6,3},{7,2},{8,13},{9,12},{10,... | collective-permute-start | bytes 98312 | tf_op jit(solution)/shard_map/ppermute | solution.py:49
  66.4 3.7 %collective-permute-start.24 = (bf16[4,32,128]{2,1,0:T(8,128)(2,1)S(1)}, bf16[4,32,128]{2,1,0:T(8,128)(2,1)S(1)}, u32[]{:S(2)}, u32[]{:S(2)}) collective-permute-start(bf16[4,32,128]{2,1,0:T(8,128)(2,1)S(1)} %pad_maximum_fusion.5), channel_id=1, source_target_pairs={{0,3},{1,2},{2,1},{3,0},{4,7},{5,6},{6,5},{7,4},{8,11},{9,10},{10,... | collective-permute-start | bytes 98312 | tf_op jit(solution)/shard_map/ppermute | solution.py:49
  66.5 4.6 %collective-permute-start.26 = (bf16[4,32,128]{2,1,0:T(8,128)(2,1)S(1)}, bf16[4,32,128]{2,1,0:T(8,128)(2,1)S(1)}, u32[]{:S(2)}, u32[]{:S(2)}) collective-permute-start(bf16[4,32,128]{2,1,0:T(8,128)(2,1)S(1)} %pad_maximum_fusion.5), channel_id=1, source_target_pairs={{0,7},{1,6},{2,5},{3,4},{4,3},{5,2},{6,1},{7,0},{8,15},{9,14},{10,... | collective-permute-start | bytes 98312 | tf_op jit(solution)/shard_map/ppermute | solution.py:49

commit v4 on v3

--- a/solution.py
+++ b/solution.py
@@ -160,8 +160,8 @@
     latent = dot(y_ref[...], proj_t[...], 1, 1).astype(BF)
     crops = jnp.zeros((n, 256), F32)
     for i in range(4):
-        wide = dot(latent, shifted(CH, 256, CH * i), 1, 0).astype(BF)
-        crops += dot(picks[i], wide, 1, 0)
+        piece = dot(picks[i], latent, 1, 0).astype(BF)
+        crops += dot(piece, shifted(CH, 256, CH * i), 1, 0)
     crops = crops.astype(BF)
     arrived(copies[feature_w])
     pre = dot(crops[ROWS:n, 0:CH], w_feature[GROUPS * 256 : CROP, :], 1, 0)
@@ -233,7 +233,7 @@
             maps[:, spot] = tiles[t]
         spot = pl.ds(pl.multiple_of(p * PAIR, 128), PAIR)
         total += dot(x_ref[:, spot], maps[:, spot], 1, 1)
-    part = dot(latent[...], dot(total.astype(BF), shifted(RANK, 128, 0), 1, 0).astype(BF), 0, 0)
+    part = dot(latent[...], dot(total.astype(BF), shifted(RANK, 128, 0), 1, 0).astype(BF), 1, 0)
     lane = lax.broadcasted_iota(jnp.int32, (KH, 128), 1)
     unit = jnp.where(lane < 64, part[0:KH], pltpu.roll(part[KH : 2 * KH], 64, 1)).astype(BF)
     top, bottom = unit[0 : KH // 2], unit[KH // 2 : KH]
@@ -266,9 +266,10 @@
     face_ref, w_embed, w_feature, x_ref, keep, give, latent_ref = refs[8:]
     d = lax.axis_index("dp")
     half = parity(lax.axis_index("fsdp"), d)
-    slot = lax.broadcasted_iota(jnp.int32, (8, 16), 0)
-    lane = lax.broadcasted_iota(jnp.int32, (8, 16), 1)
-    refer = jnp.zeros((8, EMB), F32)
+    slot = lax.broadcasted_iota(jnp.int32, (8, 16 * MAXF), 0)
+    lane = lax.broadcasted_iota(jnp.int32, (8, 16 * MAXF), 1)
+    live = jnp.zeros(slot.shape, jnp.bool_)
+    chunks = []
     for k_slot in range(MAXF):
         who = ident[0, k_slot]
         apart = (who >> 6) ^ d
@@ -280,8 +281,10 @@
         found = jnp.zeros((16, EMB), BF)
         for k in range(4):
             found = jnp.where(dx == k, jnp.where(here, near[k][at, :], far[k][at, :]), found)
-        live = (slot == k_slot) & (lane == (spot & 15)) & (k_slot < count[0])
-        refer += dot(live.astype(BF), found, 1, 0)
+        hit = (slot == k_slot) & (lane == 16 * k_slot + (spot & 15))
+        live = live | (hit & (k_slot < count[0]))
+        chunks.append(found)
+    refer = dot(live.astype(BF), jnp.concatenate(chunks, axis=0), 1, 0)
     emb = face_ref[8:16]
     norm_e = jnp.sqrt(jnp.sum(emb * emb, axis=-1, keepdims=True) + eps_norm)
     norm_r = jnp.sqrt(jnp.sum(refer * refer, axis=-1, keepdims=True) + eps_norm)
@@ -290,26 +293,26 @@
         loss_scale * (refer / (norm_e * norm_r) - cosine * emb / (norm_e * norm_e))
     ).astype(BF)
     d_feature = dot(d_embed, w_embed[...], 1, 1)
-    d_pre = (d_feature * gelu_slope(face_ref[0:8])).astype(BF)
+    d_pre = (d_feature * face_ref[0:8]).astype(BF)
     parts = [
         dot(d_pre, w_feature[256 * g : 256 * g + 256, :], 1, 1) for g in range(GROUPS)
     ]
     d_crop = jnp.concatenate(parts, axis=0).astype(BF)
     last = dot(d_pre, w_feature[GROUPS * 256 : CROP, :], 1, 1).astype(BF)
-    index = lax.broadcasted_iota(jnp.int32, (TOK, ROWS), 1)
-    token = lax.broadcasted_iota(jnp.int32, (TOK, ROWS), 0)
-    tail = lax.broadcasted_iota(jnp.int32, (TOK, 8), 1) + ROWS
-    pick = (token_of(rows, cols, tail, 0) == token[:, 0:8]).astype(BF)
-    d_latent = dot(pick, last, 1, 0)
+    index = lax.broadcasted_iota(jnp.int32, (ROWS, TOK), 0)
+    token = lax.broadcasted_iota(jnp.int32, (ROWS, TOK), 1)
+    tail = index[0:8] + ROWS
+    pick = (token_of(rows, cols, tail, 0) == token[0:8]).astype(BF)
+    d_latent = dot(last, pick, 0, 0)
     for i in range(4):
         pick = (token_of(rows, cols, index, i) == token).astype(BF)
-        piece = dot(d_crop, shifted(CH, 256, CH * i), 1, 1).astype(BF)
-        d_latent += dot(pick, piece, 1, 0)
+        piece = dot(shifted(CH, 256, CH * i), d_crop, 1, 1).astype(BF)
+        d_latent += dot(piece, pick, 1, 0)
     d_latent = d_latent.astype(BF)
     latent_ref[...] = d_latent
     lane = lax.broadcasted_iota(jnp.int32, (KH, 128), 1)
     for p in range(8):
-        part = dot(d_latent, x_ref[:, p * PAIR : p * PAIR + PAIR], 0, 0)
+        part = dot(d_latent, x_ref[:, p * PAIR : p * PAIR + PAIR], 1, 0)
         for u in range(6):
             top = part[0:KH, 128 * (u // 2) : 128 * (u // 2) + 128]
             bottom = part[KH : 2 * KH, 128 * (u // 2) : 128 * (u // 2) + 128]
@@ -331,7 +334,7 @@
     shares = jax.ShapeDtypeStruct((16, 3, KH // 2, 128), BF)
     return pl.pallas_call(
         main_kernel,
-        out_shape=(shares, shares, jax.ShapeDtypeStruct((TOK, CH), BF)),
+        out_shape=(shares, shares, jax.ShapeDtypeStruct((CH, TOK), BF)),
         in_specs=[SMEM] * 4 + vmem(12),
         out_specs=tuple(vmem(3)),
         compiler_params=params(24),
@@ -351,7 +354,7 @@
     cross_ref[...] = dot(total.astype(BF), shifted(CH, 128, 64), 1, 1).astype(BF)
     stack[CH : CH + RANK, :] = maps[...]
     widen = shifted(CH, 128, 0).astype(F32) + dot(cross_ref[...], shifted(RANK, 128, CH), 1, 0)
-    wide = dot(latent[...], widen.astype(BF), 1, 0).astype(BF)
+    wide = dot(latent[...], widen.astype(BF), 0, 0).astype(BF)
     copies = []
     for i in range(D // BLOCK):
         slab[i] = dot(wide, stack[:, BLOCK * i : BLOCK * i + BLOCK], 1, 0).astype(BF)
@@ -423,9 +426,10 @@
     return sum(t.astype(F32) for t in terms).astype(BF)
 
 
-def fan(value, **axis):
+def fan(value, order, **axis):
     ((name, _),) = axis.items()
-    return [send(value, flip(**{name: k, "c": 1})) for k in (1, 2, 3)]
+    parts = {k: send(value, flip(**{name: k, "c": 1})) for k in order}
+    return [parts[k] for k in (1, 2, 3)]
 
 
 def parity(f, d):
@@ -473,7 +477,7 @@
     v = exchange(v, members(lambda zl, y, zh, x, c: (y, x, c ^ (zl & 1))))
     other = send(v, flip(c=1))
     v = jnp.concatenate([jnp.where(half == 0, v, other), jnp.where(half == 0, other, v)], axis=1)
-    return add(v, *fan(v, x=0))
+    return add(v, *fan(v, (1, 2, 3), x=0))
 
 
 def local(
@@ -500,10 +504,13 @@
         block_out, w_feature, w_embed,
     )
     maps = after(maps, table)
-    tables = fan(table, x=0)
-    maps = jnp.concatenate([maps] + fan(maps, zl=0))
+    tables = fan(table, (1, 2, 3), x=0)
+    maps = jnp.concatenate([maps] + fan(maps, (1, 2, 3), zl=0))
     tables = [table] + tables
-    blocks = [maps] + fan(maps, y=0)
+    blocks = [maps] + fan(maps, (1, 2, 3), y=0)
+    faces = after(faces, maps)
+    upper = lax.broadcasted_iota(jnp.int32, faces.shape, 0) < 8
+    faces = jnp.where(upper, gelu_slope(faces), faces)
     tables += [send(part, flip(c=1)) for part in tables]
     blocks += [send(part, flip(c=1)) for part in blocks]
     keep, give, d_latent = main(

time: 72.3 us -> 71.6 us (level)
  other arithmetic: 0.19 us -> 1.02 us
  local copies, waits for them, and re-layouts: 1.66 us -> 0.91 us
    select_n x0 -> x1, other arithmetic: none -> 0.83 us  [local(): faces = jnp.where(upper, gelu_slope(faces), faces)]
    unnamed x22 -> x20, local copies, waits for them, and re-layouts: 1.59 us -> 0.84 us
  transfers between devices with their start and end apart: 27 -> 27, of which waited for: 10 -> 10; matrix products, arithmetic and copies ran while one was open for 1% -> 2% of each run, Pallas kernels for 16% -> 16%
where the time goes in v4:
time: 71.6 us; the launch traced here: 71.4 us
  starting transfers between devices  34.4 us (48%)
  Pallas kernels  13.4 us (19%)
  waiting for transfers between devices  10.6 us (15%)
  blocking collectives  9.42 us (13%)
  between operations  1.58 us (2%)
  other arithmetic  1.02 us (1%)
  local copies, waits for them, and re-layouts  0.91 us (1%)
    ppermute x27, starting transfers between devices, send(): return lax.ppermute(value, AXES, perm)  34.4 us
    ppermute x27, waiting for transfers between devices, send(): return lax.ppermute(value, AXES, perm)  10.6 us
    all_to_all x1, blocking collectives, exchange(): v = lax.all_to_all(v, AXES, 0, 0, axis_index_groups=groups, tiled=True)  9.42 us
    pallas_call x1, Pallas kernels, front(): pl.pallas_call(front_kernel, out_shape=(jax.ShapeDtypeStruct((1, CH, 256)...  6.87 us
    pallas_call x1, Pallas kernels, main(): pl.pallas_call(main_kernel, out_shape=(shares, shares, jax.ShapeDtypeStru...  2.66 us
    pallas_call x1, Pallas kernels, through(): pl.pallas_call(through_kernel, out_shape=(jax.ShapeDtypeStruct((TOK, D),...  1.82 us
  transfers between devices with their start and end apart: 27, of which 10 were waited for; matrix products, arithmetic and copies ran while one was open for 2% of the time, Pallas kernels for 16%

profile of v4, /device:TPU:1, one launch (start us, length us, event | category | flops | bytes accessed | tf_op | source)
XLA Modules:
  0.0 71.4 jit_solution(17948257725158134796)
XLA Ops:
  0.6 7.5 %collective-permute-start = (bf16[64,512]{1,0:T(8,128)(2,1)}, bf16[64,512]{1,0:T(8,128)(2,1)S(1)}, u32[]{:S(2)}, u32[]{:S(2)}) collective-permute-start(bf16[64,512]{1,0:T(8,128)(2,1)} %param.21), channel_id=1, source_target_pairs={{0,137},{1,136},{2,139},{3,138},{4,141},{5,140},{6,143},{7,142},{8... | collective-permute-start | bytes 196616 | tf_op jit(solution)/shard_map/ppermute | solution.py:49
  8.2 6.9 %front.1 = (bf16[1,64,256]{2,1,0:T(8,128)(2,1)}, bf16[64,192]{1,0:T(8,128)(2,1)}, f32[16,512]{1,0:T(8,128)}) custom-call(s32[1,6]{1,0:T(1,128)} %rows.3, s32[1,6]{1,0:T(1,128)} %cols.3, bf16[64,3072]{1,0:T(8,128)(2,1)} %bitcast.18, bf16[192,3072]{1,0:T(8,128)(2,1)} %weight_hbm.1, bf16[64,192]{1,0:T(8,128)(2,1)} %bitcast.20, bf16[64,192]{1,0:T(8,128)(2,1)} %b_hbm.1, ...), custom_call_target="tpu_custom_call" | custom-call | flops 4 | bytes 4 | tf_op jit(solution)/shard_map/front/pallas_call | solution.py:177
  15.1 0.0 collective-permute-done
  15.1 1.2 %collective-permute-start.10 = (bf16[1,64,256]{2,1,0:T(8,128)(2,1)}, bf16[1,64,256]{2,1,0:T(8,128)(2,1)S(1)}, u32[]{:S(2)}, u32[]{:S(2)}) collective-permute-start(bf16[1,64,256]{2,1,0:T(8,128)(2,1)} %get-tuple-element.20), channel_id=1, source_target_pairs={{0,193},{1,192},{2,195},{3,194},{4,197},{5,196},{6,199},{7,198},{8... | collective-permute-start | bytes 98312 | tf_op jit(solution)/shard_map/ppermute | solution.py:49
  16.3 1.0 %collective-permute-start.9 = (bf16[1,64,256]{2,1,0:T(8,128)(2,1)}, bf16[1,64,256]{2,1,0:T(8,128)(2,1)S(1)}, u32[]{:S(2)}, u32[]{:S(2)}) collective-permute-start(bf16[1,64,256]{2,1,0:T(8,128)(2,1)} %get-tuple-element.20), channel_id=1, source_target_pairs={{0,129},{1,128},{2,131},{3,130},{4,133},{5,132},{6,135},{7,134},{8... | collective-permute-start | bytes 98312 | tf_op jit(solution)/shard_map/ppermute | solution.py:49
  17.4 1.2 %collective-permute-start.8 = (bf16[1,64,256]{2,1,0:T(8,128)(2,1)}, bf16[1,64,256]{2,1,0:T(8,128)(2,1)S(1)}, u32[]{:S(2)}, u32[]{:S(2)}) collective-permute-start(bf16[1,64,256]{2,1,0:T(8,128)(2,1)} %get-tuple-element.20), channel_id=1, source_target_pairs={{0,65},{1,64},{2,67},{3,66},{4,69},{5,68},{6,71},{7,70},{8,73},{9,... | collective-permute-start | bytes 98312 | tf_op jit(solution)/shard_map/ppermute | solution.py:49
  18.5 0.8 %constant_dynamic-update-slice_fusion.5 = bf16[4,64,256]{2,1,0:T(8,128)(2,1)S(1)} fusion(bf16[1,64,256]{2,1,0:T(8,128)(2,1)} %get-tuple-element.20), kind=kLoop, calls=%fused_computation.33 | loop fusion | bytes 65536
  19.3 0.9 %collective-permute-start.4 = (bf16[128,512]{1,0:T(8,128)(2,1)S(1)}, bf16[128,512]{1,0:T(8,128)(2,1)S(1)}, u32[]{:S(2)}, u32[]{:S(2)}) collective-permute-start(bf16[128,512]{1,0:T(8,128)(2,1)S(1)} %constant_dynamic-update-slice_fusion.refs_0_), channel_id=1, source_target_pairs={{0,1},{1,0},{2,3},{3,2},{4,5},{5,4},{6,7},{7,6},{8,9},{9,8},{10,11... | collective-permute-start | bytes 393224 | tf_op jit(solution)/shard_map/ppermute | solution.py:49
  20.2 2.4 %collective-permute-start.3 = (bf16[128,512]{1,0:T(8,128)(2,1)S(1)}, bf16[128,512]{1,0:T(8,128)(2,1)S(1)}, u32[]{:S(2)}, u32[]{:S(2)}) collective-permute-start(bf16[128,512]{1,0:T(8,128)(2,1)S(1)} %constant_dynamic-update-slice_fusion.refs_0_), channel_id=1, source_target_pairs={{0,7},{1,6},{2,5},{3,4},{4,3},{5,2},{6,1},{7,0},{8,15},{9,14},{10,... | collective-permute-start | bytes 393224 | tf_op jit(solution)/shard_map/ppermute | solution.py:49
  22.6 1.8 %collective-permute-start.2 = (bf16[128,512]{1,0:T(8,128)(2,1)S(1)}, bf16[128,512]{1,0:T(8,128)(2,1)S(1)}, u32[]{:S(2)}, u32[]{:S(2)}) collective-permute-start(bf16[128,512]{1,0:T(8,128)(2,1)S(1)} %constant_dynamic-update-slice_fusion.refs_0_), channel_id=1, source_target_pairs={{0,5},{1,4},{2,7},{3,6},{4,1},{5,0},{6,3},{7,2},{8,13},{9,12},{10,... | collective-permute-start | bytes 393224 | tf_op jit(solution)/shard_map/ppermute | solution.py:49
  24.4 0.0 collective-permute-done.9
  24.4 0.8 %collective-permute-start.1 = (bf16[128,512]{1,0:T(8,128)(2,1)S(1)}, bf16[128,512]{1,0:T(8,128)(2,1)S(1)}, u32[]{:S(2)}, u32[]{:S(2)}) collective-permute-start(bf16[128,512]{1,0:T(8,128)(2,1)S(1)} %constant_dynamic-update-slice_fusion.refs_0_), channel_id=1, source_target_pairs={{0,3},{1,2},{2,1},{3,0},{4,7},{5,6},{6,5},{7,4},{8,11},{9,10},{10,... | collective-permute-start | bytes 393224 | tf_op jit(solution)/shard_map/ppermute | solution.py:49
  25.2 2.6 %collective-permute-start.13 = (bf16[4,64,256]{2,1,0:T(8,128)(2,1)S(1)}, bf16[4,64,256]{2,1,0:T(8,128)(2,1)S(1)}, u32[]{:S(2)}, u32[]{:S(2)}) collective-permute-start(bf16[4,64,256]{2,1,0:T(8,128)(2,1)S(1)} %constant_dynamic-update-slice_fusion.2.refs_0_), channel_id=1, source_target_pairs={{0,49},{1,48},{2,51},{3,50},{4,53},{5,52},{6,55},{7,54},{8,57},{9,... | collective-permute-start | bytes 393224 | tf_op jit(solution)/shard_map/ppermute | solution.py:49
  27.8 0.9 %collective-permute-start.12 = (bf16[4,64,256]{2,1,0:T(8,128)(2,1)S(1)}, bf16[4,64,256]{2,1,0:T(8,128)(2,1)S(1)}, u32[]{:S(2)}, u32[]{:S(2)}) collective-permute-start(bf16[4,64,256]{2,1,0:T(8,128)(2,1)S(1)} %constant_dynamic-update-slice_fusion.2.refs_0_), channel_id=1, source_target_pairs={{0,33},{1,32},{2,35},{3,34},{4,37},{5,36},{6,39},{7,38},{8,41},{9,... | collective-permute-start | bytes 393224 | tf_op jit(solution)/shard_map/ppermute | solution.py:49
  28.7 1.5 %collective-permute-start.11 = (bf16[4,64,256]{2,1,0:T(8,128)(2,1)S(1)}, bf16[4,64,256]{2,1,0:T(8,128)(2,1)S(1)}, u32[]{:S(2)}, u32[]{:S(2)}) collective-permute-start(bf16[4,64,256]{2,1,0:T(8,128)(2,1)S(1)} %constant_dynamic-update-slice_fusion.2.refs_0_), channel_id=1, source_target_pairs={{0,17},{1,16},{2,19},{3,18},{4,21},{5,20},{6,23},{7,22},{8,25},{9,... | collective-permute-start | bytes 393224 | tf_op jit(solution)/shard_map/ppermute | solution.py:49
  30.2 1.4 %collective-permute-done.1.refs_1_ = bf16[128,512]{1,0:T(8,128)(2,1)S(1)} collective-permute-done((bf16[128,512]{1,0:T(8,128)(2,1)S(1)}, bf16[128,512]{1,0:T(8,128)(2,1)S(1)}, u32[]{:S(2)}, u32[]{:S(2)}) %collective-permute-start.1) | collective-permute-done | bytes 131104 | tf_op jit(solution)/shard_map/ppermute | solution.py:49
  31.6 0.0 collective-permute-start.6
  32.3 0.7 %collective-permute-done.13.refs_3_ = bf16[4,64,256]{2,1,0:T(8,128)(2,1)S(1)} collective-permute-done((bf16[4,64,256]{2,1,0:T(8,128)(2,1)S(1)}, bf16[4,64,256]{2,1,0:T(8,128)(2,1)S(1)}, u32[]{:S(2)}, u32[]{:S(2)}) %collective-permute-start.13) | collective-permute-done | bytes 131104 | tf_op jit(solution)/shard_map/ppermute | solution.py:49
  33.0 1.3 %collective-permute-start.14 = (bf16[4,64,256]{2,1,0:T(8,128)(2,1)S(1)}, bf16[4,64,256]{2,1,0:T(8,128)(2,1)S(1)}, u32[]{:S(2)}, u32[]{:S(2)}) collective-permute-start(bf16[4,64,256]{2,1,0:T(8,128)(2,1)S(1)} %constant_dynamic-update-slice_fusion.2.refs_0_), channel_id=1, source_target_pairs={{0,1},{1,0},{2,3},{3,2},{4,5},{5,4},{6,7},{7,6},{8,9},{9,8},{10,11... | collective-permute-start | bytes 393224 | tf_op jit(solution)/shard_map/ppermute | solution.py:49
  34.4 1.0 %collective-permute-done.12.refs_2_ = bf16[4,64,256]{2,1,0:T(8,128)(2,1)S(1)} collective-permute-done((bf16[4,64,256]{2,1,0:T(8,128)(2,1)S(1)}, bf16[4,64,256]{2,1,0:T(8,128)(2,1)S(1)}, u32[]{:S(2)}, u32[]{:S(2)}) %collective-permute-start.12) | collective-permute-done | bytes 131104 | tf_op jit(solution)/shard_map/ppermute | solution.py:49
  35.4 0.4 collective-permute-start.5
  35.8 0.1 collective-permute-start.17
  35.9 0.4 collective-permute-start.16
  36.3 0.3 collective-permute-start.15
  36.6 0.8 %fusion.10.refs_8_ = f32[16,512]{1,0:T(8,128)S(1)} fusion(f32[16,512]{1,0:T(8,128)} %get-tuple-element.21, pred[16]{0:T(512)(128)(4,1)S(1)} %iota_compare_fusion), kind=kLoop, calls=%fused_computation.24 | loop fusion | flops 139264 | bytes 65552 | tf_op jit(solution)/shard_map/jit(_where)/select_n | solution.py:513
  37.5 2.7 %main.1 = (bf16[16,3,16,128]{3,2,1,0:T(8,128)(2,1)S(1)}, bf16[16,3,16,128]{3,2,1,0:T(8,128)(2,1)S(1)}, bf16[64,256]{1,0:T(8,128)(2,1)S(1)}) custom-call(s32[1,6]{1,0:T(1,128)S(1)} %copy-done.4, s32[1,6]{1,0:T(1,128)S(1)} %copy-done.5, s32[1,6]{1,0:T(1,128)S(1)} %copy-done.6, s32[1]{0:T(128)S(6)} %copy.20.count, ...), custom_call_target="tpu_custom_call" | custom-call | flops 3 | bytes 3 | tf_op jit(solution)/shard_map/main/pallas_call | solution.py:335
  40.2 1.0 %low.1 = (bf16[64,3072]{1,0:T(8,128)(2,1)S(1)}, bf16[1,16,128]{2,1,0:T(8,128)(2,1)S(1)}, bf16[1,16,128]{2,1,0:T(8,128)(2,1)S(1)}) custom-call(bf16[256,3072]{1,0:T(8,128)(2,1)S(1)} %copy-done.1, bf16[64,256]{1,0:T(8,128)(2,1)S(1)} %get-tuple-element.22.latent, bf16[4,64,256]{2,1,0:T(8,128)(2,1)S(1)} %constant_dynamic-update-slice_fusion.2.refs_0_, ...), custom_call_target="tpu_custom_call" | custom-call | flops 2 | bytes 2 | tf_op jit(solution)/shard_map/low/pallas_call | solution.py:247
  41.2 0.3 collective-permute-start.19
  41.5 0.3 collective-permute-start.18
  41.7 0.7 collective-permute-done.19
  42.4 0.5 collective-permute-done.18
  42.9 0.1 add_convert_fusion
  43.0 0.0 copy-start.3
  43.0 3.1 %collective-permute-start.20 = (bf16[13,16,128]{2,1,0:T(8,128)(2,1)S(1)}, bf16[13,16,128]{2,1,0:T(8,128)(2,1)S(1)}, u32[]{:S(2)}, u32[]{:S(2)}) collective-permute-start(bf16[13,16,128]{2,1,0:T(8,128)(2,1)S(1)} %get-tuple-element.39), channel_id=1, source_target_pairs={{0,32},{1,33},{2,34},{3,35},{4,36},{5,37},{6,38},{7,39},{8,40},{9,... | collective-permute-start | bytes 159752 | tf_op jit(solution)/shard_map/ppermute | solution.py:49
  46.2 0.8 %collective-permute-start.21 = (bf16[13,16,128]{2,1,0:T(8,128)(2,1)S(1)}, bf16[13,16,128]{2,1,0:T(8,128)(2,1)S(1)}, u32[]{:S(2)}, u32[]{:S(2)}) collective-permute-start(bf16[13,16,128]{2,1,0:T(8,128)(2,1)S(1)} %get-tuple-element.40), channel_id=1, source_target_pairs={{0,17},{1,16},{2,19},{3,18},{4,21},{5,20},{6,23},{7,22},{8,25},{9,... | collective-permute-start | bytes 159752 | tf_op jit(solution)/shard_map/ppermute | solution.py:49
  47.0 0.2 collective-permute-start.22
  47.2 0.5 collective-permute-done.20
  47.7 2.6 %collective-permute-done.21 = bf16[13,16,128]{2,1,0:T(8,128)(2,1)S(1)} collective-permute-done((bf16[13,16,128]{2,1,0:T(8,128)(2,1)S(1)}, bf16[13,16,128]{2,1,0:T(8,128)(2,1)S(1)}, u32[]{:S(2)}, u32[]{:S(2)}) %collective-permute-start.21) | collective-permute-done | bytes 53280 | tf_op jit(solution)/shard_map/ppermute | solution.py:49
  50.2 1.5 %collective-permute-done.22 = bf16[13,16,128]{2,1,0:T(8,128)(2,1)S(1)} collective-permute-done((bf16[13,16,128]{2,1,0:T(8,128)(2,1)S(1)}, bf16[13,16,128]{2,1,0:T(8,128)(2,1)S(1)}, u32[]{:S(2)}, u32[]{:S(2)}) %collective-permute-start.22) | collective-permute-done | bytes 53280 | tf_op jit(solution)/shard_map/ppermute | solution.py:49
  51.9 9.4 %all_to_all.5 = bf16[8,4,16,128]{3,2,1,0:T(8,128)(2,1)S(1)} all-to-all(bf16[8,4,16,128]{3,2,1,0:T(8,128)(2,1)S(1)} %bitcast.17), channel_id=1, replica_groups={{0,8,65,73,128,136,193,201},{1,9,64,72,129,137,192,200},{2,10,67,75,130..., dimensions={0} | all-to-all | bytes 262144 | tf_op jit(solution)/shard_map/all_to_all | solution.py:440
  61.3 1.5 %collective-permute-start.23 = (bf16[4,16,128]{2,1,0:T(8,128)(2,1)S(1)}, bf16[4,16,128]{2,1,0:T(8,128)(2,1)S(1)}, u32[]{:S(2)}, u32[]{:S(2)}) collective-permute-start(bf16[4,16,128]{2,1,0:T(8,128)(2,1)S(1)} %reduce_sum.12), channel_id=1, source_target_pairs={{0,1},{1,0},{2,3},{3,2},{4,5},{5,4},{6,7},{7,6},{8,9},{9,8},{10,11... | collective-permute-start | bytes 49160 | tf_op jit(solution)/shard_map/ppermute | solution.py:49
  62.8 0.8 %collective-permute-done.23 = bf16[4,16,128]{2,1,0:T(8,128)(2,1)S(1)} collective-permute-done((bf16[4,16,128]{2,1,0:T(8,128)(2,1)S(1)}, bf16[4,16,128]{2,1,0:T(8,128)(2,1)S(1)}, u32[]{:S(2)}, u32[]{:S(2)}) %collective-permute-start.23) | collective-permute-done | bytes 16416 | tf_op jit(solution)/shard_map/ppermute | solution.py:49
  63.6 2.0 %collective-permute-start.25 = (bf16[4,32,128]{2,1,0:T(8,128)(2,1)S(1)}, bf16[4,32,128]{2,1,0:T(8,128)(2,1)S(1)}, u32[]{:S(2)}, u32[]{:S(2)}) collective-permute-start(bf16[4,32,128]{2,1,0:T(8,128)(2,1)S(1)} %pad_maximum_fusion.5), channel_id=1, source_target_pairs={{0,5},{1,4},{2,7},{3,6},{4,1},{5,0},{6,3},{7,2},{8,13},{9,12},{10,... | collective-permute-start | bytes 98312 | tf_op jit(solution)/shard_map/ppermute | solution.py:49
  65.7 0.1 collective-permute-start.24
  65.8 1.8 %collective-permute-start.26 = (bf16[4,32,128]{2,1,0:T(8,128)(2,1)S(1)}, bf16[4,32,128]{2,1,0:T(8,128)(2,1)S(1)}, u32[]{:S(2)}, u32[]{:S(2)}) collective-permute-start(bf16[4,32,128]{2,1,0:T(8,128)(2,1)S(1)} %pad_maximum_fusion.5), channel_id=1, source_target_pairs={{0,7},{1,6},{2,5},{3,4},{4,3},{5,2},{6,1},{7,0},{8,15},{9,14},{10,... | collective-permute-start | bytes 98312 | tf_op jit(solution)/shard_map/ppermute | solution.py:49
  67.6 1.8 %through.1 = (bf16[256,3072]{1,0:T(8,128)(2,1)}, bf16[64,64]{1,0:T(8,128)(2,1)S(1)}) custom-call(bf16[64,256]{1,0:T(8,128)(2,1)S(1)} %get-tuple-element.22.latent, bf16[64,3072]{1,0:T(8,128)(2,1)S(1)} %get-tuple-element.23.maps, bf16[4,64,256]{2,1,0:T(8,128)(2,1)S(1)} %constant_dynamic-update-slice_fusion.2.refs_0_, ...), custom_call_target="tpu_custom_call" | custom-call | flops 3 | bytes 3 | tf_op jit(solution)/shard_map/through/pallas_call | solution.py:371
  69.4 0.9 %collective-permute-done.26 = bf16[4,32,128]{2,1,0:T(8,128)(2,1)S(1)} collective-permute-done((bf16[4,32,128]{2,1,0:T(8,128)(2,1)S(1)}, bf16[4,32,128]{2,1,0:T(8,128)(2,1)S(1)}, u32[]{:S(2)}, u32[]{:S(2)}) %collective-permute-start.26) | collective-permute-done | bytes 32800 | tf_op jit(solution)/shard_map/ppermute | solution.py:49
  70.4 1.0 %last.1 = (f32[64,192]{1,0:T(8,128)}, f32[64,192]{1,0:T(8,128)}) custom-call(bf16[4,32,128]{2,1,0:T(8,128)(2,1)S(1)} %add_convert_fusion.2.units, bf16[64,64]{1,0:T(8,128)(2,1)S(1)} %get-tuple-element.29.cross, bf16[64,192]{1,0:T(8,128)(2,1)S(1)} %copy-done.3), custom_call_target="tpu_custom_call" | custom-call | flops 1 | bytes 1 | tf_op jit(solution)/shard_map/last/pallas_call | solution.py:411
  (50 shorter events, 0.3 us)
Async XLA Ops:
  0.6 14.4 %collective-permute-start = (bf16[64,512]{1,0:T(8,128)(2,1)}, bf16[64,512]{1,0:T(8,128)(2,1)S(1)}, u32[]{:S(2)}, u32[]{:S(2)}) collective-permute-start(bf16[64,512]{1,0:T(8,128)(2,1)} %param.21), channel_id=1, source_target_pairs={{0,137},{1,136},{2,139},{3,138},{4,141},{5,140},{6,143},{7,142},{8... | collective-permute-start | bytes 196616 | tf_op jit(solution)/shard_map/ppermute | solution.py:49
  8.1 6.9 %copy-start.7 = (bf16[64,512]{1,0:T(8,128)(2,1)S(1)}, bf16[64,512]{1,0:T(8,128)(2,1)}, u32[]{:S(2)}) copy-start(bf16[64,512]{1,0:T(8,128)(2,1)} %param.21) | copy-start | bytes 196612
  8.1 29.3 %copy-start = (bf16[3136,512]{1,0:T(8,128)(2,1)S(1)}, bf16[3136,512]{1,0:T(8,128)(2,1)}, u32[]{:S(2)}) copy-start(bf16[3136,512]{1,0:T(8,128)(2,1)} %refs_10_.1) | copy-start | bytes 9633796
  8.1 29.3 %copy-start.1 = (bf16[256,3072]{1,0:T(8,128)(2,1)S(1)}, bf16[256,3072]{1,0:T(8,128)(2,1)}, u32[]{:S(2)}) copy-start(bf16[256,3072]{1,0:T(8,128)(2,1)} %x_ref.1) | copy-start | bytes 4718596
  8.1 29.3 %copy-start.2 = (bf16[512,512]{1,0:T(8,128)(2,1)S(1)}, bf16[512,512]{1,0:T(8,128)(2,1)}, u32[]{:S(2)}) copy-start(bf16[512,512]{1,0:T(8,128)(2,1)} %refs_9_.1) | copy-start | bytes 1572868
  8.1 29.3 %copy-start.4 = (s32[1,6]{1,0:T(1,128)S(1)}, s32[1,6]{1,0:T(1,128)}, u32[]{:S(2)}) copy-start(s32[1,6]{1,0:T(1,128)} %rows.3) | copy-start | bytes 76
  8.2 29.3 %copy-start.5 = (s32[1,6]{1,0:T(1,128)S(1)}, s32[1,6]{1,0:T(1,128)}, u32[]{:S(2)}) copy-start(s32[1,6]{1,0:T(1,128)} %cols.3) | copy-start | bytes 76
  8.2 29.3 %copy-start.6 = (s32[1,6]{1,0:T(1,128)S(1)}, s32[1,6]{1,0:T(1,128)}, u32[]{:S(2)}) copy-start(s32[1,6]{1,0:T(1,128)} %ident.1) | copy-start | bytes 76
  15.1 10.1 %collective-permute-start.10 = (bf16[1,64,256]{2,1,0:T(8,128)(2,1)}, bf16[1,64,256]{2,1,0:T(8,128)(2,1)S(1)}, u32[]{:S(2)}, u32[]{:S(2)}) collective-permute-start(bf16[1,64,256]{2,1,0:T(8,128)(2,1)} %get-tuple-element.20), channel_id=1, source_target_pairs={{0,193},{1,192},{2,195},{3,194},{4,197},{5,196},{6,199},{7,198},{8... | collective-permute-start | bytes 98312 | tf_op jit(solution)/shard_map/ppermute | solution.py:49
  16.3 8.1 %collective-permute-start.9 = (bf16[1,64,256]{2,1,0:T(8,128)(2,1)}, bf16[1,64,256]{2,1,0:T(8,128)(2,1)S(1)}, u32[]{:S(2)}, u32[]{:S(2)}) collective-permute-start(bf16[1,64,256]{2,1,0:T(8,128)(2,1)} %get-tuple-element.20), channel_id=1, source_target_pairs={{0,129},{1,128},{2,131},{3,130},{4,133},{5,132},{6,135},{7,134},{8... | collective-permute-start | bytes 98312 | tf_op jit(solution)/shard_map/ppermute | solution.py:49
  17.4 5.2 %collective-permute-start.8 = (bf16[1,64,256]{2,1,0:T(8,128)(2,1)}, bf16[1,64,256]{2,1,0:T(8,128)(2,1)S(1)}, u32[]{:S(2)}, u32[]{:S(2)}) collective-permute-start(bf16[1,64,256]{2,1,0:T(8,128)(2,1)} %get-tuple-element.20), channel_id=1, source_target_pairs={{0,65},{1,64},{2,67},{3,66},{4,69},{5,68},{6,71},{7,70},{8,73},{9,... | collective-permute-start | bytes 98312 | tf_op jit(solution)/shard_map/ppermute | solution.py:49
  19.3 8.5 %collective-permute-start.4 = (bf16[128,512]{1,0:T(8,128)(2,1)S(1)}, bf16[128,512]{1,0:T(8,128)(2,1)S(1)}, u32[]{:S(2)}, u32[]{:S(2)}) collective-permute-start(bf16[128,512]{1,0:T(8,128)(2,1)S(1)} %constant_dynamic-update-slice_fusion.refs_0_), channel_id=1, source_target_pairs={{0,1},{1,0},{2,3},{3,2},{4,5},{5,4},{6,7},{7,6},{8,9},{9,8},{10,11... | collective-permute-start | bytes 393224 | tf_op jit(solution)/shard_map/ppermute | solution.py:49
  20.2 8.5 %collective-permute-start.3 = (bf16[128,512]{1,0:T(8,128)(2,1)S(1)}, bf16[128,512]{1,0:T(8,128)(2,1)S(1)}, u32[]{:S(2)}, u32[]{:S(2)}) collective-permute-start(bf16[128,512]{1,0:T(8,128)(2,1)S(1)} %constant_dynamic-update-slice_fusion.refs_0_), channel_id=1, source_target_pairs={{0,7},{1,6},{2,5},{3,4},{4,3},{5,2},{6,1},{7,0},{8,15},{9,14},{10,... | collective-permute-start | bytes 393224 | tf_op jit(solution)/shard_map/ppermute | solution.py:49
  22.6 7.6 %collective-permute-start.2 = (bf16[128,512]{1,0:T(8,128)(2,1)S(1)}, bf16[128,512]{1,0:T(8,128)(2,1)S(1)}, u32[]{:S(2)}, u32[]{:S(2)}) collective-permute-start(bf16[128,512]{1,0:T(8,128)(2,1)S(1)} %constant_dynamic-update-slice_fusion.refs_0_), channel_id=1, source_target_pairs={{0,5},{1,4},{2,7},{3,6},{4,1},{5,0},{6,3},{7,2},{8,13},{9,12},{10,... | collective-permute-start | bytes 393224 | tf_op jit(solution)/shard_map/ppermute | solution.py:49
  24.4 7.2 %collective-permute-start.1 = (bf16[128,512]{1,0:T(8,128)(2,1)S(1)}, bf16[128,512]{1,0:T(8,128)(2,1)S(1)}, u32[]{:S(2)}, u32[]{:S(2)}) collective-permute-start(bf16[128,512]{1,0:T(8,128)(2,1)S(1)} %constant_dynamic-update-slice_fusion.refs_0_), channel_id=1, source_target_pairs={{0,3},{1,2},{2,1},{3,0},{4,7},{5,6},{6,5},{7,4},{8,11},{9,10},{10,... | collective-permute-start | bytes 393224 | tf_op jit(solution)/shard_map/ppermute | solution.py:49
  25.2 7.8 %collective-permute-start.13 = (bf16[4,64,256]{2,1,0:T(8,128)(2,1)S(1)}, bf16[4,64,256]{2,1,0:T(8,128)(2,1)S(1)}, u32[]{:S(2)}, u32[]{:S(2)}) collective-permute-start(bf16[4,64,256]{2,1,0:T(8,128)(2,1)S(1)} %constant_dynamic-update-slice_fusion.2.refs_0_), channel_id=1, source_target_pairs={{0,49},{1,48},{2,51},{3,50},{4,53},{5,52},{6,55},{7,54},{8,57},{9,... | collective-permute-start | bytes 393224 | tf_op jit(solution)/shard_map/ppermute | solution.py:49
  27.8 7.5 %collective-permute-start.12 = (bf16[4,64,256]{2,1,0:T(8,128)(2,1)S(1)}, bf16[4,64,256]{2,1,0:T(8,128)(2,1)S(1)}, u32[]{:S(2)}, u32[]{:S(2)}) collective-permute-start(bf16[4,64,256]{2,1,0:T(8,128)(2,1)S(1)} %constant_dynamic-update-slice_fusion.2.refs_0_), channel_id=1, source_target_pairs={{0,33},{1,32},{2,35},{3,34},{4,37},{5,36},{6,39},{7,38},{8,41},{9,... | collective-permute-start | bytes 393224 | tf_op jit(solution)/shard_map/ppermute | solution.py:49
  28.7 7.0 %collective-permute-start.11 = (bf16[4,64,256]{2,1,0:T(8,128)(2,1)S(1)}, bf16[4,64,256]{2,1,0:T(8,128)(2,1)S(1)}, u32[]{:S(2)}, u32[]{:S(2)}) collective-permute-start(bf16[4,64,256]{2,1,0:T(8,128)(2,1)S(1)} %constant_dynamic-update-slice_fusion.2.refs_0_), channel_id=1, source_target_pairs={{0,17},{1,16},{2,19},{3,18},{4,21},{5,20},{6,23},{7,22},{8,25},{9,... | collective-permute-start | bytes 393224 | tf_op jit(solution)/shard_map/ppermute | solution.py:49
  30.2 5.7 %collective-permute-start.7 = (bf16[128,512]{1,0:T(8,128)(2,1)S(1)}, bf16[128,512]{1,0:T(8,128)(2,1)S(1)}, u32[]{:S(2)}, u32[]{:S(2)}) collective-permute-start(bf16[128,512]{1,0:T(8,128)(2,1)S(1)} %collective-permute-done.3.refs_3_), channel_id=1, source_target_pairs={{0,1},{1,0},{2,3},{3,2},{4,5},{5,4},{6,7},{7,6},{8,9},{9,8},{10,11... | collective-permute-start | bytes 393224 | tf_op jit(solution)/shard_map/ppermute | solution.py:49
  31.6 4.7 %collective-permute-start.6 = (bf16[128,512]{1,0:T(8,128)(2,1)S(1)}, bf16[128,512]{1,0:T(8,128)(2,1)S(1)}, u32[]{:S(2)}, u32[]{:S(2)}) collective-permute-start(bf16[128,512]{1,0:T(8,128)(2,1)S(1)} %collective-permute-done.2.refs_2_), channel_id=1, source_target_pairs={{0,1},{1,0},{2,3},{3,2},{4,5},{5,4},{6,7},{7,6},{8,9},{9,8},{10,11... | collective-permute-start | bytes 393224 | tf_op jit(solution)/shard_map/ppermute | solution.py:49
  33.0 7.1 %collective-permute-start.14 = (bf16[4,64,256]{2,1,0:T(8,128)(2,1)S(1)}, bf16[4,64,256]{2,1,0:T(8,128)(2,1)S(1)}, u32[]{:S(2)}, u32[]{:S(2)}) collective-permute-start(bf16[4,64,256]{2,1,0:T(8,128)(2,1)S(1)} %constant_dynamic-update-slice_fusion.2.refs_0_), channel_id=1, source_target_pairs={{0,1},{1,0},{2,3},{3,2},{4,5},{5,4},{6,7},{7,6},{8,9},{9,8},{10,11... | collective-permute-start | bytes 393224 | tf_op jit(solution)/shard_map/ppermute | solution.py:49
  35.4 2.0 %collective-permute-start.5 = (bf16[128,512]{1,0:T(8,128)(2,1)S(1)}, bf16[128,512]{1,0:T(8,128)(2,1)S(1)}, u32[]{:S(2)}, u32[]{:S(2)}) collective-permute-start(bf16[128,512]{1,0:T(8,128)(2,1)S(1)} %collective-permute-done.1.refs_1_), channel_id=1, source_target_pairs={{0,1},{1,0},{2,3},{3,2},{4,5},{5,4},{6,7},{7,6},{8,9},{9,8},{10,11... | collective-permute-start | bytes 393224 | tf_op jit(solution)/shard_map/ppermute | solution.py:49
  35.8 4.4 %collective-permute-start.17 = (bf16[4,64,256]{2,1,0:T(8,128)(2,1)S(1)}, bf16[4,64,256]{2,1,0:T(8,128)(2,1)S(1)}, u32[]{:S(2)}, u32[]{:S(2)}) collective-permute-start(bf16[4,64,256]{2,1,0:T(8,128)(2,1)S(1)} %collective-permute-done.13.refs_3_), channel_id=1, source_target_pairs={{0,1},{1,0},{2,3},{3,2},{4,5},{5,4},{6,7},{7,6},{8,9},{9,8},{10,11... | collective-permute-start | bytes 393224 | tf_op jit(solution)/shard_map/ppermute | solution.py:49
  35.9 4.2 %collective-permute-start.16 = (bf16[4,64,256]{2,1,0:T(8,128)(2,1)S(1)}, bf16[4,64,256]{2,1,0:T(8,128)(2,1)S(1)}, u32[]{:S(2)}, u32[]{:S(2)}) collective-permute-start(bf16[4,64,256]{2,1,0:T(8,128)(2,1)S(1)} %collective-permute-done.12.refs_2_), channel_id=1, source_target_pairs={{0,1},{1,0},{2,3},{3,2},{4,5},{5,4},{6,7},{7,6},{8,9},{9,8},{10,11... | collective-permute-start | bytes 393224 | tf_op jit(solution)/shard_map/ppermute | solution.py:49
  36.3 3.9 %collective-permute-start.15 = (bf16[4,64,256]{2,1,0:T(8,128)(2,1)S(1)}, bf16[4,64,256]{2,1,0:T(8,128)(2,1)S(1)}, u32[]{:S(2)}, u32[]{:S(2)}) collective-permute-start(bf16[4,64,256]{2,1,0:T(8,128)(2,1)S(1)} %collective-permute-done.11.refs_1_), channel_id=1, source_target_pairs={{0,1},{1,0},{2,3},{3,2},{4,5},{5,4},{6,7},{7,6},{8,9},{9,8},{10,11... | collective-permute-start | bytes 393224 | tf_op jit(solution)/shard_map/ppermute | solution.py:49
  41.2 1.2 %collective-permute-start.19 = (bf16[1,16,128]{2,1,0:T(8,128)(2,1)S(1)}, bf16[1,16,128]{2,1,0:T(8,128)(2,1)S(1)}, u32[]{:S(2)}, u32[]{:S(2)}) collective-permute-start(bf16[1,16,128]{2,1,0:T(8,128)(2,1)S(1)} %get-tuple-element.28), channel_id=1, source_target_pairs={{0,1},{1,0},{2,3},{3,2},{4,5},{5,4},{6,7},{7,6},{8,9},{9,8},{10,11... | collective-permute-start | bytes 12296 | tf_op jit(solution)/shard_map/ppermute | solution.py:49
  41.5 1.4 %collective-permute-start.18 = (bf16[16,3,16,128]{3,2,1,0:T(8,128)(2,1)S(1)}, bf16[16,3,16,128]{3,2,1,0:T(8,128)(2,1)S(1)}, u32[]{:S(2)}, u32[]{:S(2)}) collective-permute-start(bf16[16,3,16,128]{3,2,1,0:T(8,128)(2,1)S(1)} %get-tuple-element.26), channel_id=1, source_target_pairs={{0,1},{1,0},{2,3},{3,2},{4,5},{5,4},{6,7},{7,6},{8,9},{9,8},{10,11... | collective-permute-start | bytes 589832 | tf_op jit(solution)/shard_map/ppermute | solution.py:49
  43.0 27.3 %copy-start.3 = (bf16[64,192]{1,0:T(8,128)(2,1)S(1)}, bf16[64,192]{1,0:T(8,128)(2,1)}, u32[]{:S(2)}) copy-start(bf16[64,192]{1,0:T(8,128)(2,1)} %get-tuple-element.30.own_proj) | copy-start | bytes 73732
  43.0 4.6 %collective-permute-start.20 = (bf16[13,16,128]{2,1,0:T(8,128)(2,1)S(1)}, bf16[13,16,128]{2,1,0:T(8,128)(2,1)S(1)}, u32[]{:S(2)}, u32[]{:S(2)}) collective-permute-start(bf16[13,16,128]{2,1,0:T(8,128)(2,1)S(1)} %get-tuple-element.39), channel_id=1, source_target_pairs={{0,32},{1,33},{2,34},{3,35},{4,36},{5,37},{6,38},{7,39},{8,40},{9,... | collective-permute-start | bytes 159752 | tf_op jit(solution)/shard_map/ppermute | solution.py:49
  46.2 4.1 %collective-permute-start.21 = (bf16[13,16,128]{2,1,0:T(8,128)(2,1)S(1)}, bf16[13,16,128]{2,1,0:T(8,128)(2,1)S(1)}, u32[]{:S(2)}, u32[]{:S(2)}) collective-permute-start(bf16[13,16,128]{2,1,0:T(8,128)(2,1)S(1)} %get-tuple-element.40), channel_id=1, source_target_pairs={{0,17},{1,16},{2,19},{3,18},{4,21},{5,20},{6,23},{7,22},{8,25},{9,... | collective-permute-start | bytes 159752 | tf_op jit(solution)/shard_map/ppermute | solution.py:49
  47.0 4.8 %collective-permute-start.22 = (bf16[13,16,128]{2,1,0:T(8,128)(2,1)S(1)}, bf16[13,16,128]{2,1,0:T(8,128)(2,1)S(1)}, u32[]{:S(2)}, u32[]{:S(2)}) collective-permute-start(bf16[13,16,128]{2,1,0:T(8,128)(2,1)S(1)} %get-tuple-element.41), channel_id=1, source_target_pairs={{0,49},{1,48},{2,51},{3,50},{4,53},{5,52},{6,55},{7,54},{8,57},{9,... | collective-permute-start | bytes 159752 | tf_op jit(solution)/shard_map/ppermute | solution.py:49
  61.3 2.3 %collective-permute-start.23 = (bf16[4,16,128]{2,1,0:T(8,128)(2,1)S(1)}, bf16[4,16,128]{2,1,0:T(8,128)(2,1)S(1)}, u32[]{:S(2)}, u32[]{:S(2)}) collective-permute-start(bf16[4,16,128]{2,1,0:T(8,128)(2,1)S(1)} %reduce_sum.12), channel_id=1, source_target_pairs={{0,1},{1,0},{2,3},{3,2},{4,5},{5,4},{6,7},{7,6},{8,9},{9,8},{10,11... | collective-permute-start | bytes 49160 | tf_op jit(solution)/shard_map/ppermute | solution.py:49
  63.6 5.7 %collective-permute-start.25 = (bf16[4,32,128]{2,1,0:T(8,128)(2,1)S(1)}, bf16[4,32,128]{2,1,0:T(8,128)(2,1)S(1)}, u32[]{:S(2)}, u32[]{:S(2)}) collective-permute-start(bf16[4,32,128]{2,1,0:T(8,128)(2,1)S(1)} %pad_maximum_fusion.5), channel_id=1, source_target_pairs={{0,5},{1,4},{2,7},{3,6},{4,1},{5,0},{6,3},{7,2},{8,13},{9,12},{10,... | collective-permute-start | bytes 98312 | tf_op jit(solution)/shard_map/ppermute | solution.py:49
  65.7 3.7 %collective-permute-start.24 = (bf16[4,32,128]{2,1,0:T(8,128)(2,1)S(1)}, bf16[4,32,128]{2,1,0:T(8,128)(2,1)S(1)}, u32[]{:S(2)}, u32[]{:S(2)}) collective-permute-start(bf16[4,32,128]{2,1,0:T(8,128)(2,1)S(1)} %pad_maximum_fusion.5), channel_id=1, source_target_pairs={{0,3},{1,2},{2,1},{3,0},{4,7},{5,6},{6,5},{7,4},{8,11},{9,10},{10,... | collective-permute-start | bytes 98312 | tf_op jit(solution)/shard_map/ppermute | solution.py:49
  65.8 4.6 %collective-permute-start.26 = (bf16[4,32,128]{2,1,0:T(8,128)(2,1)S(1)}, bf16[4,32,128]{2,1,0:T(8,128)(2,1)S(1)}, u32[]{:S(2)}, u32[]{:S(2)}) collective-permute-start(bf16[4,32,128]{2,1,0:T(8,128)(2,1)S(1)} %pad_maximum_fusion.5), channel_id=1, source_target_pairs={{0,7},{1,6},{2,5},{3,4},{4,3},{5,2},{6,1},{7,0},{8,15},{9,14},{10,... | collective-permute-start | bytes 98312 | tf_op jit(solution)/shard_map/ppermute | solution.py:49

commit v5 on v4

--- a/solution.py
+++ b/solution.py
@@ -223,49 +223,26 @@
             yield p, [t.astype(BF) for t in tiles], left[:, 128:256] + right[:, 128:256]
 
 
-def low_kernel(x_ref, latent, *refs):
-    blocks, (maps, keep, give) = refs[0:8], refs[8:]
-    f, c = lax.axis_index("fsdp"), lax.axis_index("dp") & 1
-    total = jnp.zeros((TOK, RANK), F32)
+def gelu_slope(preact):
+    return jax.jvp(jax.nn.gelu, (preact,), (jnp.ones_like(preact),))[1]
+
+
+def main_kernel(
+    rows, cols, ident, count, *refs,
+):
+    near, far, blocks = refs[0:4], refs[4:8], refs[8:16]
+    face_ref, w_embed, w_feature, x_ref, keep, give, latent_ref, maps = refs[16:]
+    d = lax.axis_index("dp")
+    f, c = lax.axis_index("fsdp"), d & 1
+    half = parity(f, d)
+    low = jnp.zeros((TOK, RANK), F32)
     for p, tiles, _ in side_by_side(f, c, 0, blocks):
         for t in range(3):
             spot = pl.ds(pl.multiple_of(p * PAIR + 128 * t, 128), 128)
             maps[:, spot] = tiles[t]
         spot = pl.ds(pl.multiple_of(p * PAIR, 128), PAIR)
-        total += dot(x_ref[:, spot], maps[:, spot], 1, 1)
-    part = dot(latent[...], dot(total.astype(BF), shifted(RANK, 128, 0), 1, 0).astype(BF), 1, 0)
-    lane = lax.broadcasted_iota(jnp.int32, (KH, 128), 1)
-    unit = jnp.where(lane < 64, part[0:KH], pltpu.roll(part[KH : 2 * KH], 64, 1)).astype(BF)
-    top, bottom = unit[0 : KH // 2], unit[KH // 2 : KH]
-    half = parity(f, lax.axis_index("dp"))
-    keep[0] = jnp.where(half == 0, top, bottom)
-    give[0] = jnp.where(half == 0, bottom, top)
-
-
-def low_maps(*args):
-    share = jax.ShapeDtypeStruct((1, KH // 2, 128), BF)
-    return pl.pallas_call(
-        low_kernel,
-        out_shape=(jax.ShapeDtypeStruct((RANK, D), BF), share, share),
-        in_specs=vmem(10),
-        out_specs=tuple(vmem(3)),
-        compiler_params=params(16),
-        cost_estimate=cost(2),
-        name="low",
-    )(*args)
-
-
-def gelu_slope(preact):
-    return jax.jvp(jax.nn.gelu, (preact,), (jnp.ones_like(preact),))[1]
-
-
-def main_kernel(
-    rows, cols, ident, count, *refs,
-):
-    near, far = refs[0:4], refs[4:8]
-    face_ref, w_embed, w_feature, x_ref, keep, give, latent_ref = refs[8:]
-    d = lax.axis_index("dp")
-    half = parity(lax.axis_index("fsdp"), d)
+        low += dot(x_ref[:, spot], maps[:, spot], 1, 1)
+    low = dot(low.astype(BF), shifted(RANK, 128, 0), 1, 0).astype(BF)
     slot = lax.broadcasted_iota(jnp.int32, (8, 16 * MAXF), 0)
     lane = lax.broadcasted_iota(jnp.int32, (8, 16 * MAXF), 1)
     live = jnp.zeros(slot.shape, jnp.bool_)
@@ -311,6 +288,10 @@
     d_latent = d_latent.astype(BF)
     latent_ref[...] = d_latent
     lane = lax.broadcasted_iota(jnp.int32, (KH, 128), 1)
+    part = dot(d_latent, low, 1, 0)
+    unit = jnp.where(lane < 64, part[0:KH], pltpu.roll(part[KH : 2 * KH], 64, 1))
+    for u in range(3):
+        share(half, unit.astype(BF), keep, give, 16, u)
     for p in range(8):
         part = dot(d_latent, x_ref[:, p * PAIR : p * PAIR + PAIR], 1, 0)
         for u in range(6):
@@ -331,12 +312,17 @@
 
 
 def main(*args):
-    shares = jax.ShapeDtypeStruct((16, 3, KH // 2, 128), BF)
+    shares = jax.ShapeDtypeStruct((17, 3, KH // 2, 128), BF)
     return pl.pallas_call(
         main_kernel,
-        out_shape=(shares, shares, jax.ShapeDtypeStruct((CH, TOK), BF)),
-        in_specs=[SMEM] * 4 + vmem(12),
-        out_specs=tuple(vmem(3)),
+        out_shape=(
+            shares,
+            shares,
+            jax.ShapeDtypeStruct((CH, TOK), BF),
+            jax.ShapeDtypeStruct((RANK, D), BF),
+        ),
+        in_specs=[SMEM] * 4 + vmem(20),
+        out_specs=tuple(vmem(4)),
         compiler_params=params(24),
         cost_estimate=cost(3),
         name="main",
@@ -464,13 +450,13 @@
     return list(groups.values())
 
 
-def reduce_all(keep, give, keep_low, give_low, f, half):
+def reduce_all(keep, give, f, half):
     zl, y = f // 4, f % 4
     v = add(keep, send(give, flip(c=1)))
-    low = add(keep_low, send(give_low, flip(c=1)))
+    v, low = v[:16], v[16, :1]
     v = v.reshape((4, 12) + v.shape[2:])
     part = lambda k: jnp.concatenate([slab_of(v, y ^ k, 1)[0], low])
-    v = add(part(0), *[send(part(k), flip(y=k, c=k & 1)) for k in (2, 1, 3)])
+    v = add(part(0), *[send(part(k), flip(y=k, c=k & 1)) for k in (3, 1, 2)])
     v, low = v[:12].reshape((4, 3) + v.shape[1:]), v[12:]
     v = beside(v, low)
     v = jnp.broadcast_to(v[:, None], (4, 2) + v.shape[1:]).reshape((8,) + v.shape[1:])
@@ -511,14 +497,14 @@
     faces = after(faces, maps)
     upper = lax.broadcasted_iota(jnp.int32, faces.shape, 0) < 8
     faces = jnp.where(upper, gelu_slope(faces), faces)
+    blocks = [maps] + [after(part, faces) for part in blocks[1:]]
     tables += [send(part, flip(c=1)) for part in tables]
     blocks += [send(part, flip(c=1)) for part in blocks]
-    keep, give, d_latent = main(
+    keep, give, d_latent, whole_a = main(
         box_rows, box_cols, identity, face_count,
-        *tables, faces, w_embed, w_feature, block_in,
+        *tables, *blocks, faces, w_embed, w_feature, block_in,
     )
-    whole_a, keep_low, give_low = low_maps(block_in, d_latent, *blocks)
-    total = reduce_all(keep, give, keep_low, give_low, f, parity(f, d))
+    total = reduce_all(keep, give, f, parity(f, d))
     grad_in, cross = through(d_latent, whole_a, *blocks)
     grad_a, grad_b = last(total, cross, own_proj)
     return grad_in, grad_a.T, grad_b

time: 71.6 us -> 72 us (level)
  blocking collectives: 9.42 us -> 11.3 us
  waiting for transfers between devices: 10.6 us -> 9.1 us
    all_to_all x1, blocking collectives: 9.42 us -> 11.3 us  [exchange(): v = lax.all_to_all(v, AXES, 0, 0, axis_index_groups=groups, tiled=True)]
    ppermute x27 -> x26, waiting for transfers between devices: 10.6 us -> 9.1 us  [send(): return lax.ppermute(value, AXES, perm)]
    pallas_call x1 -> x0, Pallas kernels: 1.04 us -> none  [low_maps(): pl.pallas_call(low_kernel, out_shape=(jax.ShapeDtypeStruct((RANK, D), BF)...]
    ppermute x27 -> x26, starting transfers between devices: 34.4 us -> 34.8 us  [send(): return lax.ppermute(value, AXES, perm)]
  transfers between devices with their start and end apart: 27 -> 26, of which waited for: 10 -> 12; matrix products, arithmetic and copies ran while one was open for 2% -> 2% of each run, Pallas kernels for 16% -> 12%
where the time goes in v5:
time: 72 us; the launch traced here: 71.8 us
  starting transfers between devices  34.8 us (48%)
  Pallas kernels  13 us (18%)
  blocking collectives  11.3 us (16%)
  waiting for transfers between devices  9.1 us (13%)
  between operations  1.58 us (2%)
  other arithmetic  1.02 us (1%)
  local copies, waits for them, and re-layouts  0.93 us (1%)
    ppermute x26, starting transfers between devices, send(): return lax.ppermute(value, AXES, perm)  34.8 us
    all_to_all x1, blocking collectives, exchange(): v = lax.all_to_all(v, AXES, 0, 0, axis_index_groups=groups, tiled=True)  11.3 us
    ppermute x26, waiting for transfers between devices, send(): return lax.ppermute(value, AXES, perm)  9.1 us
    pallas_call x1, Pallas kernels, front(): pl.pallas_call(front_kernel, out_shape=(jax.ShapeDtypeStruct((1, CH, 256)...  6.87 us
    pallas_call x1, Pallas kernels, main(): pl.pallas_call(main_kernel, out_shape=(shares, shares, jax.ShapeDtypeStru...  3.29 us
    pallas_call x1, Pallas kernels, through(): pl.pallas_call(through_kernel, out_shape=(jax.ShapeDtypeStruct((TOK, D),...  1.83 us
  transfers between devices with their start and end apart: 26, of which 12 were waited for; matrix products, arithmetic and copies ran while one was open for 2% of the time, Pallas kernels for 12%

profile of v5, /device:TPU:1, one launch (start us, length us, event | category | flops | bytes accessed | tf_op | source)
XLA Modules:
  0.0 71.8 jit_solution(13004506526298163040)
XLA Ops:
  0.6 7.5 %collective-permute-start = (bf16[64,512]{1,0:T(8,128)(2,1)}, bf16[64,512]{1,0:T(8,128)(2,1)S(1)}, u32[]{:S(2)}, u32[]{:S(2)}) collective-permute-start(bf16[64,512]{1,0:T(8,128)(2,1)} %param.21), channel_id=1, source_target_pairs={{0,137},{1,136},{2,139},{3,138},{4,141},{5,140},{6,143},{7,142},{8... | collective-permute-start | bytes 196616 | tf_op jit(solution)/shard_map/ppermute | solution.py:49
  8.2 6.9 %front.1 = (bf16[1,64,256]{2,1,0:T(8,128)(2,1)}, bf16[64,192]{1,0:T(8,128)(2,1)}, f32[16,512]{1,0:T(8,128)}) custom-call(s32[1,6]{1,0:T(1,128)} %rows.3, s32[1,6]{1,0:T(1,128)} %cols.3, bf16[64,3072]{1,0:T(8,128)(2,1)} %bitcast.20, bf16[192,3072]{1,0:T(8,128)(2,1)} %weight_hbm.1, bf16[64,192]{1,0:T(8,128)(2,1)} %bitcast.22, bf16[64,192]{1,0:T(8,128)(2,1)} %b_hbm.1, ...), custom_call_target="tpu_custom_call" | custom-call | flops 4 | bytes 4 | tf_op jit(solution)/shard_map/front/pallas_call | solution.py:177
  15.1 0.4 collective-permute-start.8
  15.4 0.8 %constant_dynamic-update-slice_fusion.5 = bf16[4,64,256]{2,1,0:T(8,128)(2,1)S(1)} fusion(bf16[1,64,256]{2,1,0:T(8,128)(2,1)} %get-tuple-element.20), kind=kLoop, calls=%fused_computation.33 | loop fusion | bytes 65536
  16.2 1.9 %collective-permute-start.9 = (bf16[1,64,256]{2,1,0:T(8,128)(2,1)}, bf16[1,64,256]{2,1,0:T(8,128)(2,1)S(1)}, u32[]{:S(2)}, u32[]{:S(2)}) collective-permute-start(bf16[1,64,256]{2,1,0:T(8,128)(2,1)} %get-tuple-element.20), channel_id=1, source_target_pairs={{0,129},{1,128},{2,131},{3,130},{4,133},{5,132},{6,135},{7,134},{8... | collective-permute-start | bytes 98312 | tf_op jit(solution)/shard_map/ppermute | solution.py:49
  18.2 1.2 %collective-permute-start.10 = (bf16[1,64,256]{2,1,0:T(8,128)(2,1)}, bf16[1,64,256]{2,1,0:T(8,128)(2,1)S(1)}, u32[]{:S(2)}, u32[]{:S(2)}) collective-permute-start(bf16[1,64,256]{2,1,0:T(8,128)(2,1)} %get-tuple-element.20), channel_id=1, source_target_pairs={{0,193},{1,192},{2,195},{3,194},{4,197},{5,196},{6,199},{7,198},{8... | collective-permute-start | bytes 98312 | tf_op jit(solution)/shard_map/ppermute | solution.py:49
  19.3 2.0 %collective-permute-start.1 = (bf16[128,512]{1,0:T(8,128)(2,1)S(1)}, bf16[128,512]{1,0:T(8,128)(2,1)S(1)}, u32[]{:S(2)}, u32[]{:S(2)}) collective-permute-start(bf16[128,512]{1,0:T(8,128)(2,1)S(1)} %constant_dynamic-update-slice_fusion.refs_0_), channel_id=1, source_target_pairs={{0,3},{1,2},{2,1},{3,0},{4,7},{5,6},{6,5},{7,4},{8,11},{9,10},{10,... | collective-permute-start | bytes 393224 | tf_op jit(solution)/shard_map/ppermute | solution.py:49
  21.3 2.0 %collective-permute-start.2 = (bf16[128,512]{1,0:T(8,128)(2,1)S(1)}, bf16[128,512]{1,0:T(8,128)(2,1)S(1)}, u32[]{:S(2)}, u32[]{:S(2)}) collective-permute-start(bf16[128,512]{1,0:T(8,128)(2,1)S(1)} %constant_dynamic-update-slice_fusion.refs_0_), channel_id=1, source_target_pairs={{0,5},{1,4},{2,7},{3,6},{4,1},{5,0},{6,3},{7,2},{8,13},{9,12},{10,... | collective-permute-start | bytes 393224 | tf_op jit(solution)/shard_map/ppermute | solution.py:49
  23.3 0.2 collective-permute-done.10
  23.5 3.4 %collective-permute-start.13 = (bf16[4,64,256]{2,1,0:T(8,128)(2,1)S(1)}, bf16[4,64,256]{2,1,0:T(8,128)(2,1)S(1)}, u32[]{:S(2)}, u32[]{:S(2)}) collective-permute-start(bf16[4,64,256]{2,1,0:T(8,128)(2,1)S(1)} %constant_dynamic-update-slice_fusion.2.refs_8_.refs_0_), channel_id=1, source_target_pairs={{0,49},{1,48},{2,51},{3,50},{4,53},{5,52},{6,55},{7,54},{8,57},{9,... | collective-permute-start | bytes 393224 | tf_op jit(solution)/shard_map/ppermute | solution.py:49
  26.9 0.3 collective-permute-start.12
  27.2 2.0 %collective-permute-start.3 = (bf16[128,512]{1,0:T(8,128)(2,1)S(1)}, bf16[128,512]{1,0:T(8,128)(2,1)S(1)}, u32[]{:S(2)}, u32[]{:S(2)}) collective-permute-start(bf16[128,512]{1,0:T(8,128)(2,1)S(1)} %constant_dynamic-update-slice_fusion.refs_0_), channel_id=1, source_target_pairs={{0,7},{1,6},{2,5},{3,4},{4,3},{5,2},{6,1},{7,0},{8,15},{9,14},{10,... | collective-permute-start | bytes 393224 | tf_op jit(solution)/shard_map/ppermute | solution.py:49
  29.2 0.6 collective-permute-start.4
  29.8 0.5 collective-permute-done.2.refs_2_
  30.3 1.8 %collective-permute-start.11 = (bf16[4,64,256]{2,1,0:T(8,128)(2,1)S(1)}, bf16[4,64,256]{2,1,0:T(8,128)(2,1)S(1)}, u32[]{:S(2)}, u32[]{:S(2)}) collective-permute-start(bf16[4,64,256]{2,1,0:T(8,128)(2,1)S(1)} %constant_dynamic-update-slice_fusion.2.refs_8_.refs_0_), channel_id=1, source_target_pairs={{0,17},{1,16},{2,19},{3,18},{4,21},{5,20},{6,23},{7,22},{8,25},{9,... | collective-permute-start | bytes 393224 | tf_op jit(solution)/shard_map/ppermute | solution.py:49
  32.0 1.7 %collective-permute-done.13.refs_11_.refs_3_ = bf16[4,64,256]{2,1,0:T(8,128)(2,1)S(1)} collective-permute-done((bf16[4,64,256]{2,1,0:T(8,128)(2,1)S(1)}, bf16[4,64,256]{2,1,0:T(8,128)(2,1)S(1)}, u32[]{:S(2)}, u32[]{:S(2)}) %collective-permute-start.13) | collective-permute-done | bytes 131104 | tf_op jit(solution)/shard_map/ppermute | solution.py:49
  33.7 0.0 collective-permute-start.14
  33.7 0.0 collective-permute-done.12.refs_10_.refs_2_
  33.7 0.5 collective-permute-start.5
  34.2 0.8 %fusion.10.refs_16_ = f32[16,512]{1,0:T(8,128)S(1)} fusion(f32[16,512]{1,0:T(8,128)} %get-tuple-element.22, pred[16]{0:T(512)(128)(4,1)S(1)} %iota_compare_fusion), kind=kLoop, calls=%fused_computation.24 | loop fusion | flops 139264 | bytes 65552 | tf_op jit(solution)/shard_map/jit(_where)/select_n | solution.py:499
  35.1 0.1 collective-permute-start.6
  35.1 1.0 %collective-permute-done.11.refs_9_.refs_1_ = bf16[4,64,256]{2,1,0:T(8,128)(2,1)S(1)} collective-permute-done((bf16[4,64,256]{2,1,0:T(8,128)(2,1)S(1)}, bf16[4,64,256]{2,1,0:T(8,128)(2,1)S(1)}, u32[]{:S(2)}, u32[]{:S(2)}) %collective-permute-start.11) | collective-permute-done | bytes 131104 | tf_op jit(solution)/shard_map/ppermute | solution.py:49
  36.1 0.4 collective-permute-start.7
  36.5 0.0 collective-permute-done.4.refs_4_
  36.5 0.1 collective-permute-start.17
  36.6 0.4 collective-permute-start.16
  37.0 0.3 collective-permute-start.15
  38.0 0.1 collective-permute-done.16.refs_14_.refs_6_
  38.0 0.3 collective-permute-done.15.refs_13_.refs_5_
  38.4 3.3 %main.1 = (bf16[17,3,16,128]{3,2,1,0:T(8,128)(2,1)S(1)}, bf16[17,3,16,128]{3,2,1,0:T(8,128)(2,1)S(1)}, bf16[64,256]{1,0:T(8,128)(2,1)S(1)}, bf16[64,3072]{1,0:T(8,128)(2,1)S(1)}) custom-call(s32[1,6]{1,0:T(1,128)S(1)} %copy-done.4, s32[1,6]{1,0:T(1,128)S(1)} %copy-done.5, s32[1,6]{1,0:T(1,128)S(1)} %copy-done.6, s32[1]{0:T(128)S(6)} %copy.20.count, ...), custom_call_target="tpu_custom_call" | custom-call | flops 3 | bytes 3 | tf_op jit(solution)/shard_map/main/pallas_call | solution.py:316
  41.7 0.4 collective-permute-start.18
  42.1 1.2 %collective-permute-done.18 = bf16[17,3,16,128]{3,2,1,0:T(8,128)(2,1)S(1)} collective-permute-done((bf16[17,3,16,128]{3,2,1,0:T(8,128)(2,1)S(1)}, bf16[17,3,16,128]{3,2,1,0:T(8,128)(2,1)S(1)}, u32[]{:S(2)}, u32[]{:S(2)}) %collective-permute-start.18) | collective-permute-done | bytes 208928 | tf_op jit(solution)/shard_map/ppermute | solution.py:49
  43.2 0.1 add_convert_fusion
  43.4 0.0 copy-start.3
  43.4 3.0 %collective-permute-start.19 = (bf16[13,16,128]{2,1,0:T(8,128)(2,1)S(1)}, bf16[13,16,128]{2,1,0:T(8,128)(2,1)S(1)}, u32[]{:S(2)}, u32[]{:S(2)}) collective-permute-start(bf16[13,16,128]{2,1,0:T(8,128)(2,1)S(1)} %get-tuple-element.41), channel_id=1, source_target_pairs={{0,49},{1,48},{2,51},{3,50},{4,53},{5,52},{6,55},{7,54},{8,57},{9,... | collective-permute-start | bytes 159752 | tf_op jit(solution)/shard_map/ppermute | solution.py:49
  46.4 1.3 %collective-permute-start.21 = (bf16[13,16,128]{2,1,0:T(8,128)(2,1)S(1)}, bf16[13,16,128]{2,1,0:T(8,128)(2,1)S(1)}, u32[]{:S(2)}, u32[]{:S(2)}) collective-permute-start(bf16[13,16,128]{2,1,0:T(8,128)(2,1)S(1)} %get-tuple-element.43), channel_id=1, source_target_pairs={{0,32},{1,33},{2,34},{3,35},{4,36},{5,37},{6,38},{7,39},{8,40},{9,... | collective-permute-start | bytes 159752 | tf_op jit(solution)/shard_map/ppermute | solution.py:49
  47.7 0.7 %collective-permute-done.19 = bf16[13,16,128]{2,1,0:T(8,128)(2,1)S(1)} collective-permute-done((bf16[13,16,128]{2,1,0:T(8,128)(2,1)S(1)}, bf16[13,16,128]{2,1,0:T(8,128)(2,1)S(1)}, u32[]{:S(2)}, u32[]{:S(2)}) %collective-permute-start.19) | collective-permute-done | bytes 53280 | tf_op jit(solution)/shard_map/ppermute | solution.py:49
  48.4 2.0 %collective-permute-done.20 = bf16[13,16,128]{2,1,0:T(8,128)(2,1)S(1)} collective-permute-done((bf16[13,16,128]{2,1,0:T(8,128)(2,1)S(1)}, bf16[13,16,128]{2,1,0:T(8,128)(2,1)S(1)}, u32[]{:S(2)}, u32[]{:S(2)}) %collective-permute-start.20) | collective-permute-done | bytes 53280 | tf_op jit(solution)/shard_map/ppermute | solution.py:49
  50.5 0.4 collective-permute-done.21
  51.0 11.3 %all_to_all.5 = bf16[8,4,16,128]{3,2,1,0:T(8,128)(2,1)S(1)} all-to-all(bf16[8,4,16,128]{3,2,1,0:T(8,128)(2,1)S(1)} %bitcast.19), channel_id=1, replica_groups={{0,8,65,73,128,136,193,201},{1,9,64,72,129,137,192,200},{2,10,67,75,130..., dimensions={0} | all-to-all | bytes 262144 | tf_op jit(solution)/shard_map/all_to_all | solution.py:426
  62.4 1.1 %collective-permute-start.22 = (bf16[4,16,128]{2,1,0:T(8,128)(2,1)S(1)}, bf16[4,16,128]{2,1,0:T(8,128)(2,1)S(1)}, u32[]{:S(2)}, u32[]{:S(2)}) collective-permute-start(bf16[4,16,128]{2,1,0:T(8,128)(2,1)S(1)} %reduce_sum.12), channel_id=1, source_target_pairs={{0,1},{1,0},{2,3},{3,2},{4,5},{5,4},{6,7},{7,6},{8,9},{9,8},{10,11... | collective-permute-start | bytes 49160 | tf_op jit(solution)/shard_map/ppermute | solution.py:49
  63.5 0.8 %collective-permute-done.22 = bf16[4,16,128]{2,1,0:T(8,128)(2,1)S(1)} collective-permute-done((bf16[4,16,128]{2,1,0:T(8,128)(2,1)S(1)}, bf16[4,16,128]{2,1,0:T(8,128)(2,1)S(1)}, u32[]{:S(2)}, u32[]{:S(2)}) %collective-permute-start.22) | collective-permute-done | bytes 16416 | tf_op jit(solution)/shard_map/ppermute | solution.py:49
  64.3 0.4 collective-permute-start.23
  64.7 1.5 %collective-permute-start.24 = (bf16[4,32,128]{2,1,0:T(8,128)(2,1)S(1)}, bf16[4,32,128]{2,1,0:T(8,128)(2,1)S(1)}, u32[]{:S(2)}, u32[]{:S(2)}) collective-permute-start(bf16[4,32,128]{2,1,0:T(8,128)(2,1)S(1)} %pad_maximum_fusion.5), channel_id=1, source_target_pairs={{0,5},{1,4},{2,7},{3,6},{4,1},{5,0},{6,3},{7,2},{8,13},{9,12},{10,... | collective-permute-start | bytes 98312 | tf_op jit(solution)/shard_map/ppermute | solution.py:49
  66.2 2.6 %collective-permute-start.25 = (bf16[4,32,128]{2,1,0:T(8,128)(2,1)S(1)}, bf16[4,32,128]{2,1,0:T(8,128)(2,1)S(1)}, u32[]{:S(2)}, u32[]{:S(2)}) collective-permute-start(bf16[4,32,128]{2,1,0:T(8,128)(2,1)S(1)} %pad_maximum_fusion.5), channel_id=1, source_target_pairs={{0,7},{1,6},{2,5},{3,4},{4,3},{5,2},{6,1},{7,0},{8,15},{9,14},{10,... | collective-permute-start | bytes 98312 | tf_op jit(solution)/shard_map/ppermute | solution.py:49
  68.8 1.8 %through.1 = (bf16[256,3072]{1,0:T(8,128)(2,1)}, bf16[64,64]{1,0:T(8,128)(2,1)S(1)}) custom-call(bf16[64,256]{1,0:T(8,128)(2,1)S(1)} %get-tuple-element.26.latent, bf16[64,3072]{1,0:T(8,128)(2,1)S(1)} %get-tuple-element.27.maps, bf16[4,64,256]{2,1,0:T(8,128)(2,1)S(1)} %constant_dynamic-update-slice_fusion.2.refs_8_.refs_0_, ...), custom_call_target="tpu_custom_call" | custom-call | flops 3 | bytes 3 | tf_op jit(solution)/shard_map/through/pallas_call | solution.py:357
  70.6 0.1 collective-permute-done.25
  70.8 1.0 %last.1 = (f32[64,192]{1,0:T(8,128)}, f32[64,192]{1,0:T(8,128)}) custom-call(bf16[4,32,128]{2,1,0:T(8,128)(2,1)S(1)} %add_convert_fusion.2.units, bf16[64,64]{1,0:T(8,128)(2,1)S(1)} %get-tuple-element.31.cross, bf16[64,192]{1,0:T(8,128)(2,1)S(1)} %copy-done.3), custom_call_target="tpu_custom_call" | custom-call | flops 1 | bytes 1 | tf_op jit(solution)/shard_map/last/pallas_call | solution.py:397
  (48 shorter events, 0.3 us)
Async XLA Ops:
  0.6 14.4 %collective-permute-start = (bf16[64,512]{1,0:T(8,128)(2,1)}, bf16[64,512]{1,0:T(8,128)(2,1)S(1)}, u32[]{:S(2)}, u32[]{:S(2)}) collective-permute-start(bf16[64,512]{1,0:T(8,128)(2,1)} %param.21), channel_id=1, source_target_pairs={{0,137},{1,136},{2,139},{3,138},{4,141},{5,140},{6,143},{7,142},{8... | collective-permute-start | bytes 196616 | tf_op jit(solution)/shard_map/ppermute | solution.py:49
  8.1 6.9 %copy-start.7 = (bf16[64,512]{1,0:T(8,128)(2,1)S(1)}, bf16[64,512]{1,0:T(8,128)(2,1)}, u32[]{:S(2)}) copy-start(bf16[64,512]{1,0:T(8,128)(2,1)} %param.21) | copy-start | bytes 196612
  8.1 30.2 %copy-start = (bf16[3136,512]{1,0:T(8,128)(2,1)S(1)}, bf16[3136,512]{1,0:T(8,128)(2,1)}, u32[]{:S(2)}) copy-start(bf16[3136,512]{1,0:T(8,128)(2,1)} %refs_18_.1) | copy-start | bytes 9633796
  8.1 30.2 %copy-start.1 = (bf16[512,512]{1,0:T(8,128)(2,1)S(1)}, bf16[512,512]{1,0:T(8,128)(2,1)}, u32[]{:S(2)}) copy-start(bf16[512,512]{1,0:T(8,128)(2,1)} %refs_17_.1) | copy-start | bytes 1572868
  8.1 30.2 %copy-start.2 = (bf16[256,3072]{1,0:T(8,128)(2,1)S(1)}, bf16[256,3072]{1,0:T(8,128)(2,1)}, u32[]{:S(2)}) copy-start(bf16[256,3072]{1,0:T(8,128)(2,1)} %refs_19_.1) | copy-start | bytes 4718596
  8.1 30.2 %copy-start.4 = (s32[1,6]{1,0:T(1,128)S(1)}, s32[1,6]{1,0:T(1,128)}, u32[]{:S(2)}) copy-start(s32[1,6]{1,0:T(1,128)} %rows.3) | copy-start | bytes 76
  8.2 30.2 %copy-start.5 = (s32[1,6]{1,0:T(1,128)S(1)}, s32[1,6]{1,0:T(1,128)}, u32[]{:S(2)}) copy-start(s32[1,6]{1,0:T(1,128)} %cols.3) | copy-start | bytes 76
  8.2 30.2 %copy-start.6 = (s32[1,6]{1,0:T(1,128)S(1)}, s32[1,6]{1,0:T(1,128)}, u32[]{:S(2)}) copy-start(s32[1,6]{1,0:T(1,128)} %ident.1) | copy-start | bytes 76
  15.1 8.2 %collective-permute-start.8 = (bf16[1,64,256]{2,1,0:T(8,128)(2,1)}, bf16[1,64,256]{2,1,0:T(8,128)(2,1)S(1)}, u32[]{:S(2)}, u32[]{:S(2)}) collective-permute-start(bf16[1,64,256]{2,1,0:T(8,128)(2,1)} %get-tuple-element.20), channel_id=1, source_target_pairs={{0,65},{1,64},{2,67},{3,66},{4,69},{5,68},{6,71},{7,70},{8,73},{9,... | collective-permute-start | bytes 98312 | tf_op jit(solution)/shard_map/ppermute | solution.py:49
  16.2 7.0 %collective-permute-start.9 = (bf16[1,64,256]{2,1,0:T(8,128)(2,1)}, bf16[1,64,256]{2,1,0:T(8,128)(2,1)S(1)}, u32[]{:S(2)}, u32[]{:S(2)}) collective-permute-start(bf16[1,64,256]{2,1,0:T(8,128)(2,1)} %get-tuple-element.20), channel_id=1, source_target_pairs={{0,129},{1,128},{2,131},{3,130},{4,133},{5,132},{6,135},{7,134},{8... | collective-permute-start | bytes 98312 | tf_op jit(solution)/shard_map/ppermute | solution.py:49
  18.2 5.3 %collective-permute-start.10 = (bf16[1,64,256]{2,1,0:T(8,128)(2,1)}, bf16[1,64,256]{2,1,0:T(8,128)(2,1)S(1)}, u32[]{:S(2)}, u32[]{:S(2)}) collective-permute-start(bf16[1,64,256]{2,1,0:T(8,128)(2,1)} %get-tuple-element.20), channel_id=1, source_target_pairs={{0,193},{1,192},{2,195},{3,194},{4,197},{5,196},{6,199},{7,198},{8... | collective-permute-start | bytes 98312 | tf_op jit(solution)/shard_map/ppermute | solution.py:49
  19.3 9.9 %collective-permute-start.1 = (bf16[128,512]{1,0:T(8,128)(2,1)S(1)}, bf16[128,512]{1,0:T(8,128)(2,1)S(1)}, u32[]{:S(2)}, u32[]{:S(2)}) collective-permute-start(bf16[128,512]{1,0:T(8,128)(2,1)S(1)} %constant_dynamic-update-slice_fusion.refs_0_), channel_id=1, source_target_pairs={{0,3},{1,2},{2,1},{3,0},{4,7},{5,6},{6,5},{7,4},{8,11},{9,10},{10,... | collective-permute-start | bytes 393224 | tf_op jit(solution)/shard_map/ppermute | solution.py:49
  21.3 9.0 %collective-permute-start.2 = (bf16[128,512]{1,0:T(8,128)(2,1)S(1)}, bf16[128,512]{1,0:T(8,128)(2,1)S(1)}, u32[]{:S(2)}, u32[]{:S(2)}) collective-permute-start(bf16[128,512]{1,0:T(8,128)(2,1)S(1)} %constant_dynamic-update-slice_fusion.refs_0_), channel_id=1, source_target_pairs={{0,5},{1,4},{2,7},{3,6},{4,1},{5,0},{6,3},{7,2},{8,13},{9,12},{10,... | collective-permute-start | bytes 393224 | tf_op jit(solution)/shard_map/ppermute | solution.py:49
  23.5 10.2 %collective-permute-start.13 = (bf16[4,64,256]{2,1,0:T(8,128)(2,1)S(1)}, bf16[4,64,256]{2,1,0:T(8,128)(2,1)S(1)}, u32[]{:S(2)}, u32[]{:S(2)}) collective-permute-start(bf16[4,64,256]{2,1,0:T(8,128)(2,1)S(1)} %constant_dynamic-update-slice_fusion.2.refs_8_.refs_0_), channel_id=1, source_target_pairs={{0,49},{1,48},{2,51},{3,50},{4,53},{5,52},{6,55},{7,54},{8,57},{9,... | collective-permute-start | bytes 393224 | tf_op jit(solution)/shard_map/ppermute | solution.py:49
  26.9 6.8 %collective-permute-start.12 = (bf16[4,64,256]{2,1,0:T(8,128)(2,1)S(1)}, bf16[4,64,256]{2,1,0:T(8,128)(2,1)S(1)}, u32[]{:S(2)}, u32[]{:S(2)}) collective-permute-start(bf16[4,64,256]{2,1,0:T(8,128)(2,1)S(1)} %constant_dynamic-update-slice_fusion.2.refs_8_.refs_0_), channel_id=1, source_target_pairs={{0,33},{1,32},{2,35},{3,34},{4,37},{5,36},{6,39},{7,38},{8,41},{9,... | collective-permute-start | bytes 393224 | tf_op jit(solution)/shard_map/ppermute | solution.py:49
  27.2 7.9 %collective-permute-start.3 = (bf16[128,512]{1,0:T(8,128)(2,1)S(1)}, bf16[128,512]{1,0:T(8,128)(2,1)S(1)}, u32[]{:S(2)}, u32[]{:S(2)}) collective-permute-start(bf16[128,512]{1,0:T(8,128)(2,1)S(1)} %constant_dynamic-update-slice_fusion.refs_0_), channel_id=1, source_target_pairs={{0,7},{1,6},{2,5},{3,4},{4,3},{5,2},{6,1},{7,0},{8,15},{9,14},{10,... | collective-permute-start | bytes 393224 | tf_op jit(solution)/shard_map/ppermute | solution.py:49
  29.2 7.3 %collective-permute-start.4 = (bf16[128,512]{1,0:T(8,128)(2,1)S(1)}, bf16[128,512]{1,0:T(8,128)(2,1)S(1)}, u32[]{:S(2)}, u32[]{:S(2)}) collective-permute-start(bf16[128,512]{1,0:T(8,128)(2,1)S(1)} %constant_dynamic-update-slice_fusion.refs_0_), channel_id=1, source_target_pairs={{0,1},{1,0},{2,3},{3,2},{4,5},{5,4},{6,7},{7,6},{8,9},{9,8},{10,11... | collective-permute-start | bytes 393224 | tf_op jit(solution)/shard_map/ppermute | solution.py:49
  30.3 5.8 %collective-permute-start.11 = (bf16[4,64,256]{2,1,0:T(8,128)(2,1)S(1)}, bf16[4,64,256]{2,1,0:T(8,128)(2,1)S(1)}, u32[]{:S(2)}, u32[]{:S(2)}) collective-permute-start(bf16[4,64,256]{2,1,0:T(8,128)(2,1)S(1)} %constant_dynamic-update-slice_fusion.2.refs_8_.refs_0_), channel_id=1, source_target_pairs={{0,17},{1,16},{2,19},{3,18},{4,21},{5,20},{6,23},{7,22},{8,25},{9,... | collective-permute-start | bytes 393224 | tf_op jit(solution)/shard_map/ppermute | solution.py:49
  33.7 2.9 %collective-permute-start.14 = (bf16[4,64,256]{2,1,0:T(8,128)(2,1)S(1)}, bf16[4,64,256]{2,1,0:T(8,128)(2,1)S(1)}, u32[]{:S(2)}, u32[]{:S(2)}) collective-permute-start(bf16[4,64,256]{2,1,0:T(8,128)(2,1)S(1)} %constant_dynamic-update-slice_fusion.2.refs_8_.refs_0_), channel_id=1, source_target_pairs={{0,1},{1,0},{2,3},{3,2},{4,5},{5,4},{6,7},{7,6},{8,9},{9,8},{10,11... | collective-permute-start | bytes 393224 | tf_op jit(solution)/shard_map/ppermute | solution.py:49
  33.7 3.3 %collective-permute-start.5 = (bf16[128,512]{1,0:T(8,128)(2,1)S(1)}, bf16[128,512]{1,0:T(8,128)(2,1)S(1)}, u32[]{:S(2)}, u32[]{:S(2)}) collective-permute-start(bf16[128,512]{1,0:T(8,128)(2,1)S(1)} %collective-permute-done.1.refs_1_), channel_id=1, source_target_pairs={{0,1},{1,0},{2,3},{3,2},{4,5},{5,4},{6,7},{7,6},{8,9},{9,8},{10,11... | collective-permute-start | bytes 393224 | tf_op jit(solution)/shard_map/ppermute | solution.py:49
  35.1 2.9 %collective-permute-start.6 = (bf16[128,512]{1,0:T(8,128)(2,1)S(1)}, bf16[128,512]{1,0:T(8,128)(2,1)S(1)}, u32[]{:S(2)}, u32[]{:S(2)}) collective-permute-start(bf16[128,512]{1,0:T(8,128)(2,1)S(1)} %collective-permute-done.2.refs_2_), channel_id=1, source_target_pairs={{0,1},{1,0},{2,3},{3,2},{4,5},{5,4},{6,7},{7,6},{8,9},{9,8},{10,11... | collective-permute-start | bytes 393224 | tf_op jit(solution)/shard_map/ppermute | solution.py:49
  36.1 1.9 %collective-permute-start.7 = (bf16[128,512]{1,0:T(8,128)(2,1)S(1)}, bf16[128,512]{1,0:T(8,128)(2,1)S(1)}, u32[]{:S(2)}, u32[]{:S(2)}) collective-permute-start(bf16[128,512]{1,0:T(8,128)(2,1)S(1)} %collective-permute-done.3.refs_3_), channel_id=1, source_target_pairs={{0,1},{1,0},{2,3},{3,2},{4,5},{5,4},{6,7},{7,6},{8,9},{9,8},{10,11... | collective-permute-start | bytes 393224 | tf_op jit(solution)/shard_map/ppermute | solution.py:49
  36.5 1.5 %collective-permute-start.17 = (bf16[4,64,256]{2,1,0:T(8,128)(2,1)S(1)}, bf16[4,64,256]{2,1,0:T(8,128)(2,1)S(1)}, u32[]{:S(2)}, u32[]{:S(2)}) collective-permute-start(bf16[4,64,256]{2,1,0:T(8,128)(2,1)S(1)} %collective-permute-done.13.refs_11_.refs_3_), channel_id=1, source_target_pairs={{0,1},{1,0},{2,3},{3,2},{4,5},{5,4},{6,7},{7,6},{8,9},{9,8},{10,11... | collective-permute-start | bytes 393224 | tf_op jit(solution)/shard_map/ppermute | solution.py:49
  36.6 1.4 %collective-permute-start.16 = (bf16[4,64,256]{2,1,0:T(8,128)(2,1)S(1)}, bf16[4,64,256]{2,1,0:T(8,128)(2,1)S(1)}, u32[]{:S(2)}, u32[]{:S(2)}) collective-permute-start(bf16[4,64,256]{2,1,0:T(8,128)(2,1)S(1)} %collective-permute-done.12.refs_10_.refs_2_), channel_id=1, source_target_pairs={{0,1},{1,0},{2,3},{3,2},{4,5},{5,4},{6,7},{7,6},{8,9},{9,8},{10,11... | collective-permute-start | bytes 393224 | tf_op jit(solution)/shard_map/ppermute | solution.py:49
  37.0 1.3 %collective-permute-start.15 = (bf16[4,64,256]{2,1,0:T(8,128)(2,1)S(1)}, bf16[4,64,256]{2,1,0:T(8,128)(2,1)S(1)}, u32[]{:S(2)}, u32[]{:S(2)}) collective-permute-start(bf16[4,64,256]{2,1,0:T(8,128)(2,1)S(1)} %collective-permute-done.11.refs_9_.refs_1_), channel_id=1, source_target_pairs={{0,1},{1,0},{2,3},{3,2},{4,5},{5,4},{6,7},{7,6},{8,9},{9,8},{10,11... | collective-permute-start | bytes 393224 | tf_op jit(solution)/shard_map/ppermute | solution.py:49
  41.7 1.5 %collective-permute-start.18 = (bf16[17,3,16,128]{3,2,1,0:T(8,128)(2,1)S(1)}, bf16[17,3,16,128]{3,2,1,0:T(8,128)(2,1)S(1)}, u32[]{:S(2)}, u32[]{:S(2)}) collective-permute-start(bf16[17,3,16,128]{3,2,1,0:T(8,128)(2,1)S(1)} %get-tuple-element.30), channel_id=1, source_target_pairs={{0,1},{1,0},{2,3},{3,2},{4,5},{5,4},{6,7},{7,6},{8,9},{9,8},{10,11... | collective-permute-start | bytes 626696 | tf_op jit(solution)/shard_map/ppermute | solution.py:49
  43.4 27.4 %copy-start.3 = (bf16[64,192]{1,0:T(8,128)(2,1)S(1)}, bf16[64,192]{1,0:T(8,128)(2,1)}, u32[]{:S(2)}) copy-start(bf16[64,192]{1,0:T(8,128)(2,1)} %get-tuple-element.32.own_proj) | copy-start | bytes 73732
  43.4 5.0 %collective-permute-start.19 = (bf16[13,16,128]{2,1,0:T(8,128)(2,1)S(1)}, bf16[13,16,128]{2,1,0:T(8,128)(2,1)S(1)}, u32[]{:S(2)}, u32[]{:S(2)}) collective-permute-start(bf16[13,16,128]{2,1,0:T(8,128)(2,1)S(1)} %get-tuple-element.41), channel_id=1, source_target_pairs={{0,49},{1,48},{2,51},{3,50},{4,53},{5,52},{6,55},{7,54},{8,57},{9,... | collective-permute-start | bytes 159752 | tf_op jit(solution)/shard_map/ppermute | solution.py:49
  46.4 4.0 %collective-permute-start.20 = (bf16[13,16,128]{2,1,0:T(8,128)(2,1)S(1)}, bf16[13,16,128]{2,1,0:T(8,128)(2,1)S(1)}, u32[]{:S(2)}, u32[]{:S(2)}) collective-permute-start(bf16[13,16,128]{2,1,0:T(8,128)(2,1)S(1)} %get-tuple-element.42), channel_id=1, source_target_pairs={{0,17},{1,16},{2,19},{3,18},{4,21},{5,20},{6,23},{7,22},{8,25},{9,... | collective-permute-start | bytes 159752 | tf_op jit(solution)/shard_map/ppermute | solution.py:49
  46.4 4.5 %collective-permute-start.21 = (bf16[13,16,128]{2,1,0:T(8,128)(2,1)S(1)}, bf16[13,16,128]{2,1,0:T(8,128)(2,1)S(1)}, u32[]{:S(2)}, u32[]{:S(2)}) collective-permute-start(bf16[13,16,128]{2,1,0:T(8,128)(2,1)S(1)} %get-tuple-element.43), channel_id=1, source_target_pairs={{0,32},{1,33},{2,34},{3,35},{4,36},{5,37},{6,38},{7,39},{8,40},{9,... | collective-permute-start | bytes 159752 | tf_op jit(solution)/shard_map/ppermute | solution.py:49
  62.4 1.9 %collective-permute-start.22 = (bf16[4,16,128]{2,1,0:T(8,128)(2,1)S(1)}, bf16[4,16,128]{2,1,0:T(8,128)(2,1)S(1)}, u32[]{:S(2)}, u32[]{:S(2)}) collective-permute-start(bf16[4,16,128]{2,1,0:T(8,128)(2,1)S(1)} %reduce_sum.12), channel_id=1, source_target_pairs={{0,1},{1,0},{2,3},{3,2},{4,5},{5,4},{6,7},{7,6},{8,9},{9,8},{10,11... | collective-permute-start | bytes 49160 | tf_op jit(solution)/shard_map/ppermute | solution.py:49
  64.3 6.3 %collective-permute-start.23 = (bf16[4,32,128]{2,1,0:T(8,128)(2,1)S(1)}, bf16[4,32,128]{2,1,0:T(8,128)(2,1)S(1)}, u32[]{:S(2)}, u32[]{:S(2)}) collective-permute-start(bf16[4,32,128]{2,1,0:T(8,128)(2,1)S(1)} %pad_maximum_fusion.5), channel_id=1, source_target_pairs={{0,3},{1,2},{2,1},{3,0},{4,7},{5,6},{6,5},{7,4},{8,11},{9,10},{10,... | collective-permute-start | bytes 98312 | tf_op jit(solution)/shard_map/ppermute | solution.py:49
  64.7 5.9 %collective-permute-start.24 = (bf16[4,32,128]{2,1,0:T(8,128)(2,1)S(1)}, bf16[4,32,128]{2,1,0:T(8,128)(2,1)S(1)}, u32[]{:S(2)}, u32[]{:S(2)}) collective-permute-start(bf16[4,32,128]{2,1,0:T(8,128)(2,1)S(1)} %pad_maximum_fusion.5), channel_id=1, source_target_pairs={{0,5},{1,4},{2,7},{3,6},{4,1},{5,0},{6,3},{7,2},{8,13},{9,12},{10,... | collective-permute-start | bytes 98312 | tf_op jit(solution)/shard_map/ppermute | solution.py:49
  66.2 4.6 %collective-permute-start.25 = (bf16[4,32,128]{2,1,0:T(8,128)(2,1)S(1)}, bf16[4,32,128]{2,1,0:T(8,128)(2,1)S(1)}, u32[]{:S(2)}, u32[]{:S(2)}) collective-permute-start(bf16[4,32,128]{2,1,0:T(8,128)(2,1)S(1)} %pad_maximum_fusion.5), channel_id=1, source_target_pairs={{0,7},{1,6},{2,5},{3,4},{4,3},{5,2},{6,1},{7,0},{8,15},{9,14},{10,... | collective-permute-start | bytes 98312 | tf_op jit(solution)/shard_map/ppermute | solution.py:49
